TPU v7x, 32 devices: a whole 2x2x4 slice. The times are simulated.
32 devices in a mesh: job: 2 (over y), tok: 4 (over z), can: 4 (over x, core).
Axes of the slice: x: 2, y: 2, z: 4, core: 2. Of those that a mesh axis runs over, the one named last changes fastest.
Arguments:
- train_acts: bfloat16 [4096, 14336], P(('job', 'tok')), parts along dimension 0, may hold values from -6 to 6
- train_grads: bfloat16 [4096, 4096], P(('job', 'tok')), parts along dimension 0, may hold values from -6 to 6
- train_segment: int32 [4096], P(('job', 'tok')), parts along dimension 0, may hold values from 0 to 15, as said below
- canary_acts: bfloat16 [1024, 14336], P(('job', 'tok', 'can')), parts along dimension 0, may hold values from -6 to 6
- canary_grads: bfloat16 [1024, 4096], P(('job', 'tok', 'can')), parts along dimension 0, may hold values from -6 to 6
- canary_segment: int32 [1024], P(('job', 'tok', 'can')), parts along dimension 0, may hold values from 0 to 15, never falling along the last dimension, each value on 1 to 64 neighbouring positions
Outputs:
- scores: float32 [32, 16], P(('job', 'tok'), 'can'), parts along dimension 0
There are 2 independent parts, one for each index of `job`. A program takes and returns all parts, laid end to end along the dimension named above; each array names one. Nothing has to cross between parts.
Inputs may be any that keep to these rules, and one draw needn't show every extreme that they name: `train_segment`: ids never fall; the 512 training tokens of block b (tokens b * 512 to b * 512 + 511) belong to the sequences b * 4 to b * 4 + 3, each of them non-empty. `canary_segment`: ids never fall; every canary sequence has 1 to 64 tokens.
All inputs are finite; a program needn't handle non-finite values.
Results may differ from a plain program's by a relative error of at most 0.0003.
Values may be sent and summed in bfloat16 or wider, within the bound.
No kernel may reach another device: no remote copies, remote signals or barrier semaphores. Data moves between devices by JAX's collectives and lax.ppermute only.
A program may use at most 64 MiB of HBM per device.

v0:
```python
import math

import jax
import jax.numpy as jnp
from jax import lax
from jax.sharding import PartitionSpec as P

FF = 14336
D = 4096
SEQ_DEV = 4
CSEQ = 16


def pair_terms(train_acts, train_grads, acts_piece, grads_piece, segment_piece):
    contract = (((1,), (1,)), ((), ()))
    x_gram = lax.dot_general(train_acts, acts_piece, contract, preferred_element_type=jnp.float32)
    g_gram = lax.dot_general(train_grads, grads_piece, contract, preferred_element_type=jnp.float32)
    member = (segment_piece[:, None] == jnp.arange(CSEQ, dtype=jnp.int32)[None, :]).astype(
        jnp.float32
    )
    return jnp.dot(
        x_gram * g_gram, member, precision=lax.Precision.HIGHEST, preferred_element_type=jnp.float32
    )


def local(train_acts, train_grads, train_segment, canary_acts, canary_grads, canary_segment):
    contract = (((1,), (1,)), ((), ()))
    local_ids = train_segment - lax.axis_index("tok") * SEQ_DEV
    owner = (local_ids[:, None] == jnp.arange(SEQ_DEV, dtype=jnp.int32)[None, :]).astype(
        jnp.float32
    )
    self_x = lax.dot_general(train_acts, train_acts, contract, preferred_element_type=jnp.float32)
    self_g = lax.dot_general(train_grads, train_grads, contract, preferred_element_type=jnp.float32)
    left = jnp.dot(
        self_x * self_g, owner, precision=lax.Precision.HIGHEST, preferred_element_type=jnp.float32
    )
    self_score = jnp.sum(owner * left, axis=0)
    gathered = (
        lax.all_gather(canary_acts, "tok", axis=0, tiled=True),
        lax.all_gather(canary_grads, "tok", axis=0, tiled=True),
        lax.all_gather(canary_segment, "tok", axis=0, tiled=True),
    )
    per_token = pair_terms(train_acts, train_grads, gathered[0], gathered[1], gathered[2])
    partial_scores = lax.dot_general(
        owner,
        per_token,
        (((0,), (0,)), ((), ())),
        precision=lax.Precision.HIGHEST,
        preferred_element_type=jnp.float32,
    )
    summed = lax.psum_scatter(partial_scores, "can", scatter_dimension=1, tiled=True)
    canary_total = canary_acts.shape[0] * lax.axis_size("tok") * lax.axis_size("can")
    scale = math.sqrt(FF * D * (canary_total / CSEQ))
    norm_factor = jnp.sqrt(self_score / (FF * D) + 1.0)
    return summed / (scale * norm_factor[:, None])


def solution(mesh):
    placed = (
        P(("job", "tok"), None),
        P(("job", "tok"), None),
        P(("job", "tok")),
        P(("job", "tok", "can"), None),
        P(("job", "tok", "can"), None),
        P(("job", "tok", "can")),
    )
    return jax.shard_map(
        local, mesh=mesh, in_specs=placed, out_specs=P(("job", "tok"), "can"), check_vma=False
    )
```

profile of v0, /device:TPU:0, one launch (start us, length us, event | category | flops | bytes accessed | tf_op | source)
XLA Modules:
  0.0 130.1 jit_solution(5373240643068022139)
XLA Ops:
  6.5 0.0 all-gather.3.cloned.1.call-start
  6.5 0.7 all-gather.3.cloned.1.call-update
  7.3 0.0 all-gather.5.cloned.1.call-start
  7.3 0.7 all-gather.5.cloned.1.call-update
  8.0 1.2 dynamic-slice
  9.9 0.9 dynamic-update-slice
  10.8 9.9 %all-reduce = s32[128]{0:T(128)S(1)} all-reduce(s32[128]{0:T(128)S(1)} %dynamic-update-slice), channel_id=1, replica_groups=mesh['job'=2,'tok'=4,'can'=4] {'tok'}, use_global_device_ids=true, to_apply=%add | all-reduce | flops 128 | bytes 1024
  20.7 0.0 copy-start.1
  20.7 6.0 %fusion.7 = f32[512,512]{1,0:T(8,128)S(1)} fusion(bf16[512,4096]{1,0:T(8,128)(2,1)} %param.7), kind=kOutput, calls=%fused_computation.15 | convolution fusion | flops 2147483648 | bytes 5242880 | tf_op jit(solution)/shard_map/dot_general | solution.py:33
  26.7 0.0 copy-done.1
  26.7 0.6 dynamic-slice.1
  27.9 0.0 copy-start
  27.9 17.4 %convolution_multiply_fusion = f32[512,512]{1,0:T(8,128)S(1)} fusion(f32[512,512]{1,0:T(8,128)S(1)} %fusion.7, bf16[512,14336]{1,0:T(8,128)(2,1)} %param.6), kind=kOutput, calls=%fused_computation | convolution fusion | flops 7516454912 | bytes 16777216 | tf_op jit(solution)/shard_map/dot_general | solution.py:32
  45.3 0.0 copy-done
  45.4 0.7 fusion
  46.1 37.7 %all-gather.3.cloned.1.call-done = bf16[128,14336]{1,0:T(8,128)(2,1)} async-done(((bf16[32,14336]{1,0:T(8,128)(2,1)}), bf16[128,14336]{1,0:T(8,128)(2,1)}) %all-gather.3.cloned.1.call-update) | async-done | bytes 3670032 | tf_op jit(solution)/shard_map/all_gather | solution.py:39
  83.8 8.3 %fusion.6 = f32[512,128]{1,0:T(8,128)S(1)} fusion(bf16[512,14336]{1,0:T(8,128)(2,1)} %param.6, bf16[128,14336]{1,0:T(8,128)(2,1)} %all-gather.3.cloned.1.call-done), kind=kOutput, calls=%fused_computation.14 | convolution fusion | flops 1879048192 | bytes 18612224 | tf_op jit(solution)/shard_map/dot_general | solution.py:16
  92.1 19.8 %all-gather.5.cloned.1.call-done = bf16[128,4096]{1,0:T(8,128)(2,1)} async-done(((bf16[32,4096]{1,0:T(8,128)(2,1)}), bf16[128,4096]{1,0:T(8,128)(2,1)}) %all-gather.5.cloned.1.call-update) | async-done | bytes 1048592 | tf_op jit(solution)/shard_map/all_gather | solution.py:40
  111.9 3.7 %convolution_multiply_fusion.1 = f32[512,128]{1,0:T(8,128)S(1)} fusion(f32[512,128]{1,0:T(8,128)S(1)} %fusion.6, bf16[512,4096]{1,0:T(8,128)(2,1)} %param.7, bf16[128,4096]{1,0:T(8,128)(2,1)} %all-gather.5.cloned.1.call-done), kind=kOutput, calls=%fused_computation.1 | convolution fusion | flops 536936448 | bytes 5767168 | tf_op jit(solution)/shard_map/dot_general | solution.py:17
  115.7 0.3 fusion.1
  116.0 0.2 fusion.3
  116.2 6.4 %all-reduce.1 = f32[4,16]{1,0:T(4,128)S(1)} all-reduce(f32[4,16]{1,0:T(4,128)S(1)} %fusion.3), channel_id=2, replica_groups=mesh['job'=2,'tok'=4,'can'=4] {'can'}, use_global_device_ids=true, to_apply=%region_0.0.clone | all-reduce | flops 64 | bytes 512
  122.6 0.7 dynamic-slice_divide_fusion
  (3 shorter events, 0.0 us)
Async XLA Ops:
  6.5 77.2 %all-gather.3.cloned.1.call-start = ((), (), s32[]{:S(2)}) async-start(), calls=%async_computation | async-start | bytes 4587520 | tf_op jit(solution)/shard_map/all_gather | solution.py:39
  7.3 104.7 %all-gather.5.cloned.1.call-start = ((), (), s32[]{:S(2)}) async-start(), calls=%async_computation.1 | async-start | bytes 1310720 | tf_op jit(solution)/shard_map/all_gather | solution.py:40
  20.7 6.0 %copy-start.1 = (u32[32]{0:T(128)S(1)}, u32[32]{0:T(128)}, u32[]{:S(2)}) copy-start(u32[32]{0:T(128)} %constant.25) | copy-start | bytes 388
  27.9 17.4 %copy-start = (s32[512]{0:T(512)S(1)}, s32[512]{0:T(512)}, u32[]{:S(2)}) copy-start(s32[512]{0:T(512)} %param.8) | copy-start | bytes 6148
Sparse Core Ops, SparseCore 0:
  8.9 74.8 all-gather.2
  85.3 26.5 all-gather.4
where the time goes:
time: 130 us
  waiting for transfers between devices  58.9 us (45%)
  matrix products  36.6 us (28%)
  blocking collectives  16.3 us (13%)
  between operations  14.8 us (11%)
  local copies, waits for them, and re-layouts  2.7 us (2%)
    all_gather x1, waiting for transfers between devices, local(): lax.all_gather(canary_acts, 'tok', axis=0, tiled=True)  37.7 us
    all_gather x1, waiting for transfers between devices, local(): lax.all_gather(canary_grads, 'tok', axis=0, tiled=True)  19.8 us
    dot_general x1, matrix products, local(): lax.dot_general(train_acts, train_acts, contract, preferred_element_type=...  17.4 us
    unnamed x2, blocking collectives  16.3 us
    dot_general x1, matrix products, pair_terms(): lax.dot_general(train_acts, acts_piece, contract, preferred_element_type=...  8.29 us
    dot_general x1, matrix products, local(): lax.dot_general(train_grads, train_grads, contract, preferred_element_typ...  5.99 us
    dot_general x1, matrix products, pair_terms(): lax.dot_general(train_grads, grads_piece, contract, preferred_element_typ...  3.74 us
    unnamed x8, local copies, waits for them, and re-layouts  2.7 us
  transfers between devices with their start and end apart: 2, of which 2 were waited for; matrix products, arithmetic and copies ran while one was open for 27% of the time, Pallas kernels for 0%

commit v1 on v0

v1 whole, which is shorter than its diff:
```python
import math

import jax
import jax.numpy as jnp
from jax import lax
from jax.experimental import pallas as pl
from jax.experimental.pallas import tpu as pltpu
from jax.sharding import PartitionSpec as P

FF = 14336
D = 4096
SEQ_DEV = 4
CSEQ = 16
LANES = 128
FIRST = 10752
ROWS = (((1,), (1,)), ((), ()))


def gram(left, right):
    return lax.dot_general(left, right, ROWS, preferred_element_type=jnp.float32)


def exact(left, right, dims):
    return lax.dot_general(
        left, right, (dims, ((), ())), precision=lax.Precision.HIGHEST, preferred_element_type=jnp.float32
    )


def after(value, *earlier):
    return lax.optimization_barrier((value,) + earlier)[0]


def after2(one, two, earlier):
    return lax.optimization_barrier((one, two) + tuple(earlier))[:2]


def call(kernel, scalar, inputs, specs, steps, out, scratch, depth, name):
    return pl.pallas_call(
        kernel,
        grid_spec=pltpu.PrefetchScalarGridSpec(
            num_scalar_prefetch=1,
            grid=(steps,),
            in_specs=specs,
            out_specs=pl.BlockSpec(out, lambda k, s: (0, 0)),
            scratch_shapes=scratch,
        ),
        out_shape=jax.ShapeDtypeStruct(out, jnp.float32),
        cost_estimate=pl.CostEstimate(flops=512 * 256 * depth, bytes_accessed=1024 * depth, transcendentals=0),
        compiler_params=pltpu.CompilerParams(vmem_limit_bytes=56 << 20),
        name=name,
    )(scalar.reshape(1).astype(jnp.int32), *inputs)


def in_order(z, own, down, up, second, far):
    return jnp.concatenate([own, jnp.where(z < 3, down, far), second, jnp.where(z > 0, up, far)], axis=0)


def cross_gram(base, train, pieces, cut, block):
    rows, per = train.shape[0], pieces[0].shape[0]
    low, high = cut

    def kernel(z_ref, base_ref, train_ref, own, down, up, second, far, out_ref):
        right = in_order(z_ref[0], own[...], down[...], up[...], second[...], far[...])
        part = gram(train_ref[...], right)

        @pl.when(pl.program_id(0) == 0)
        def _():
            out_ref[...] = base_ref[...] + part

        @pl.when(pl.program_id(0) > 0)
        def _():
            out_ref[...] += part

    whole = pl.BlockSpec((rows, 4 * per), lambda k, s: (0, 0))
    near = pl.BlockSpec((per, block), lambda k, s: (0, low // block + k))
    late = pl.BlockSpec((per, block), lambda k, s: (0, k))
    wide = pl.BlockSpec((rows, block), lambda k, s: (0, low // block + k))
    specs = [whole, wide] + [near] * 3 + [late] * 2
    inputs = (base, train) + tuple(pieces)
    steps = (high - low) // block
    return call(kernel, lax.axis_index("tok"), inputs, specs, steps, (rows, 4 * per), [], high - low, "cross_gram")


def score_shares(x_gram, owner_rows, self_rows, train, pieces, block):
    rows, depth = train.shape
    per = pieces[0].shape[0]
    steps = depth // block

    def kernel(z_ref, x_ref, owner_ref, self_ref, train_ref, *refs):
        total, out_ref = refs[-1], refs[-2]
        z = z_ref[0]
        part = gram(train_ref[...], in_order(z, *[r[...] for r in refs[:5]]))

        @pl.when(pl.program_id(0) == 0)
        def _():
            total[...] = part

        @pl.when(pl.program_id(0) > 0)
        def _():
            total[...] += part

        @pl.when(pl.program_id(0) == steps - 1)
        def _():
            pair = x_ref[...] * total[...]
            by_train = exact(owner_ref[...], pair, ((1,), (0,)))
            ids = in_order(z, *[r[...].astype(jnp.float32) for r in refs[5:10]])
            lane = lax.broadcasted_iota(jnp.int32, ids.shape, 1)
            member = (ids == lane.astype(jnp.float32)).astype(jnp.float32)
            scores = exact(by_train, member, ((1,), (0,)))
            out_ref[...] = jnp.where(lax.broadcasted_iota(jnp.int32, scores.shape, 1) < CSEQ, scores, self_ref[...])

    whole = pl.BlockSpec((rows, 4 * per), lambda k, s: (0, 0))
    wide = pl.BlockSpec((rows, block), lambda k, s: (0, k))
    piece = pl.BlockSpec((per, block), lambda k, s: (0, k))
    tag = pl.BlockSpec((per, LANES), lambda k, s: (0, depth // LANES))
    seq = owner_rows.shape[0]
    specs = [
        whole,
        pl.BlockSpec((seq, rows), lambda k, s: (0, 0)),
        pl.BlockSpec((seq, LANES), lambda k, s: (0, 0)),
        wide,
    ]
    specs = specs + [piece] * 5 + [tag] * 5
    inputs = (x_gram, owner_rows, self_rows, train) + tuple(pieces) * 2
    scratch = [pltpu.VMEM((rows, 4 * per), jnp.float32)]
    return call(kernel, lax.axis_index("tok"), inputs, specs, steps, (seq, LANES), scratch, depth, "score_shares")


DOWN = [(1, 0), (2, 1), (3, 2)]
UP = [(0, 1), (1, 2), (2, 3)]
FAR = [(1, 0), (2, 3)]


def line_scores(train_acts, train_grads, owner_rows, self_rows, canary_acts, canary_grads, canary_segment):
    z = lax.axis_index("tok")
    tag = jnp.broadcast_to(canary_segment.astype(canary_grads.dtype)[:, None], (canary_segment.shape[0], LANES))
    tagged = jnp.concatenate([canary_grads, tag], axis=1)

    acts_down = lax.ppermute(canary_acts, "tok", DOWN)
    acts_up = lax.ppermute(canary_acts, "tok", UP)
    grads_down = lax.ppermute(tagged, "tok", DOWN)
    grads_up = lax.ppermute(tagged, "tok", UP)

    acts_down, acts_up = after2(acts_down, acts_up, ())
    acts_down2 = lax.ppermute(acts_down, "tok", DOWN[:2])
    acts_up2 = lax.ppermute(acts_up, "tok", UP[1:])
    grads_down, grads_up = after2(grads_down, grads_up, (acts_down, acts_up))
    grads_down2 = lax.ppermute(grads_down, "tok", DOWN[:2])
    grads_up2 = lax.ppermute(grads_up, "tok", UP[1:])

    acts_down2, acts_up2 = after2(acts_down2, acts_up2, (grads_down, grads_up))
    second_a = jnp.where(z < 2, acts_down2[:, :FIRST], acts_up2[:, :FIRST])
    far_a = lax.ppermute(second_a, "tok", FAR)
    acts_down2, acts_up2 = after2(acts_down2, acts_up2, (second_a,))
    second_b = jnp.where(z < 2, acts_down2[:, FIRST:], acts_up2[:, FIRST:])
    far_b = lax.ppermute(second_b, "tok", FAR)
    grads_down2, grads_up2 = after2(grads_down2, grads_up2, (second_b,))
    second_g = jnp.where(z < 2, grads_down2, grads_up2)
    far_g = lax.ppermute(second_g, "tok", FAR)

    x_gram = jnp.zeros((train_acts.shape[0], 4 * canary_acts.shape[0]), jnp.float32)
    near = (canary_acts, acts_down, acts_up)
    x_gram = cross_gram(x_gram, train_acts, near + (second_a, far_a), (0, FIRST), 3584)
    x_gram = cross_gram(x_gram, train_acts, near + (second_b, after(far_b, x_gram)), (FIRST, FF), 1792)
    pieces = (tagged, grads_down, grads_up, second_g, after(far_g, x_gram))
    return score_shares(x_gram, owner_rows, self_rows, train_grads, pieces, 2048)


def finish(shares, canary_total):
    can = lax.axis_size("can")
    width = CSEQ // can
    total = shares
    for k in range(1, can):
        total = total + lax.ppermute(shares, "can", [(i, (i + k) % can) for i in range(can)])
    own = lax.dynamic_slice(total, (0, lax.axis_index("can") * width), (SEQ_DEV, width))
    scale = math.sqrt(FF * D * (canary_total / CSEQ))
    return own / (scale * jnp.sqrt(total[:SEQ_DEV, CSEQ] / (FF * D) + 1.0)[:, None])


def local(train_acts, train_grads, train_segment, canary_acts, canary_grads, canary_segment):
    tok, can = lax.axis_size("tok"), lax.axis_size("can")
    rows = train_acts.shape[0]
    canary_total = canary_acts.shape[0] * tok * can
    local_ids = train_segment - lax.axis_index("tok") * SEQ_DEV
    owner_rows = (jnp.arange(8, dtype=jnp.int32)[:, None] == local_ids[None, :]).astype(jnp.float32)

    share = rows // can
    start = lax.axis_index("can") * share
    self_pair = gram(train_acts, lax.dynamic_slice_in_dim(train_acts, start, share, 0))
    self_pair = self_pair * gram(train_grads, lax.dynamic_slice_in_dim(train_grads, start, share, 0))
    left = exact(owner_rows, self_pair, ((1,), (0,)))
    self_share = jnp.sum(left * lax.dynamic_slice_in_dim(owner_rows, start, share, 1), axis=1)
    self_rows = jnp.broadcast_to(self_share[:, None], (8, LANES))

    if tok == 4:
        shares = line_scores(
            train_acts, train_grads, owner_rows, self_rows, canary_acts, canary_grads, canary_segment
        )
    else:
        ids = lax.all_gather(canary_segment, "tok", axis=0, tiled=True)
        pair = gram(train_acts, lax.all_gather(canary_acts, "tok", axis=0, tiled=True))
        pair = pair * gram(train_grads, lax.all_gather(canary_grads, "tok", axis=0, tiled=True))
        member = (ids[:, None] == jnp.arange(CSEQ, dtype=jnp.int32)[None, :]).astype(jnp.float32)
        scores = exact(exact(owner_rows, pair, ((1,), (0,))), member, ((1,), (0,)))
        shares = jnp.concatenate([scores, self_rows[:, CSEQ:]], axis=1)
    return finish(shares, canary_total)


def solution(mesh):
    placed = (
        P(("job", "tok"), None),
        P(("job", "tok"), None),
        P(("job", "tok")),
        P(("job", "tok", "can"), None),
        P(("job", "tok", "can"), None),
        P(("job", "tok", "can")),
    )
    return jax.shard_map(
        local, mesh=mesh, in_specs=placed, out_specs=P(("job", "tok"), "can"), check_vma=False
    )
```

time: 130 us -> 102 us (0.78)
  the two profiles are of different devices: /device:TPU:0 before, /device:TPU:29 now
where the time goes in v1:
time: 102 us
  waiting for transfers between devices  33.9 us (33%)
  starting transfers between devices  27.5 us (27%)
  Pallas kernels  16.3 us (16%)
  matrix products  15.7 us (15%)
  other arithmetic  5.67 us (6%)
  local copies, waits for them, and re-layouts  2.45 us (2%)
    pallas_call x3, Pallas kernels, call(): pl.pallas_call(kernel, grid_spec=pltpu.PrefetchScalarGridSpec(num_scalar_...  16.3 us
    dot_general x2, matrix products, gram(): lax.dot_general(left, right, ROWS, preferred_element_type=jnp.float32)  15.4 us
    ppermute x1, waiting for transfers between devices, line_scores(): far_a = lax.ppermute(second_a, 'tok', FAR)  11.8 us
    ppermute x3, starting transfers between devices, finish(): lax.ppermute(shares, 'can', [(i, (i + k) % can) for i in range(can)])  10.1 us
    ppermute x1, waiting for transfers between devices, line_scores(): acts_up2 = lax.ppermute(acts_up, 'tok', UP[1:])  7.88 us
    ppermute x1, waiting for transfers between devices, line_scores(): acts_down = lax.ppermute(canary_acts, 'tok', DOWN)  6.86 us
    ppermute x1, starting transfers between devices, line_scores(): grads_down = lax.ppermute(tagged, 'tok', DOWN)  4 us
    ppermute x1, waiting for transfers between devices, line_scores(): acts_up = lax.ppermute(canary_acts, 'tok', UP)  3.75 us
  transfers between devices with their start and end apart: 14, of which 8 were waited for; matrix products, arithmetic and copies ran while one was open for 20% of the time, Pallas kernels for 12%

profile of v1, /device:TPU:29, one launch (start us, length us, event | category | flops | bytes accessed | tf_op | source)
XLA Modules:
  0.0 101.9 jit_solution(4547069089910745277)
XLA Ops:
  0.0 2.1 %collective-permute-start = (bf16[32,14336]{1,0:T(8,128)(2,1)}, bf16[32,14336]{1,0:T(8,128)(2,1)S(1)}, u32[]{:S(2)}, u32[]{:S(2)}) collective-permute-start(bf16[32,14336]{1,0:T(8,128)(2,1)} %own.3), channel_id=1, source_target_pairs={{4,0},{8,4},{12,8},{5,1},{9,5},{13,9},{6,2},{10,6},{14,10},{7,3},{... | collective-permute-start | bytes 2752520 | tf_op jit(solution)/shard_map/ppermute | solution.py:139
  2.1 1.3 %collective-permute-start.1 = (bf16[32,14336]{1,0:T(8,128)(2,1)}, bf16[32,14336]{1,0:T(8,128)(2,1)S(1)}, u32[]{:S(2)}, u32[]{:S(2)}) collective-permute-start(bf16[32,14336]{1,0:T(8,128)(2,1)} %own.3), channel_id=1, source_target_pairs={{0,4},{4,8},{8,12},{1,5},{5,9},{9,13},{2,6},{6,10},{10,14},{3,7},{... | collective-permute-start | bytes 2752520 | tf_op jit(solution)/shard_map/ppermute | solution.py:140
  3.4 0.7 convert_element_type.6
  4.1 0.1 broadcast_in_dim.7
  4.2 1.0 pad_maximum_fusion.refs_0_.refs_5_
  5.1 0.0 copy-start.3
  5.1 4.0 %collective-permute-start.4 = (bf16[32,4224]{1,0:T(8,128)(2,1)S(1)}, bf16[32,4224]{1,0:T(8,128)(2,1)S(1)}, u32[]{:S(2)}, u32[]{:S(2)}) collective-permute-start(bf16[32,4224]{1,0:T(8,128)(2,1)S(1)} %pad_maximum_fusion.refs_0_.refs_5_), channel_id=1, source_target_pairs={{4,0},{8,4},{12,8},{5,1},{9,5},{13,9},{6,2},{10,6},{14,10},{7,3},{... | collective-permute-start | bytes 811016 | tf_op jit(solution)/shard_map/ppermute | solution.py:141
  9.2 1.3 %collective-permute-start.5 = (bf16[32,4224]{1,0:T(8,128)(2,1)S(1)}, bf16[32,4224]{1,0:T(8,128)(2,1)S(1)}, u32[]{:S(2)}, u32[]{:S(2)}) collective-permute-start(bf16[32,4224]{1,0:T(8,128)(2,1)S(1)} %pad_maximum_fusion.refs_0_.refs_5_), channel_id=1, source_target_pairs={{0,4},{4,8},{8,12},{1,5},{5,9},{9,13},{2,6},{6,10},{10,14},{3,7},{... | collective-permute-start | bytes 811016 | tf_op jit(solution)/shard_map/ppermute | solution.py:142
  10.5 4.0 %fusion.6 = f32[128,512]{1,0:T(8,128)S(1)} fusion(bf16[512,4096]{1,0:T(8,128)(2,1)} %train_ref.5, s32[]{:T(128)S(6)} %select_n.36), kind=kOutput, calls=%fused_computation.5 | convolution fusion | flops 536870912 | bytes 5505028 | tf_op jit(solution)/shard_map/dot_general | solution.py:20
  14.5 0.0 copy-start.12
  14.5 6.9 %collective-permute-done.down = bf16[32,14336]{1,0:T(8,128)(2,1)S(1)} collective-permute-done((bf16[32,14336]{1,0:T(8,128)(2,1)}, bf16[32,14336]{1,0:T(8,128)(2,1)S(1)}, u32[]{:S(2)}, u32[]{:S(2)}) %collective-permute-start) | collective-permute-done | bytes 917536 | tf_op jit(solution)/shard_map/ppermute | solution.py:139
  21.4 3.7 %collective-permute-done.1.up = bf16[32,14336]{1,0:T(8,128)(2,1)S(1)} collective-permute-done((bf16[32,14336]{1,0:T(8,128)(2,1)}, bf16[32,14336]{1,0:T(8,128)(2,1)S(1)}, u32[]{:S(2)}, u32[]{:S(2)}) %collective-permute-start.1) | collective-permute-done | bytes 917536 | tf_op jit(solution)/shard_map/ppermute | solution.py:140
  25.1 1.6 %collective-permute-start.2 = (bf16[32,14336]{1,0:T(8,128)(2,1)S(1)}, bf16[32,14336]{1,0:T(8,128)(2,1)}, u32[]{:S(2)}, u32[]{:S(2)}) collective-permute-start(bf16[32,14336]{1,0:T(8,128)(2,1)S(1)} %collective-permute-done.down), channel_id=1, source_target_pairs={{4,0},{8,4},{5,1},{9,5},{6,2},{10,6},{7,3},{11,7},{20,16},{24,20},... | collective-permute-start | bytes 2752520 | tf_op jit(solution)/shard_map/ppermute | solution.py:145
  26.7 1.3 %collective-permute-start.3 = (bf16[32,14336]{1,0:T(8,128)(2,1)S(1)}, bf16[32,14336]{1,0:T(8,128)(2,1)}, u32[]{:S(2)}, u32[]{:S(2)}) collective-permute-start(bf16[32,14336]{1,0:T(8,128)(2,1)S(1)} %collective-permute-done.1.up), channel_id=1, source_target_pairs={{4,8},{8,12},{5,9},{9,13},{6,10},{10,14},{7,11},{11,15},{20,24},{2... | collective-permute-start | bytes 2752520 | tf_op jit(solution)/shard_map/ppermute | solution.py:146
  28.0 11.3 %fusion.2 = f32[128,512]{1,0:T(8,128)S(1)} fusion(f32[128,512]{1,0:T(8,128)S(1)} %fusion.6, bf16[512,14336]{1,0:T(8,128)(2,1)} %train_ref.4, s32[]{:T(128)S(6)} %select_n.36), kind=kOutput, calls=%fused_computation.2 | convolution fusion | flops 1879113728 | bytes 18874372 | tf_op jit(solution)/shard_map/dot_general | solution.py:20
  39.3 0.0 copy-done.3
  39.3 0.0 copy-done
  39.3 0.0 copy-done.1
  39.4 0.0 copy-done.12
  39.4 0.0 copy-start.11
  39.4 0.0 collective-permute-done.4.refs_1_.refs_6_
  39.4 0.0 copy-start.5
  39.4 0.0 collective-permute-done.5.refs_2_.refs_7_
  39.4 0.0 copy-start.6
  39.4 0.7 collective-permute-start.8
  40.1 1.3 %collective-permute-start.9 = (bf16[32,4224]{1,0:T(8,128)(2,1)S(1)}, bf16[32,4224]{1,0:T(8,128)(2,1)S(1)}, u32[]{:S(2)}, u32[]{:S(2)}) collective-permute-start(bf16[32,4224]{1,0:T(8,128)(2,1)S(1)} %collective-permute-done.5.refs_2_.refs_7_), channel_id=1, source_target_pairs={{4,8},{8,12},{5,9},{9,13},{6,10},{10,14},{7,11},{11,15},{20,24},{2... | collective-permute-start | bytes 811016 | tf_op jit(solution)/shard_map/ppermute | solution.py:149
  41.4 0.0 collective-permute-done.2
  41.4 7.9 %collective-permute-done.3 = bf16[32,14336]{1,0:T(8,128)(2,1)} collective-permute-done((bf16[32,14336]{1,0:T(8,128)(2,1)S(1)}, bf16[32,14336]{1,0:T(8,128)(2,1)}, u32[]{:S(2)}, u32[]{:S(2)}) %collective-permute-start.3) | collective-permute-done | bytes 917536 | tf_op jit(solution)/shard_map/ppermute | solution.py:146
  49.3 1.4 %slice_select_fusion.second = bf16[32,10752]{1,0:T(8,128)(2,1)S(1)} fusion(bf16[32,14336]{1,0:T(8,128)(2,1)} %collective-permute-done.3, bf16[32,14336]{1,0:T(8,128)(2,1)} %collective-permute-done.2, pred[]{:T(512)S(6)} %lt.6), kind=kLoop, calls=%fused_computation.7 | loop fusion | flops 344064 | bytes 2064385 | tf_op jit(solution)/shard_map/jit(_where)/select_n | solution.py:152
  50.7 0.0 copy-start.2
  50.7 1.3 %collective-permute-start.6 = (bf16[32,10752]{1,0:T(8,128)(2,1)S(1)}, bf16[32,10752]{1,0:T(8,128)(2,1)S(1)}, u32[]{:S(2)}, u32[]{:S(2)}) collective-permute-start(bf16[32,10752]{1,0:T(8,128)(2,1)S(1)} %slice_select_fusion.second), channel_id=1, source_target_pairs={{4,0},{8,12},{5,1},{9,13},{6,2},{10,14},{7,3},{11,15},{20,16},{24,... | collective-permute-start | bytes 2064392 | tf_op jit(solution)/shard_map/ppermute | solution.py:153
  52.0 1.1 %slice_select_fusion.1.second = bf16[32,3584]{1,0:T(8,128)(2,1)S(1)} fusion(bf16[32,14336]{1,0:T(8,128)(2,1)} %collective-permute-done.3, bf16[32,14336]{1,0:T(8,128)(2,1)} %collective-permute-done.2, pred[]{:T(512)S(6)} %lt.6), kind=kLoop, calls=%fused_computation.10 | loop fusion | flops 114688 | bytes 688129 | tf_op jit(solution)/shard_map/jit(_where)/select_n | solution.py:155
  53.1 0.0 copy-start.8
  53.1 1.3 %collective-permute-start.7 = (bf16[32,3584]{1,0:T(8,128)(2,1)S(1)}, bf16[32,3584]{1,0:T(8,128)(2,1)S(1)}, u32[]{:S(2)}, u32[]{:S(2)}) collective-permute-start(bf16[32,3584]{1,0:T(8,128)(2,1)S(1)} %slice_select_fusion.1.second), channel_id=1, source_target_pairs={{4,0},{8,12},{5,1},{9,13},{6,2},{10,14},{7,3},{11,15},{20,16},{24,... | collective-permute-start | bytes 688136 | tf_op jit(solution)/shard_map/ppermute | solution.py:156
  54.4 0.0 collective-permute-done.8
  54.4 0.6 collective-permute-done.9
  55.1 0.0 copy-start.4
  55.1 1.3 %collective-permute-start.10 = (bf16[32,4224]{1,0:T(8,128)(2,1)S(1)}, bf16[32,4224]{1,0:T(8,128)(2,1)S(1)}, u32[]{:S(2)}, u32[]{:S(2)}) collective-permute-start(bf16[32,4224]{1,0:T(8,128)(2,1)S(1)} %broadcast_select_fusion.refs_3_.refs_8_), channel_id=1, source_target_pairs={{4,0},{8,12},{5,1},{9,13},{6,2},{10,14},{7,3},{11,15},{20,16},{24,... | collective-permute-start | bytes 811016 | tf_op jit(solution)/shard_map/ppermute | solution.py:159
  56.4 0.4 fusion.5
  56.7 11.8 %collective-permute-done.6.far = bf16[32,10752]{1,0:T(8,128)(2,1)S(1)} collective-permute-done((bf16[32,10752]{1,0:T(8,128)(2,1)S(1)}, bf16[32,10752]{1,0:T(8,128)(2,1)S(1)}, u32[]{:S(2)}, u32[]{:S(2)}) %collective-permute-start.6) | collective-permute-done | bytes 688160 | tf_op jit(solution)/shard_map/ppermute | solution.py:153
  68.5 0.8 broadcast_in_dim.6.base_ref
  69.3 0.0 copy-done.2
  69.3 0.2 copy-done.9
  69.5 7.9 %cross_gram.2.base_ref = f32[512,128]{1,0:T(8,128)} custom-call(s32[1]{0:T(128)} %bitcast.z_ref, f32[512,128]{1,0:T(8,128)} %broadcast_in_dim.6.base_ref, bf16[512,14336]{1,0:T(8,128)(2,1)} %train_ref.4, bf16[32,14336]{1,0:T(8,128)(2,1)} %own.3, bf16[32,14336]{1,0:T(8,128)(2,1)} %copy-done, bf16[32,14336]{1,0:T(8,128)(2,1)} %copy-done.1, ...), custom_call_target="tpu_custom_call" | custom-call | flops 1409286144 | bytes 11010048 | tf_op jit(solution)/shard_map/cross_gram/pallas_call | solution.py:38
  77.4 0.0 copy-done.11
  77.4 0.0 copy-done.5
  77.4 0.0 copy-done.6
  77.4 0.0 collective-permute-done.7.far
  77.4 0.0 copy-start.10
  77.5 0.7 copy-done.10
  78.1 3.9 %cross_gram.3.x_ref = f32[512,128]{1,0:T(8,128)} custom-call(s32[1]{0:T(128)} %bitcast.z_ref, f32[512,128]{1,0:T(8,128)} %cross_gram.2.base_ref, bf16[512,14336]{1,0:T(8,128)(2,1)} %train_ref.4, bf16[32,14336]{1,0:T(8,128)(2,1)} %own.3, bf16[32,14336]{1,0:T(8,128)(2,1)} %copy-done, bf16[32,14336]{1,0:T(8,128)(2,1)} %copy-done.1, bf16[32,3584]{1,0:T(8,128)(2,1)} %copy-done.8, ...), custom_call_target="tpu_custom_call" | custom-call | flops 469762048 | bytes 3670016 | tf_op jit(solution)/shard_map/cross_gram/pallas_call | solution.py:38
  82.0 0.0 collective-permute-done.10.refs_4_.refs_9_
  82.0 0.7 broadcast_in_dim.8.self_ref
  82.7 0.0 copy-done.7
  82.8 4.5 %score_shares.1 = f32[8,128]{1,0:T(8,128)} custom-call(s32[1]{0:T(128)} %bitcast.z_ref, f32[512,128]{1,0:T(8,128)} %cross_gram.3.x_ref, f32[8,512]{1,0:T(8,128)} %copy-done.11, f32[8,128]{1,0:T(8,128)} %broadcast_in_dim.8.self_ref, bf16[512,4096]{1,0:T(8,128)(2,1)} %train_ref.5, bf16[32,4224]{1,0:T(8,128)(2,1)} %copy-done.3, bf16[32,4224]{1,0:T(8,128)(2,1)} %copy-done.5, ...), custom_call_target="tpu_custom_call" | custom-call | flops 536870912 | bytes 4194304 | tf_op jit(solution)/shard_map/score_shares/pallas_call | solution.py:38
  87.2 9.6 %collective-permute-start.11 = (f32[8,128]{1,0:T(8,128)}, f32[8,128]{1,0:T(8,128)S(1)}, u32[]{:S(2)}, u32[]{:S(2)}) collective-permute-start(f32[8,128]{1,0:T(8,128)} %score_shares.1), channel_id=1, source_target_pairs={{0,1},{1,2},{2,3},{3,0},{4,5},{5,6},{6,7},{7,4},{8,9},{9,10},{10,1... | collective-permute-start | bytes 12296 | tf_op jit(solution)/shard_map/ppermute | solution.py:174
  96.8 0.3 collective-permute-start.12
  97.1 0.2 collective-permute-start.13
  97.3 0.5 collective-permute-done.11
  97.8 1.7 %collective-permute-done.12 = f32[8,128]{1,0:T(8,128)S(1)} collective-permute-done((f32[8,128]{1,0:T(8,128)}, f32[8,128]{1,0:T(8,128)S(1)}, u32[]{:S(2)}, u32[]{:S(2)}) %collective-permute-start.12) | collective-permute-done | bytes 4128 | tf_op jit(solution)/shard_map/ppermute | solution.py:174
  99.5 0.8 collective-permute-done.13
  100.3 0.7 add_add_fusion
  101.0 0.2 multiply_reduce_fusion
  101.2 0.7 dynamic-slice_divide_fusion
  (9 shorter events, 0.1 us)
Async XLA Ops:
  0.0 21.4 %collective-permute-start = (bf16[32,14336]{1,0:T(8,128)(2,1)}, bf16[32,14336]{1,0:T(8,128)(2,1)S(1)}, u32[]{:S(2)}, u32[]{:S(2)}) collective-permute-start(bf16[32,14336]{1,0:T(8,128)(2,1)} %own.3), channel_id=1, source_target_pairs={{4,0},{8,4},{12,8},{5,1},{9,5},{13,9},{6,2},{10,6},{14,10},{7,3},{... | collective-permute-start | bytes 2752520 | tf_op jit(solution)/shard_map/ppermute | solution.py:139
  2.1 23.0 %collective-permute-start.1 = (bf16[32,14336]{1,0:T(8,128)(2,1)}, bf16[32,14336]{1,0:T(8,128)(2,1)S(1)}, u32[]{:S(2)}, u32[]{:S(2)}) collective-permute-start(bf16[32,14336]{1,0:T(8,128)(2,1)} %own.3), channel_id=1, source_target_pairs={{0,4},{4,8},{8,12},{1,5},{5,9},{9,13},{2,6},{6,10},{10,14},{3,7},{... | collective-permute-start | bytes 2752520 | tf_op jit(solution)/shard_map/ppermute | solution.py:140
  5.1 34.2 %copy-start.3 = (bf16[32,4224]{1,0:T(8,128)(2,1)}, bf16[32,4224]{1,0:T(8,128)(2,1)S(1)}, u32[]{:S(2)}) copy-start(bf16[32,4224]{1,0:T(8,128)(2,1)S(1)} %pad_maximum_fusion.refs_0_.refs_5_) | copy-start | bytes 811012
  5.1 34.3 %collective-permute-start.4 = (bf16[32,4224]{1,0:T(8,128)(2,1)S(1)}, bf16[32,4224]{1,0:T(8,128)(2,1)S(1)}, u32[]{:S(2)}, u32[]{:S(2)}) collective-permute-start(bf16[32,4224]{1,0:T(8,128)(2,1)S(1)} %pad_maximum_fusion.refs_0_.refs_5_), channel_id=1, source_target_pairs={{4,0},{8,4},{12,8},{5,1},{9,5},{13,9},{6,2},{10,6},{14,10},{7,3},{... | collective-permute-start | bytes 811016 | tf_op jit(solution)/shard_map/ppermute | solution.py:141
  9.2 30.3 %collective-permute-start.5 = (bf16[32,4224]{1,0:T(8,128)(2,1)S(1)}, bf16[32,4224]{1,0:T(8,128)(2,1)S(1)}, u32[]{:S(2)}, u32[]{:S(2)}) collective-permute-start(bf16[32,4224]{1,0:T(8,128)(2,1)S(1)} %pad_maximum_fusion.refs_0_.refs_5_), channel_id=1, source_target_pairs={{0,4},{4,8},{8,12},{1,5},{5,9},{9,13},{2,6},{6,10},{10,14},{3,7},{... | collective-permute-start | bytes 811016 | tf_op jit(solution)/shard_map/ppermute | solution.py:142
  14.5 24.8 %copy-start.12 = (s32[512]{0:T(512)S(1)}, s32[512]{0:T(512)}, u32[]{:S(2)}) copy-start(s32[512]{0:T(512)} %param.8) | copy-start | bytes 6148
  21.4 17.9 %copy-start = (bf16[32,14336]{1,0:T(8,128)(2,1)}, bf16[32,14336]{1,0:T(8,128)(2,1)S(1)}, u32[]{:S(2)}) copy-start(bf16[32,14336]{1,0:T(8,128)(2,1)S(1)} %collective-permute-done.down) | copy-start | bytes 2752516
  25.1 14.2 %copy-start.1 = (bf16[32,14336]{1,0:T(8,128)(2,1)}, bf16[32,14336]{1,0:T(8,128)(2,1)S(1)}, u32[]{:S(2)}) copy-start(bf16[32,14336]{1,0:T(8,128)(2,1)S(1)} %collective-permute-done.1.up) | copy-start | bytes 2752516
  25.1 16.3 %collective-permute-start.2 = (bf16[32,14336]{1,0:T(8,128)(2,1)S(1)}, bf16[32,14336]{1,0:T(8,128)(2,1)}, u32[]{:S(2)}, u32[]{:S(2)}) collective-permute-start(bf16[32,14336]{1,0:T(8,128)(2,1)S(1)} %collective-permute-done.down), channel_id=1, source_target_pairs={{4,0},{8,4},{5,1},{9,5},{6,2},{10,6},{7,3},{11,7},{20,16},{24,20},... | collective-permute-start | bytes 2752520 | tf_op jit(solution)/shard_map/ppermute | solution.py:145
  26.7 22.6 %collective-permute-start.3 = (bf16[32,14336]{1,0:T(8,128)(2,1)S(1)}, bf16[32,14336]{1,0:T(8,128)(2,1)}, u32[]{:S(2)}, u32[]{:S(2)}) collective-permute-start(bf16[32,14336]{1,0:T(8,128)(2,1)S(1)} %collective-permute-done.1.up), channel_id=1, source_target_pairs={{4,8},{8,12},{5,9},{9,13},{6,10},{10,14},{7,11},{11,15},{20,24},{2... | collective-permute-start | bytes 2752520 | tf_op jit(solution)/shard_map/ppermute | solution.py:146
  39.4 38.0 %copy-start.11 = (f32[8,512]{1,0:T(8,128)}, f32[8,512]{1,0:T(8,128)S(1)}, u32[]{:S(2)}) copy-start(f32[8,512]{1,0:T(8,128)S(1)} %fusion.8.owner_ref) | copy-start | bytes 49156
  39.4 38.0 %copy-start.5 = (bf16[32,4224]{1,0:T(8,128)(2,1)}, bf16[32,4224]{1,0:T(8,128)(2,1)S(1)}, u32[]{:S(2)}) copy-start(bf16[32,4224]{1,0:T(8,128)(2,1)S(1)} %collective-permute-done.4.refs_1_.refs_6_) | copy-start | bytes 811012
  39.4 38.0 %copy-start.6 = (bf16[32,4224]{1,0:T(8,128)(2,1)}, bf16[32,4224]{1,0:T(8,128)(2,1)S(1)}, u32[]{:S(2)}) copy-start(bf16[32,4224]{1,0:T(8,128)(2,1)S(1)} %collective-permute-done.5.refs_2_.refs_7_) | copy-start | bytes 811012
  39.4 15.0 %collective-permute-start.8 = (bf16[32,4224]{1,0:T(8,128)(2,1)S(1)}, bf16[32,4224]{1,0:T(8,128)(2,1)S(1)}, u32[]{:S(2)}, u32[]{:S(2)}) collective-permute-start(bf16[32,4224]{1,0:T(8,128)(2,1)S(1)} %collective-permute-done.4.refs_1_.refs_6_), channel_id=1, source_target_pairs={{4,0},{8,4},{5,1},{9,5},{6,2},{10,6},{7,3},{11,7},{20,16},{24,20},... | collective-permute-start | bytes 811016 | tf_op jit(solution)/shard_map/ppermute | solution.py:148
  40.1 14.9 %collective-permute-start.9 = (bf16[32,4224]{1,0:T(8,128)(2,1)S(1)}, bf16[32,4224]{1,0:T(8,128)(2,1)S(1)}, u32[]{:S(2)}, u32[]{:S(2)}) collective-permute-start(bf16[32,4224]{1,0:T(8,128)(2,1)S(1)} %collective-permute-done.5.refs_2_.refs_7_), channel_id=1, source_target_pairs={{4,8},{8,12},{5,9},{9,13},{6,10},{10,14},{7,11},{11,15},{20,24},{2... | collective-permute-start | bytes 811016 | tf_op jit(solution)/shard_map/ppermute | solution.py:149
  50.7 18.6 %copy-start.2 = (bf16[32,10752]{1,0:T(8,128)(2,1)}, bf16[32,10752]{1,0:T(8,128)(2,1)S(1)}, u32[]{:S(2)}) copy-start(bf16[32,10752]{1,0:T(8,128)(2,1)S(1)} %slice_select_fusion.second) | copy-start | bytes 2064388
  50.7 17.8 %collective-permute-start.6 = (bf16[32,10752]{1,0:T(8,128)(2,1)S(1)}, bf16[32,10752]{1,0:T(8,128)(2,1)S(1)}, u32[]{:S(2)}, u32[]{:S(2)}) collective-permute-start(bf16[32,10752]{1,0:T(8,128)(2,1)S(1)} %slice_select_fusion.second), channel_id=1, source_target_pairs={{4,0},{8,12},{5,1},{9,13},{6,2},{10,14},{7,3},{11,15},{20,16},{24,... | collective-permute-start | bytes 2064392 | tf_op jit(solution)/shard_map/ppermute | solution.py:153
  53.1 24.3 %copy-start.8 = (bf16[32,3584]{1,0:T(8,128)(2,1)}, bf16[32,3584]{1,0:T(8,128)(2,1)S(1)}, u32[]{:S(2)}) copy-start(bf16[32,3584]{1,0:T(8,128)(2,1)S(1)} %slice_select_fusion.1.second) | copy-start | bytes 688132
  53.1 24.3 %collective-permute-start.7 = (bf16[32,3584]{1,0:T(8,128)(2,1)S(1)}, bf16[32,3584]{1,0:T(8,128)(2,1)S(1)}, u32[]{:S(2)}, u32[]{:S(2)}) collective-permute-start(bf16[32,3584]{1,0:T(8,128)(2,1)S(1)} %slice_select_fusion.1.second), channel_id=1, source_target_pairs={{4,0},{8,12},{5,1},{9,13},{6,2},{10,14},{7,3},{11,15},{20,16},{24,... | collective-permute-start | bytes 688136 | tf_op jit(solution)/shard_map/ppermute | solution.py:156
  55.1 22.4 %copy-start.4 = (bf16[32,4224]{1,0:T(8,128)(2,1)}, bf16[32,4224]{1,0:T(8,128)(2,1)S(1)}, u32[]{:S(2)}) copy-start(bf16[32,4224]{1,0:T(8,128)(2,1)S(1)} %broadcast_select_fusion.refs_3_.refs_8_) | copy-start | bytes 811012
  55.1 27.0 %collective-permute-start.10 = (bf16[32,4224]{1,0:T(8,128)(2,1)S(1)}, bf16[32,4224]{1,0:T(8,128)(2,1)S(1)}, u32[]{:S(2)}, u32[]{:S(2)}) collective-permute-start(bf16[32,4224]{1,0:T(8,128)(2,1)S(1)} %broadcast_select_fusion.refs_3_.refs_8_), channel_id=1, source_target_pairs={{4,0},{8,12},{5,1},{9,13},{6,2},{10,14},{7,3},{11,15},{20,16},{24,... | collective-permute-start | bytes 811016 | tf_op jit(solution)/shard_map/ppermute | solution.py:159
  68.5 0.9 copy-start.9
  77.4 0.7 copy-start.10
  82.0 0.7 copy-start.7
  87.2 10.6 %collective-permute-start.11 = (f32[8,128]{1,0:T(8,128)}, f32[8,128]{1,0:T(8,128)S(1)}, u32[]{:S(2)}, u32[]{:S(2)}) collective-permute-start(f32[8,128]{1,0:T(8,128)} %score_shares.1), channel_id=1, source_target_pairs={{0,1},{1,2},{2,3},{3,0},{4,5},{5,6},{6,7},{7,4},{8,9},{9,10},{10,1... | collective-permute-start | bytes 12296 | tf_op jit(solution)/shard_map/ppermute | solution.py:174
  96.8 2.7 %collective-permute-start.12 = (f32[8,128]{1,0:T(8,128)}, f32[8,128]{1,0:T(8,128)S(1)}, u32[]{:S(2)}, u32[]{:S(2)}) collective-permute-start(f32[8,128]{1,0:T(8,128)} %score_shares.1), channel_id=1, source_target_pairs={{0,2},{1,3},{2,0},{3,1},{4,6},{5,7},{6,4},{7,5},{8,10},{9,11},{10,... | collective-permute-start | bytes 12296 | tf_op jit(solution)/shard_map/ppermute | solution.py:174
  97.1 3.2 %collective-permute-start.13 = (f32[8,128]{1,0:T(8,128)}, f32[8,128]{1,0:T(8,128)S(1)}, u32[]{:S(2)}, u32[]{:S(2)}) collective-permute-start(f32[8,128]{1,0:T(8,128)} %score_shares.1), channel_id=1, source_target_pairs={{0,3},{1,0},{2,1},{3,2},{4,7},{5,4},{6,5},{7,6},{8,11},{9,8},{10,9... | collective-permute-start | bytes 12296 | tf_op jit(solution)/shard_map/ppermute | solution.py:174

commit v2 on v1

v2 whole, which is shorter than its diff:
```python
import math

import jax
import jax.numpy as jnp
from jax import lax
from jax.experimental import pallas as pl
from jax.experimental.pallas import tpu as pltpu
from jax.sharding import PartitionSpec as P

FF = 14336
D = 4096
SEQ_DEV = 4
CSEQ = 16
LANES = 128
CUT = 10240
BLOCK = 2048
ROWS = (((1,), (1,)), ((), ()))


def gram(left, right):
    return lax.dot_general(left, right, ROWS, preferred_element_type=jnp.float32)


def exact(left, right, dims):
    return lax.dot_general(
        left, right, (dims, ((), ())), precision=lax.Precision.HIGHEST, preferred_element_type=jnp.float32
    )


def after(value, *earlier):
    return lax.optimization_barrier((value,) + earlier)[0]


def after2(one, two, earlier):
    return lax.optimization_barrier((one, two) + tuple(earlier))[:2]


def call(kernel, scalar, inputs, specs, steps, out, scratch, depth, name):
    return pl.pallas_call(
        kernel,
        grid_spec=pltpu.PrefetchScalarGridSpec(
            num_scalar_prefetch=1,
            grid=(steps,),
            in_specs=specs,
            out_specs=pl.BlockSpec(out, lambda k, s: (0, 0)),
            scratch_shapes=scratch,
        ),
        out_shape=jax.ShapeDtypeStruct(out, jnp.float32),
        cost_estimate=pl.CostEstimate(flops=512 * 256 * depth, bytes_accessed=1024 * depth, transcendentals=0),
        compiler_params=pltpu.CompilerParams(vmem_limit_bytes=60 << 20),
        name=name,
    )(scalar.reshape(1).astype(jnp.int32), *inputs)


def in_order(inner, own, first, middle, middle2, outer, outer2):
    return jnp.concatenate([own, first, jnp.where(inner, middle, outer), jnp.where(inner, middle2, outer2)], axis=0)


def cross_gram(base, train, low, place, pieces, first, count):
    rows, per = train.shape[0], pieces[0].shape[0]

    def kernel(place_ref, *refs):
        train_ref, out_ref = refs[-8], refs[-1]
        part = gram(train_ref[...], in_order(place_ref[0] == 1, *[r[...] for r in refs[-7:-1]]))

        @pl.when(pl.program_id(0) == 0)
        def _():
            out_ref[...] = part if base is None else refs[0][...] + part

        @pl.when(pl.program_id(0) > 0)
        def _():
            out_ref[...] += part

    specs = gram_specs(rows, per, low, first)
    inputs = (train,) + tuple(pieces)
    if base is not None:
        specs = [pl.BlockSpec((rows, 4 * per), lambda k, s: (0, 0))] + specs
        inputs = (base,) + inputs
    return call(kernel, place, inputs, specs, count, (rows, 4 * per), [], count * BLOCK, "cross_gram")


def gram_specs(rows, per, low, first):
    near = pl.BlockSpec((per, BLOCK), lambda k, s: (0, first + k))
    late = pl.BlockSpec((per, BLOCK), lambda k, s: (0, k))
    return [pl.BlockSpec((rows, BLOCK), lambda k, s: (0, low // BLOCK + k))] + [near] * 5 + [late]


def score_shares(x_gram, g_gram, owner_rows, self_terms, train, low, place, pieces, first, count, tags):
    rows, per = train.shape[0], pieces[0].shape[0]

    def kernel(place_ref, x_ref, g_ref, owner_ref, self_ref, *refs):
        inner, out_ref, total = place_ref[0] == 1, refs[-2], refs[-1]
        part = gram(refs[0][...], in_order(inner, *[r[...] for r in refs[1:7]]))

        @pl.when(pl.program_id(0) == 0)
        def _():
            total[...] = x_ref[...] + part

        @pl.when(pl.program_id(0) > 0)
        def _():
            total[...] += part

        @pl.when(pl.program_id(0) == count - 1)
        def _():
            by_train = exact(owner_ref[...], total[...] * g_ref[...], ((1,), (0,)))
            ids = in_order(inner, *[r[...].astype(jnp.float32) for r in refs[7:13]])
            lane = lax.broadcasted_iota(jnp.int32, ids.shape, 1)
            scores = exact(by_train, (ids == lane.astype(jnp.float32)).astype(jnp.float32), ((1,), (0,)))
            own = jnp.sum(self_ref[...], axis=1, keepdims=True)
            out_ref[...] = jnp.where(lax.broadcasted_iota(jnp.int32, scores.shape, 1) < CSEQ, scores, own)

    whole = pl.BlockSpec((rows, 4 * per), lambda k, s: (0, 0))
    seq = owner_rows.shape[0]
    specs = [
        whole,
        whole,
        pl.BlockSpec((seq, rows), lambda k, s: (0, 0)),
        pl.BlockSpec(self_terms.shape, lambda k, s: (0, 0)),
    ]
    specs = specs + gram_specs(rows, per, low, first)
    specs = specs + [pl.BlockSpec((per, LANES), lambda k, s, at=t.shape[1] // LANES - 1: (0, at)) for t in tags]
    inputs = (x_gram, g_gram, owner_rows, self_terms, train) + tuple(pieces) + tuple(tags)
    scratch = [pltpu.VMEM((rows, 4 * per), jnp.float32)]
    return call(kernel, place, inputs, specs, count, (seq, LANES), scratch, count * BLOCK, "score_shares")


SIDES = [(0, 1), (1, 0), (2, 3), (3, 2)]
MIDDLE = [(1, 2), (2, 1)]
OUTWARD = [(1, 0), (2, 3)]


def line_scores(train_acts, train_grads, owner_rows, self_terms, canary_acts, canary_grads, canary_segment):
    z = lax.axis_index("tok")
    place = jnp.where((z == 1) | (z == 2), 1, 0)
    tag = jnp.broadcast_to(canary_segment.astype(canary_grads.dtype)[:, None], (canary_segment.shape[0], LANES))
    x_own = canary_acts[:, :CUT]
    y_own = jnp.concatenate([canary_grads, canary_acts[:, CUT:], tag], axis=1)

    x_first = lax.ppermute(x_own, "tok", SIDES)
    x_middle = lax.ppermute(x_own, "tok", MIDDLE)
    y_first = lax.ppermute(y_own, "tok", SIDES)
    y_middle = lax.ppermute(y_own, "tok", MIDDLE)

    x_first, x_middle = after2(x_first, x_middle, ())
    x_middle2 = lax.ppermute(x_first, "tok", MIDDLE)
    x_outer = lax.ppermute(x_middle, "tok", OUTWARD)
    y_first, y_middle = after2(y_first, y_middle, (x_first, x_middle))
    y_middle2 = lax.ppermute(y_first, "tok", MIDDLE)
    y_outer = lax.ppermute(y_middle, "tok", OUTWARD)

    x_middle2, x_outer = after2(x_middle2, x_outer, (y_first, y_middle))
    far, last = [], ()
    for name, a, b in (("x", 0, 6144), ("x", 6144, CUT), ("y", 0, D), ("y", D, y_own.shape[1])):
        array = x_middle2 if name == "x" else y_middle2
        last = (after(array, *last)[:, a:b],)
        far.append(lax.ppermute(last[0], "tok", OUTWARD))
        if len(far) == 1:
            y_middle2, y_outer = after2(y_middle2, y_outer, last)
            last = (y_outer,)

    near = (x_own, x_first, x_middle, x_middle2, x_outer)
    x_gram = cross_gram(None, train_acts, 0, place, near + (far[0],), 0, 3)
    x_gram = cross_gram(x_gram, train_acts, 6144, place, near + (after(far[1], x_gram),), 3, 2)
    near = (y_own, y_first, y_middle, y_middle2, y_outer)
    g_gram = cross_gram(None, train_grads, 0, place, near + (after(far[2], x_gram),), 0, 2)
    rest = near + (after(far[3], g_gram),)
    return score_shares(x_gram, g_gram, owner_rows, self_terms, train_acts, CUT, place, rest, 2, 2, rest)


def finish(shares, canary_total):
    can = lax.axis_size("can")
    width = CSEQ // can
    total = shares
    for k in range(1, can):
        total = total + lax.ppermute(shares, "can", [(i, (i + k) % can) for i in range(can)])
    own = lax.dynamic_slice(total, (0, lax.axis_index("can") * width), (SEQ_DEV, width))
    scale = math.sqrt(FF * D * (canary_total / CSEQ))
    return own / (scale * jnp.sqrt(total[:SEQ_DEV, CSEQ] / (FF * D) + 1.0)[:, None])


def local(train_acts, train_grads, train_segment, canary_acts, canary_grads, canary_segment):
    tok, can = lax.axis_size("tok"), lax.axis_size("can")
    rows = train_acts.shape[0]
    canary_total = canary_acts.shape[0] * tok * can
    local_ids = train_segment - lax.axis_index("tok") * SEQ_DEV
    owner_rows = (jnp.arange(8, dtype=jnp.int32)[:, None] == local_ids[None, :]).astype(jnp.float32)

    share = rows // can
    start = lax.axis_index("can") * share
    pair = gram(train_acts, lax.dynamic_slice_in_dim(train_acts, start, share, 0))
    pair = pair * gram(train_grads, lax.dynamic_slice_in_dim(train_grads, start, share, 0))
    left = exact(owner_rows, pair, ((1,), (0,)))
    self_terms = left * lax.dynamic_slice_in_dim(owner_rows, start, share, 1)

    if tok == 4:
        shares = line_scores(
            train_acts, train_grads, owner_rows, self_terms, canary_acts, canary_grads, canary_segment
        )
    else:
        ids = lax.all_gather(canary_segment, "tok", axis=0, tiled=True)
        pair = gram(train_acts, lax.all_gather(canary_acts, "tok", axis=0, tiled=True))
        pair = pair * gram(train_grads, lax.all_gather(canary_grads, "tok", axis=0, tiled=True))
        member = (ids[:, None] == jnp.arange(CSEQ, dtype=jnp.int32)[None, :]).astype(jnp.float32)
        scores = exact(exact(owner_rows, pair, ((1,), (0,))), member, ((1,), (0,)))
        self_rows = jnp.broadcast_to(jnp.sum(self_terms, axis=1)[:, None], (8, LANES - CSEQ))
        shares = jnp.concatenate([scores, self_rows], axis=1)
    return finish(shares, canary_total)


def solution(mesh):
    placed = (
        P(("job", "tok"), None),
        P(("job", "tok"), None),
        P(("job", "tok")),
        P(("job", "tok", "can"), None),
        P(("job", "tok", "can"), None),
        P(("job", "tok", "can")),
    )
    return jax.shard_map(
        local, mesh=mesh, in_specs=placed, out_specs=P(("job", "tok"), "can"), check_vma=False
    )
```

time: 102 us -> 94.4 us (0.925)
  the two profiles are of different devices: /device:TPU:29 before, /device:TPU:0 now
where the time goes in v2:
time: 94.4 us; the launch traced here: 93.8 us
  waiting for transfers between devices  27.3 us (29%)
  starting transfers between devices  19.9 us (21%)
  Pallas kernels  18.7 us (20%)
  matrix products  17.8 us (19%)
  local copies, waits for them, and re-layouts  6.72 us (7%)
  other arithmetic  3.19 us (3%)
    pallas_call x4, Pallas kernels, call(): pl.pallas_call(kernel, grid_spec=pltpu.PrefetchScalarGridSpec(num_scalar_...  18.7 us
    dot_general x2, matrix products, gram(): lax.dot_general(left, right, ROWS, preferred_element_type=jnp.float32)  16.1 us
    ppermute x1, waiting for transfers between devices, line_scores(): y_outer = lax.ppermute(y_middle, 'tok', OUTWARD)  10 us
    ppermute x1, waiting for transfers between devices, line_scores(): y_first = lax.ppermute(y_own, 'tok', SIDES)  8.55 us
    ppermute x4, starting transfers between devices, line_scores(): far.append(lax.ppermute(last[0], 'tok', OUTWARD))  5.16 us
    unnamed x26, local copies, waits for them, and re-layouts  3.75 us
    ppermute x1, starting transfers between devices, line_scores(): y_first = lax.ppermute(y_own, 'tok', SIDES)  3.61 us
    ppermute x1, starting transfers between devices, line_scores(): x_first = lax.ppermute(x_own, 'tok', SIDES)  3.09 us
  transfers between devices with their start and end apart: 15, of which 7 were waited for; matrix products, arithmetic and copies ran while one was open for 23% of the time, Pallas kernels for 15%

profile of v2, /device:TPU:0, one launch (start us, length us, event | category | flops | bytes accessed | tf_op | source)
XLA Modules:
  0.0 93.8 jit_solution(9166390676823002828)
XLA Ops:
  0.0 1.1 %slice.21.refs_1_.refs_2_ = bf16[32,10240]{1,0:T(8,128)(2,1)S(1)} slice(bf16[32,14336]{1,0:T(8,128)(2,1)} %param.9), slice={[0:32], [0:10240]} | slice | bytes 1310720 | tf_op jit(solution)/shard_map/slice | solution.py:136
  1.1 0.0 copy-start.3
  1.1 3.1 %collective-permute-start = (bf16[32,10240]{1,0:T(8,128)(2,1)S(1)}, bf16[32,10240]{1,0:T(8,128)(2,1)S(1)}, u32[]{:S(2)}, u32[]{:S(2)}) collective-permute-start(bf16[32,10240]{1,0:T(8,128)(2,1)S(1)} %slice.21.refs_1_.refs_2_), channel_id=1, source_target_pairs={{0,4},{4,0},{8,12},{12,8},{1,5},{5,1},{9,13},{13,9},{2,6},{6,2},{1... | collective-permute-start | bytes 1966088 | tf_op jit(solution)/shard_map/ppermute | solution.py:139
  4.2 1.5 %collective-permute-start.1 = (bf16[32,10240]{1,0:T(8,128)(2,1)S(1)}, bf16[32,10240]{1,0:T(8,128)(2,1)}, u32[]{:S(2)}, u32[]{:S(2)}) collective-permute-start(bf16[32,10240]{1,0:T(8,128)(2,1)S(1)} %slice.21.refs_1_.refs_2_), channel_id=1, source_target_pairs={{4,8},{8,4},{5,9},{9,5},{6,10},{10,6},{7,11},{11,7},{20,24},{24,20... | collective-permute-start | bytes 1966088 | tf_op jit(solution)/shard_map/ppermute | solution.py:140
  5.8 1.0 %slice.22 = bf16[32,4096]{1,0:T(8,128)(2,1)S(1)} slice(bf16[32,14336]{1,0:T(8,128)(2,1)} %param.9), slice={[0:32], [10240:14336]} | slice | bytes 524288 | tf_op jit(solution)/shard_map/slice | solution.py:137
  6.7 0.7 convert_element_type.6
  7.4 0.1 broadcast_in_dim.2
  7.5 1.0 %pad_maximum_fusion.refs_1_.refs_7_ = bf16[32,8320]{1,0:T(8,128)(2,1)S(1)} fusion(bf16[32,128]{1,0:T(8,128)(2,1)S(1)} %broadcast_in_dim.2, bf16[32,4096]{1,0:T(8,128)(2,1)S(1)} %slice.22, bf16[32,4096]{1,0:T(8,128)(2,1)} %param.10), kind=kLoop, calls=%fused_computation.6 | loop fusion | flops 1597440 | bytes 1064960 | tf_op jit(solution)/shard_map/concatenate | solution.py:137
  8.4 0.0 copy-start
  8.5 3.6 %collective-permute-start.4 = (bf16[32,8320]{1,0:T(8,128)(2,1)S(1)}, bf16[32,8320]{1,0:T(8,128)(2,1)S(1)}, u32[]{:S(2)}, u32[]{:S(2)}) collective-permute-start(bf16[32,8320]{1,0:T(8,128)(2,1)S(1)} %pad_maximum_fusion.refs_1_.refs_7_), channel_id=1, source_target_pairs={{0,4},{4,0},{8,12},{12,8},{1,5},{5,1},{9,13},{13,9},{2,6},{6,2},{1... | collective-permute-start | bytes 1597448 | tf_op jit(solution)/shard_map/ppermute | solution.py:141
  12.1 0.7 collective-permute-start.5
  12.8 4.0 %fusion.5 = f32[128,512]{1,0:T(8,128)S(1)} fusion(bf16[512,4096]{1,0:T(8,128)(2,1)} %refs_0_.4, s32[]{:T(128)S(6)} %select_n.13), kind=kOutput, calls=%fused_computation.4 | convolution fusion | flops 536870912 | bytes 5505028 | tf_op jit(solution)/shard_map/dot_general | solution.py:21
  16.8 0.0 copy-start.12
  16.8 3.0 %collective-permute-done.refs_2_.refs_3_ = bf16[32,10240]{1,0:T(8,128)(2,1)S(1)} collective-permute-done((bf16[32,10240]{1,0:T(8,128)(2,1)S(1)}, bf16[32,10240]{1,0:T(8,128)(2,1)S(1)}, u32[]{:S(2)}, u32[]{:S(2)}) %collective-permute-start) | collective-permute-done | bytes 655392 | tf_op jit(solution)/shard_map/ppermute | solution.py:139
  19.8 0.9 copy-done.6
  20.7 0.0 collective-permute-done.1.refs_3_.refs_4_
  20.7 0.7 collective-permute-start.2
  21.4 1.3 %collective-permute-start.3 = (bf16[32,10240]{1,0:T(8,128)(2,1)}, bf16[32,10240]{1,0:T(8,128)(2,1)}, u32[]{:S(2)}, u32[]{:S(2)}) collective-permute-start(bf16[32,10240]{1,0:T(8,128)(2,1)} %collective-permute-done.1.refs_3_.refs_4_), channel_id=1, source_target_pairs={{4,0},{8,12},{5,1},{9,13},{6,2},{10,14},{7,3},{11,15},{20,16},{24,... | collective-permute-start | bytes 1966088 | tf_op jit(solution)/shard_map/ppermute | solution.py:146
  22.7 8.5 %collective-permute-done.4.refs_2_.refs_8_ = bf16[32,8320]{1,0:T(8,128)(2,1)S(1)} collective-permute-done((bf16[32,8320]{1,0:T(8,128)(2,1)S(1)}, bf16[32,8320]{1,0:T(8,128)(2,1)S(1)}, u32[]{:S(2)}, u32[]{:S(2)}) %collective-permute-start.4) | collective-permute-done | bytes 532512 | tf_op jit(solution)/shard_map/ppermute | solution.py:141
  31.2 0.0 collective-permute-done.5.refs_3_.refs_9_
  31.2 0.7 collective-permute-start.7
  31.9 1.3 %collective-permute-start.8 = (bf16[32,8320]{1,0:T(8,128)(2,1)S(1)}, bf16[32,8320]{1,0:T(8,128)(2,1)}, u32[]{:S(2)}, u32[]{:S(2)}) collective-permute-start(bf16[32,8320]{1,0:T(8,128)(2,1)S(1)} %collective-permute-done.5.refs_3_.refs_9_), channel_id=1, source_target_pairs={{4,0},{8,12},{5,1},{9,13},{6,2},{10,14},{7,3},{11,15},{20,16},{24,... | collective-permute-start | bytes 1597448 | tf_op jit(solution)/shard_map/ppermute | solution.py:149
  33.2 12.0 %fusion.2 = f32[128,512]{1,0:T(8,128)} fusion(f32[128,512]{1,0:T(8,128)S(1)} %fusion.5, bf16[512,14336]{1,0:T(8,128)(2,1)} %refs_0_.5, s32[]{:T(128)S(6)} %select_n.13), kind=kOutput, calls=%fused_computation.2 | convolution fusion | flops 1879113728 | bytes 18874372 | tf_op jit(solution)/shard_map/dot_general | solution.py:21
  45.2 0.0 copy-done.3
  45.2 0.0 copy-done
  45.2 0.0 copy-done.4
  45.2 0.0 copy-done.5
  45.2 0.0 copy-done.12
  45.3 0.0 collective-permute-done.2.refs_4_.refs_5_
  45.3 0.0 copy-start.2
  45.3 0.9 collective-permute-done.3.refs_5_.refs_6_
  46.2 1.3 %collective-permute-start.6 = (bf16[32,6144]{1,0:T(8,128)(2,1)S(1)}, bf16[32,6144]{1,0:T(8,128)(2,1)S(1)}, u32[]{:S(2)}, u32[]{:S(2)}) collective-permute-start(bf16[32,6144]{1,0:T(8,128)(2,1)S(1)} %slice.28), channel_id=1, source_target_pairs={{4,0},{8,12},{5,1},{9,13},{6,2},{10,14},{7,3},{11,15},{20,16},{24,... | collective-permute-start | bytes 1179656 | tf_op jit(solution)/shard_map/ppermute | solution.py:156
  47.5 0.0 collective-permute-done.7.refs_4_.refs_10_
  47.5 0.0 copy-start.1
  47.5 10.0 %collective-permute-done.8.refs_5_.refs_11_ = bf16[32,8320]{1,0:T(8,128)(2,1)} collective-permute-done((bf16[32,8320]{1,0:T(8,128)(2,1)S(1)}, bf16[32,8320]{1,0:T(8,128)(2,1)}, u32[]{:S(2)}, u32[]{:S(2)}) %collective-permute-start.8) | collective-permute-done | bytes 532512 | tf_op jit(solution)/shard_map/ppermute | solution.py:149
  57.6 0.7 slice.24
  58.3 1.3 %collective-permute-start.9 = (bf16[32,4096]{1,0:T(8,128)(2,1)}, bf16[32,4096]{1,0:T(8,128)(2,1)S(1)}, u32[]{:S(2)}, u32[]{:S(2)}) collective-permute-start(bf16[32,4096]{1,0:T(8,128)(2,1)} %slice.24), channel_id=1, source_target_pairs={{4,0},{8,12},{5,1},{9,13},{6,2},{10,14},{7,3},{11,15},{20,16},{24,... | collective-permute-start | bytes 786440 | tf_op jit(solution)/shard_map/ppermute | solution.py:156
  59.6 1.3 %collective-permute-start.10 = (bf16[32,4096]{1,0:T(8,128)(2,1)S(1)}, bf16[32,4096]{1,0:T(8,128)(2,1)S(1)}, u32[]{:S(2)}, u32[]{:S(2)}) collective-permute-start(bf16[32,4096]{1,0:T(8,128)(2,1)S(1)} %slice.25), channel_id=1, source_target_pairs={{4,0},{8,12},{5,1},{9,13},{6,2},{10,14},{7,3},{11,15},{20,16},{24,... | collective-permute-start | bytes 786440 | tf_op jit(solution)/shard_map/ppermute | solution.py:156
  61.0 1.3 %collective-permute-start.11 = (bf16[32,4224]{1,0:T(8,128)(2,1)S(1)}, bf16[32,4224]{1,0:T(8,128)(2,1)S(1)}, u32[]{:S(2)}, u32[]{:S(2)}) collective-permute-start(bf16[32,4224]{1,0:T(8,128)(2,1)S(1)} %slice.26), channel_id=1, source_target_pairs={{4,0},{8,12},{5,1},{9,13},{6,2},{10,14},{7,3},{11,15},{20,16},{24,... | collective-permute-start | bytes 811016 | tf_op jit(solution)/shard_map/ppermute | solution.py:156
  62.3 1.8 %convolution_multiply_fusion.self_ref = f32[8,128]{1,0:T(8,128)} fusion(f32[128,512]{1,0:T(8,128)} %fusion.2, s32[512]{0:T(512)S(1)} %broadcast_subtract_fusion, f32[8,512]{1,0:T(8,128)S(1)} %fusion.7.owner_ref, s32[]{:T(128)S(6)} %select_n.13), kind=kOutput, calls=%fused_computation.3 | convolution fusion | flops 6296576 | bytes 272388 | tf_op jit(solution)/shard_map/dot_general | solution.py:25
  64.1 1.7 %collective-permute-done.6.refs_6_ = bf16[32,6144]{1,0:T(8,128)(2,1)S(1)} collective-permute-done((bf16[32,6144]{1,0:T(8,128)(2,1)S(1)}, bf16[32,6144]{1,0:T(8,128)(2,1)S(1)}, u32[]{:S(2)}, u32[]{:S(2)}) %collective-permute-start.6) | collective-permute-done | bytes 393248 | tf_op jit(solution)/shard_map/ppermute | solution.py:156
  65.8 0.0 copy-done.2
  65.8 0.7 copy-done.8
  66.5 5.8 %cross_gram.3.refs_0_ = f32[512,128]{1,0:T(8,128)} custom-call(s32[1]{0:T(128)} %bitcast.place_ref, bf16[512,14336]{1,0:T(8,128)(2,1)} %refs_0_.5, bf16[32,10240]{1,0:T(8,128)(2,1)} %copy-done.3, bf16[32,10240]{1,0:T(8,128)(2,1)} %copy-done.6, bf16[32,10240]{1,0:T(8,128)(2,1)} %collective-permute-done.1.refs_3_.refs_4_, bf16[32,10240]{1,0:T(8,128)(2,1)} %copy-done.2, ...), custom_call_target="tpu_custom_call" | custom-call | flops 805306368 | bytes 6291456 | tf_op jit(solution)/shard_map/cross_gram/pallas_call | solution.py:39
  72.3 0.0 copy-done.11
  72.3 0.0 collective-permute-done.9.refs_7_
  72.3 0.0 copy-start.9
  72.3 0.7 copy-done.9
  73.1 4.3 %cross_gram.4.x_ref = f32[512,128]{1,0:T(8,128)} custom-call(s32[1]{0:T(128)} %bitcast.place_ref, f32[512,128]{1,0:T(8,128)} %cross_gram.3.refs_0_, bf16[512,14336]{1,0:T(8,128)(2,1)} %refs_0_.5, bf16[32,10240]{1,0:T(8,128)(2,1)} %copy-done.3, bf16[32,10240]{1,0:T(8,128)(2,1)} %copy-done.6, bf16[32,10240]{1,0:T(8,128)(2,1)} %collective-permute-done.1.refs_3_.refs_4_, ...), custom_call_target="tpu_custom_call" | custom-call | flops 536870912 | bytes 4194304 | tf_op jit(solution)/shard_map/cross_gram/pallas_call | solution.py:39
  77.3 0.0 collective-permute-done.10.refs_6_
  77.3 0.7 copy-done.10
  78.0 4.0 %cross_gram.5.g_ref = f32[512,128]{1,0:T(8,128)} custom-call(s32[1]{0:T(128)} %bitcast.place_ref, bf16[512,4096]{1,0:T(8,128)(2,1)} %refs_0_.4, bf16[32,8320]{1,0:T(8,128)(2,1)} %copy-done, bf16[32,8320]{1,0:T(8,128)(2,1)} %copy-done.4, bf16[32,8320]{1,0:T(8,128)(2,1)} %copy-done.5, bf16[32,8320]{1,0:T(8,128)(2,1)} %copy-done.1, ...), custom_call_target="tpu_custom_call" | custom-call | flops 536870912 | bytes 4194304 | tf_op jit(solution)/shard_map/cross_gram/pallas_call | solution.py:39
  82.0 0.0 collective-permute-done.11.refs_6_.refs_12_
  82.0 0.7 copy-done.7
  82.7 4.6 %score_shares.1 = f32[8,128]{1,0:T(8,128)} custom-call(s32[1]{0:T(128)} %bitcast.place_ref, f32[512,128]{1,0:T(8,128)} %cross_gram.4.x_ref, f32[512,128]{1,0:T(8,128)} %cross_gram.5.g_ref, f32[8,512]{1,0:T(8,128)} %copy-done.11, f32[8,128]{1,0:T(8,128)} %convolution_multiply_fusion.self_ref, bf16[512,14336]{1,0:T(8,128)(2,1)} %refs_0_.5, ...), custom_call_target="tpu_custom_call" | custom-call | flops 536870912 | bytes 4194304 | tf_op jit(solution)/shard_map/score_shares/pallas_call | solution.py:39
  87.4 0.0 collective-permute-start.14
  87.4 1.7 %collective-permute-start.13 = (f32[8,128]{1,0:T(8,128)}, f32[8,128]{1,0:T(8,128)S(1)}, u32[]{:S(2)}, u32[]{:S(2)}) collective-permute-start(f32[8,128]{1,0:T(8,128)} %score_shares.1), channel_id=1, source_target_pairs={{0,2},{1,3},{2,0},{3,1},{4,6},{5,7},{6,4},{7,5},{8,10},{9,11},{10,... | collective-permute-start | bytes 12296 | tf_op jit(solution)/shard_map/ppermute | solution.py:175
  89.1 0.2 collective-permute-start.12
  89.2 0.0 collective-permute-done.14
  89.2 2.0 %collective-permute-done.13 = f32[8,128]{1,0:T(8,128)S(1)} collective-permute-done((f32[8,128]{1,0:T(8,128)}, f32[8,128]{1,0:T(8,128)S(1)}, u32[]{:S(2)}, u32[]{:S(2)}) %collective-permute-start.13) | collective-permute-done | bytes 4128 | tf_op jit(solution)/shard_map/ppermute | solution.py:175
  91.3 1.0 %collective-permute-done.12 = f32[8,128]{1,0:T(8,128)S(1)} collective-permute-done((f32[8,128]{1,0:T(8,128)}, f32[8,128]{1,0:T(8,128)S(1)}, u32[]{:S(2)}, u32[]{:S(2)}) %collective-permute-start.12) | collective-permute-done | bytes 4128 | tf_op jit(solution)/shard_map/ppermute | solution.py:175
  92.3 0.7 add_add_fusion
  93.0 0.2 multiply_reduce_fusion
  93.2 0.7 dynamic-slice_divide_fusion
  (13 shorter events, 0.1 us)
Async XLA Ops:
  1.1 44.1 %copy-start.3 = (bf16[32,10240]{1,0:T(8,128)(2,1)}, bf16[32,10240]{1,0:T(8,128)(2,1)S(1)}, u32[]{:S(2)}) copy-start(bf16[32,10240]{1,0:T(8,128)(2,1)S(1)} %slice.21.refs_1_.refs_2_) | copy-start | bytes 1966084
  1.1 18.6 %collective-permute-start = (bf16[32,10240]{1,0:T(8,128)(2,1)S(1)}, bf16[32,10240]{1,0:T(8,128)(2,1)S(1)}, u32[]{:S(2)}, u32[]{:S(2)}) collective-permute-start(bf16[32,10240]{1,0:T(8,128)(2,1)S(1)} %slice.21.refs_1_.refs_2_), channel_id=1, source_target_pairs={{0,4},{4,0},{8,12},{12,8},{1,5},{5,1},{9,13},{13,9},{2,6},{6,2},{1... | collective-permute-start | bytes 1966088 | tf_op jit(solution)/shard_map/ppermute | solution.py:139
  4.2 16.4 %collective-permute-start.1 = (bf16[32,10240]{1,0:T(8,128)(2,1)S(1)}, bf16[32,10240]{1,0:T(8,128)(2,1)}, u32[]{:S(2)}, u32[]{:S(2)}) collective-permute-start(bf16[32,10240]{1,0:T(8,128)(2,1)S(1)} %slice.21.refs_1_.refs_2_), channel_id=1, source_target_pairs={{4,8},{8,4},{5,9},{9,5},{6,10},{10,6},{7,11},{11,7},{20,24},{24,20... | collective-permute-start | bytes 1966088 | tf_op jit(solution)/shard_map/ppermute | solution.py:140
  8.4 36.8 %copy-start = (bf16[32,8320]{1,0:T(8,128)(2,1)}, bf16[32,8320]{1,0:T(8,128)(2,1)S(1)}, u32[]{:S(2)}) copy-start(bf16[32,8320]{1,0:T(8,128)(2,1)S(1)} %pad_maximum_fusion.refs_1_.refs_7_) | copy-start | bytes 1597444
  8.5 22.7 %collective-permute-start.4 = (bf16[32,8320]{1,0:T(8,128)(2,1)S(1)}, bf16[32,8320]{1,0:T(8,128)(2,1)S(1)}, u32[]{:S(2)}, u32[]{:S(2)}) collective-permute-start(bf16[32,8320]{1,0:T(8,128)(2,1)S(1)} %pad_maximum_fusion.refs_1_.refs_7_), channel_id=1, source_target_pairs={{0,4},{4,0},{8,12},{12,8},{1,5},{5,1},{9,13},{13,9},{2,6},{6,2},{1... | collective-permute-start | bytes 1597448 | tf_op jit(solution)/shard_map/ppermute | solution.py:141
  12.1 19.1 %collective-permute-start.5 = (bf16[32,8320]{1,0:T(8,128)(2,1)S(1)}, bf16[32,8320]{1,0:T(8,128)(2,1)S(1)}, u32[]{:S(2)}, u32[]{:S(2)}) collective-permute-start(bf16[32,8320]{1,0:T(8,128)(2,1)S(1)} %pad_maximum_fusion.refs_1_.refs_7_), channel_id=1, source_target_pairs={{4,8},{8,4},{5,9},{9,5},{6,10},{10,6},{7,11},{11,7},{20,24},{24,20... | collective-permute-start | bytes 1597448 | tf_op jit(solution)/shard_map/ppermute | solution.py:142
  16.8 28.4 %copy-start.12 = (s32[512]{0:T(512)S(1)}, s32[512]{0:T(512)}, u32[]{:S(2)}) copy-start(s32[512]{0:T(512)} %param.8) | copy-start | bytes 6148
  19.8 0.9 copy-start.6
  20.7 24.6 %collective-permute-start.2 = (bf16[32,10240]{1,0:T(8,128)(2,1)}, bf16[32,10240]{1,0:T(8,128)(2,1)S(1)}, u32[]{:S(2)}, u32[]{:S(2)}) collective-permute-start(bf16[32,10240]{1,0:T(8,128)(2,1)} %copy-done.6), channel_id=1, source_target_pairs={{4,8},{8,4},{5,9},{9,5},{6,10},{10,6},{7,11},{11,7},{20,24},{24,20... | collective-permute-start | bytes 1966088 | tf_op jit(solution)/shard_map/ppermute | solution.py:145
  21.4 24.8 %collective-permute-start.3 = (bf16[32,10240]{1,0:T(8,128)(2,1)}, bf16[32,10240]{1,0:T(8,128)(2,1)}, u32[]{:S(2)}, u32[]{:S(2)}) collective-permute-start(bf16[32,10240]{1,0:T(8,128)(2,1)} %collective-permute-done.1.refs_3_.refs_4_), channel_id=1, source_target_pairs={{4,0},{8,12},{5,1},{9,13},{6,2},{10,14},{7,3},{11,15},{20,16},{24,... | collective-permute-start | bytes 1966088 | tf_op jit(solution)/shard_map/ppermute | solution.py:146
  31.2 14.0 %copy-start.4 = (bf16[32,8320]{1,0:T(8,128)(2,1)}, bf16[32,8320]{1,0:T(8,128)(2,1)S(1)}, u32[]{:S(2)}) copy-start(bf16[32,8320]{1,0:T(8,128)(2,1)S(1)} %collective-permute-done.4.refs_2_.refs_8_) | copy-start | bytes 1597444
  31.2 14.0 %copy-start.5 = (bf16[32,8320]{1,0:T(8,128)(2,1)}, bf16[32,8320]{1,0:T(8,128)(2,1)S(1)}, u32[]{:S(2)}) copy-start(bf16[32,8320]{1,0:T(8,128)(2,1)S(1)} %collective-permute-done.5.refs_3_.refs_9_) | copy-start | bytes 1597444
  31.2 16.3 %collective-permute-start.7 = (bf16[32,8320]{1,0:T(8,128)(2,1)S(1)}, bf16[32,8320]{1,0:T(8,128)(2,1)S(1)}, u32[]{:S(2)}, u32[]{:S(2)}) collective-permute-start(bf16[32,8320]{1,0:T(8,128)(2,1)S(1)} %collective-permute-done.4.refs_2_.refs_8_), channel_id=1, source_target_pairs={{4,8},{8,4},{5,9},{9,5},{6,10},{10,6},{7,11},{11,7},{20,24},{24,20... | collective-permute-start | bytes 1597448 | tf_op jit(solution)/shard_map/ppermute | solution.py:148
  31.9 25.7 %collective-permute-start.8 = (bf16[32,8320]{1,0:T(8,128)(2,1)S(1)}, bf16[32,8320]{1,0:T(8,128)(2,1)}, u32[]{:S(2)}, u32[]{:S(2)}) collective-permute-start(bf16[32,8320]{1,0:T(8,128)(2,1)S(1)} %collective-permute-done.5.refs_3_.refs_9_), channel_id=1, source_target_pairs={{4,0},{8,12},{5,1},{9,13},{6,2},{10,14},{7,3},{11,15},{20,16},{24,... | collective-permute-start | bytes 1597448 | tf_op jit(solution)/shard_map/ppermute | solution.py:149
  45.3 20.5 %copy-start.2 = (bf16[32,10240]{1,0:T(8,128)(2,1)}, bf16[32,10240]{1,0:T(8,128)(2,1)S(1)}, u32[]{:S(2)}) copy-start(bf16[32,10240]{1,0:T(8,128)(2,1)S(1)} %collective-permute-done.2.refs_4_.refs_5_) | copy-start | bytes 1966084
  46.2 19.6 %collective-permute-start.6 = (bf16[32,6144]{1,0:T(8,128)(2,1)S(1)}, bf16[32,6144]{1,0:T(8,128)(2,1)S(1)}, u32[]{:S(2)}, u32[]{:S(2)}) collective-permute-start(bf16[32,6144]{1,0:T(8,128)(2,1)S(1)} %slice.28), channel_id=1, source_target_pairs={{4,0},{8,12},{5,1},{9,13},{6,2},{10,14},{7,3},{11,15},{20,16},{24,... | collective-permute-start | bytes 1179656 | tf_op jit(solution)/shard_map/ppermute | solution.py:156
  47.5 24.8 %copy-start.11 = (f32[8,512]{1,0:T(8,128)}, f32[8,512]{1,0:T(8,128)S(1)}, u32[]{:S(2)}) copy-start(f32[8,512]{1,0:T(8,128)S(1)} %fusion.7.owner_ref) | copy-start | bytes 49156
  47.5 24.8 %copy-start.1 = (bf16[32,8320]{1,0:T(8,128)(2,1)}, bf16[32,8320]{1,0:T(8,128)(2,1)S(1)}, u32[]{:S(2)}) copy-start(bf16[32,8320]{1,0:T(8,128)(2,1)S(1)} %collective-permute-done.7.refs_4_.refs_10_) | copy-start | bytes 1597444
  58.3 14.0 %collective-permute-start.9 = (bf16[32,4096]{1,0:T(8,128)(2,1)}, bf16[32,4096]{1,0:T(8,128)(2,1)S(1)}, u32[]{:S(2)}, u32[]{:S(2)}) collective-permute-start(bf16[32,4096]{1,0:T(8,128)(2,1)} %slice.24), channel_id=1, source_target_pairs={{4,0},{8,12},{5,1},{9,13},{6,2},{10,14},{7,3},{11,15},{20,16},{24,... | collective-permute-start | bytes 786440 | tf_op jit(solution)/shard_map/ppermute | solution.py:156
  59.6 17.7 %collective-permute-start.10 = (bf16[32,4096]{1,0:T(8,128)(2,1)S(1)}, bf16[32,4096]{1,0:T(8,128)(2,1)S(1)}, u32[]{:S(2)}, u32[]{:S(2)}) collective-permute-start(bf16[32,4096]{1,0:T(8,128)(2,1)S(1)} %slice.25), channel_id=1, source_target_pairs={{4,0},{8,12},{5,1},{9,13},{6,2},{10,14},{7,3},{11,15},{20,16},{24,... | collective-permute-start | bytes 786440 | tf_op jit(solution)/shard_map/ppermute | solution.py:156
  61.0 21.1 %collective-permute-start.11 = (bf16[32,4224]{1,0:T(8,128)(2,1)S(1)}, bf16[32,4224]{1,0:T(8,128)(2,1)S(1)}, u32[]{:S(2)}, u32[]{:S(2)}) collective-permute-start(bf16[32,4224]{1,0:T(8,128)(2,1)S(1)} %slice.26), channel_id=1, source_target_pairs={{4,0},{8,12},{5,1},{9,13},{6,2},{10,14},{7,3},{11,15},{20,16},{24,... | collective-permute-start | bytes 811016 | tf_op jit(solution)/shard_map/ppermute | solution.py:156
  65.8 0.7 copy-start.8
  72.3 0.7 copy-start.9
  77.3 0.7 copy-start.10
  82.0 0.7 copy-start.7
  87.4 1.8 %collective-permute-start.14 = (f32[8,128]{1,0:T(8,128)}, f32[8,128]{1,0:T(8,128)S(1)}, u32[]{:S(2)}, u32[]{:S(2)}) collective-permute-start(f32[8,128]{1,0:T(8,128)} %score_shares.1), channel_id=1, source_target_pairs={{0,3},{1,0},{2,1},{3,2},{4,7},{5,4},{6,5},{7,6},{8,11},{9,8},{10,9... | collective-permute-start | bytes 12296 | tf_op jit(solution)/shard_map/ppermute | solution.py:175
  87.4 3.9 %collective-permute-start.13 = (f32[8,128]{1,0:T(8,128)}, f32[8,128]{1,0:T(8,128)S(1)}, u32[]{:S(2)}, u32[]{:S(2)}) collective-permute-start(f32[8,128]{1,0:T(8,128)} %score_shares.1), channel_id=1, source_target_pairs={{0,2},{1,3},{2,0},{3,1},{4,6},{5,7},{6,4},{7,5},{8,10},{9,11},{10,... | collective-permute-start | bytes 12296 | tf_op jit(solution)/shard_map/ppermute | solution.py:175
  89.1 3.2 %collective-permute-start.12 = (f32[8,128]{1,0:T(8,128)}, f32[8,128]{1,0:T(8,128)S(1)}, u32[]{:S(2)}, u32[]{:S(2)}) collective-permute-start(f32[8,128]{1,0:T(8,128)} %score_shares.1), channel_id=1, source_target_pairs={{0,1},{1,2},{2,3},{3,0},{4,5},{5,6},{6,7},{7,4},{8,9},{9,10},{10,1... | collective-permute-start | bytes 12296 | tf_op jit(solution)/shard_map/ppermute | solution.py:175

commit v3 on v2

v3 whole, which is shorter than its diff:
```python
import math

import jax
import jax.numpy as jnp
from jax import lax
from jax.experimental import pallas as pl
from jax.experimental.pallas import tpu as pltpu
from jax.sharding import PartitionSpec as P

FF = 14336
D = 4096
SEQ_DEV = 4
CSEQ = 16
LANES = 128
CUT = 10240
SPLIT = 6144
BLOCK = 2048
ROWS = (((1,), (1,)), ((), ()))


def gram(left, right):
    return lax.dot_general(left, right, ROWS, preferred_element_type=jnp.float32)


def exact(left, right, dims):
    return lax.dot_general(
        left, right, (dims, ((), ())), precision=lax.Precision.HIGHEST, preferred_element_type=jnp.float32
    )


def after(value, *earlier):
    return lax.optimization_barrier((value,) + earlier)[0]


def after2(one, two, earlier):
    return lax.optimization_barrier((one, two) + tuple(earlier))[:2]


def call(kernel, inputs, specs, steps, out, scratch, depth, name):
    shapes = out if isinstance(out, list) else [out]
    result = pl.pallas_call(
        kernel,
        grid=(steps,),
        in_specs=specs,
        out_specs=[pl.BlockSpec(shape, lambda k: (0, 0)) for shape in shapes],
        scratch_shapes=scratch,
        out_shape=[jax.ShapeDtypeStruct(shape, jnp.float32) for shape in shapes],
        cost_estimate=pl.CostEstimate(flops=512 * 256 * depth, bytes_accessed=1024 * depth, transcendentals=0),
        compiler_params=pltpu.CompilerParams(vmem_limit_bytes=64 << 20),
        name=name,
    )(*inputs)
    return result if isinstance(out, list) else result[0]


def is_inner():
    z = lax.axis_index("tok")
    return (z == 1) | (z == 2)


def in_order(inner, own, first, middle, middle2, outer, outer2):
    return jnp.concatenate([own, first, jnp.where(inner, middle, outer), jnp.where(inner, middle2, outer2)], axis=0)


def cross_gram(base, train, low, pieces, first, count):
    rows, per = train.shape[0], pieces[0].shape[0]

    def kernel(*refs):
        train_ref, out_ref = refs[-8], refs[-1]
        part = gram(train_ref[...], in_order(is_inner(), *[r[...] for r in refs[-7:-1]]))

        @pl.when(pl.program_id(0) == 0)
        def _():
            out_ref[...] = part if base is None else refs[0][...] + part

        @pl.when(pl.program_id(0) > 0)
        def _():
            out_ref[...] += part

    specs = gram_specs(rows, per, low, first)
    inputs = (train,) + tuple(pieces)
    if base is not None:
        specs = [pl.BlockSpec((rows, 4 * per), lambda k: (0, 0))] + specs
        inputs = (base,) + inputs
    return call(kernel, inputs, specs, count, (rows, 4 * per), [], count * BLOCK, "cross_gram")


def gram_specs(rows, per, low, first):
    near = pl.BlockSpec((per, BLOCK), lambda k: (0, first + k))
    late = pl.BlockSpec((per, BLOCK), lambda k: (0, k))
    return [pl.BlockSpec((rows, BLOCK), lambda k: (0, low // BLOCK + k))] + [near] * 5 + [late]


def score_shares(x_gram, g_gram, owner_rows, self_terms, train, low, pieces, first, tags):
    rows, per = train.shape[0], pieces[0].shape[0]
    count = (train.shape[1] - low) // BLOCK
    can = lax.axis_size("can")
    width = CSEQ // can

    def kernel(x_ref, g_ref, owner_ref, self_ref, *refs):
        inner, total = is_inner(), refs[-1]
        part = gram(refs[0][...], in_order(inner, *[r[...] for r in refs[1:7]]))

        @pl.when(pl.program_id(0) == 0)
        def _():
            total[...] = x_ref[...] + part

        @pl.when(pl.program_id(0) > 0)
        def _():
            total[...] += part

        @pl.when(pl.program_id(0) == count - 1)
        def _():
            by_train = exact(owner_ref[...], total[...] * g_ref[...], ((1,), (0,)))
            ids = in_order(inner, *[r[...].astype(jnp.float32) for r in refs[7:13]])
            lane = lax.broadcasted_iota(jnp.int32, ids.shape, 1)
            scores = exact(by_train, (ids == lane.astype(jnp.float32)).astype(jnp.float32), ((1,), (0,)))
            own = jnp.sum(self_ref[...], axis=1, keepdims=True)
            lane = lax.broadcasted_iota(jnp.int32, scores.shape, 1)
            for k in range(can):
                to = lax.rem(lax.axis_index("can") + k, can)
                shifted = pltpu.roll(scores, lax.rem(LANES - to * width, LANES), 1)
                refs[13 + k][...] = jnp.where(lane < width, shifted, own)

    whole = pl.BlockSpec((rows, 4 * per), lambda k: (0, 0))
    seq = owner_rows.shape[0]
    specs = [
        whole,
        whole,
        pl.BlockSpec((seq, rows), lambda k: (0, 0)),
        pl.BlockSpec(self_terms.shape, lambda k: (0, 0)),
    ]
    specs = specs + gram_specs(rows, per, low, first)
    specs = specs + [pl.BlockSpec((per, LANES), lambda k, at=t.shape[1] // LANES - 1: (0, at)) for t in tags]
    inputs = (x_gram, g_gram, owner_rows, self_terms, train) + tuple(pieces) + tuple(tags)
    scratch = [pltpu.VMEM((rows, 4 * per), jnp.float32)]
    return call(kernel, inputs, specs, count, [(seq, LANES)] * can, scratch, count * BLOCK, "score_shares")


SIDES = [(0, 1), (1, 0), (2, 3), (3, 2)]
MIDDLE = [(1, 2), (2, 1)]
OUTWARD = [(1, 0), (2, 3)]


def line_scores(train_acts, train_grads, owner_rows, self_terms, canary_acts, canary_grads, canary_segment):
    tag = jnp.broadcast_to(canary_segment.astype(canary_grads.dtype)[:, None], (canary_segment.shape[0], LANES))
    x_own = canary_acts[:, :CUT]
    y_own = jnp.concatenate([canary_grads, canary_acts[:, CUT:], tag], axis=1)

    x_first = lax.ppermute(x_own, "tok", SIDES)
    x_middle = lax.ppermute(x_own, "tok", MIDDLE)
    y_first = lax.ppermute(y_own, "tok", SIDES)
    y_middle = lax.ppermute(y_own, "tok", MIDDLE)

    x_first, x_middle = after2(x_first, x_middle, ())
    x_middle2 = lax.ppermute(x_first, "tok", MIDDLE)
    x_outer = lax.ppermute(x_middle, "tok", OUTWARD)
    y_first, y_middle = after2(y_first, y_middle, (x_first, x_middle))
    y_middle2 = lax.ppermute(y_first, "tok", MIDDLE)
    y_outer = lax.ppermute(y_middle, "tok", OUTWARD)

    x_middle2, x_outer = after2(x_middle2, x_outer, (y_first, y_middle))
    part = x_middle2[:, :SPLIT]
    x_far = lax.ppermute(part, "tok", OUTWARD)
    part = after(x_middle2, part)[:, SPLIT:]
    x_far2 = lax.ppermute(part, "tok", OUTWARD)
    y_middle2, y_outer = after2(y_middle2, y_outer, (part, self_terms))
    part = after(y_middle2, y_outer)[:, :D]
    g_far = lax.ppermute(part, "tok", OUTWARD)
    part = after(y_middle2, part)[:, D:]
    y_far = lax.ppermute(part, "tok", OUTWARD)

    near = (x_own, x_first, x_middle, x_middle2, x_outer)
    first = SPLIT // BLOCK
    x_gram = cross_gram(None, train_acts, 0, near + (x_far,), 0, first)
    x_far2 = after(x_far2, x_gram)
    x_gram = cross_gram(x_gram, train_acts, SPLIT, near + (x_far2,), first, CUT // BLOCK - first)
    near = (y_own, y_first, y_middle, y_middle2, y_outer)
    g_gram = cross_gram(None, train_grads, 0, near + (after(g_far, x_gram),), 0, D // BLOCK)
    rest = near + (after(y_far, g_gram),)
    return score_shares(x_gram, g_gram, owner_rows, self_terms, train_acts, CUT, rest, D // BLOCK, rest)


def finish(shares, canary_total):
    can = lax.axis_size("can")
    width = CSEQ // can
    total = shares[0][:SEQ_DEV]
    for k in range(1, can):
        total = total + lax.ppermute(shares[k], "can", [(i, (i + k) % can) for i in range(can)])[:SEQ_DEV]
    scale = math.sqrt(FF * D * (canary_total / CSEQ))
    return total[:, :width] / (scale * jnp.sqrt(total[:, width : 2 * width] / (FF * D) + 1.0))


def local(train_acts, train_grads, train_segment, canary_acts, canary_grads, canary_segment):
    tok, can = lax.axis_size("tok"), lax.axis_size("can")
    rows = train_acts.shape[0]
    canary_total = canary_acts.shape[0] * tok * can
    local_ids = train_segment - lax.axis_index("tok") * SEQ_DEV
    owner_rows = (jnp.arange(8, dtype=jnp.int32)[:, None] == local_ids[None, :]).astype(jnp.float32)

    share = rows // can
    start = lax.axis_index("can") * share
    pair = gram(train_acts, lax.dynamic_slice_in_dim(train_acts, start, share, 0))
    pair = pair * gram(train_grads, lax.dynamic_slice_in_dim(train_grads, start, share, 0))
    left = exact(owner_rows, pair, ((1,), (0,)))
    self_terms = left * lax.dynamic_slice_in_dim(owner_rows, start, share, 1)

    if tok == 4:
        shares = line_scores(
            train_acts, train_grads, owner_rows, self_terms, canary_acts, canary_grads, canary_segment
        )
    else:
        ids = lax.all_gather(canary_segment, "tok", axis=0, tiled=True)
        pair = gram(train_acts, lax.all_gather(canary_acts, "tok", axis=0, tiled=True))
        pair = pair * gram(train_grads, lax.all_gather(canary_grads, "tok", axis=0, tiled=True))
        member = (ids[:, None] == jnp.arange(CSEQ, dtype=jnp.int32)[None, :]).astype(jnp.float32)
        scores = exact(exact(owner_rows, pair, ((1,), (0,))), member, ((1,), (0,)))
        own = jnp.broadcast_to(jnp.sum(self_terms, axis=1)[:, None], (owner_rows.shape[0], CSEQ // can))
        columns = [
            lax.dynamic_slice_in_dim(scores, lax.rem(lax.axis_index("can") + k, can) * (CSEQ // can), CSEQ // can, 1)
            for k in range(can)
        ]
        shares = [jnp.concatenate([c, own], axis=1) for c in columns]
    return finish(shares, canary_total)


def solution(mesh):
    placed = (
        P(("job", "tok"), None),
        P(("job", "tok"), None),
        P(("job", "tok")),
        P(("job", "tok", "can"), None),
        P(("job", "tok", "can"), None),
        P(("job", "tok", "can")),
    )
    return jax.shard_map(
        local, mesh=mesh, in_specs=placed, out_specs=P(("job", "tok"), "can"), check_vma=False
    )
```

time: 94.4 us -> 93.9 us (level)
  waiting for transfers between devices: 27.3 us -> 30.8 us
  local copies, waits for them, and re-layouts: 6.72 us -> 4.49 us
  matrix products: 17.8 us -> 16.2 us
    ppermute x1, waiting for transfers between devices: 0.89 us -> 9.91 us  [line_scores(): x_outer = lax.ppermute(x_middle, 'tok', OUTWARD)]
    ppermute x1, waiting for transfers between devices: 8.55 us -> 0.01 us  [line_scores(): y_first = lax.ppermute(y_own, 'tok', SIDES)]
    ppermute x7, waiting for transfers between devices: 4.81 us -> 8.64 us  [the longest x1 4.39 us: line_scores(): x_far = lax.ppermute(part, 'tok', OUTWARD)]
    unnamed x26 -> x20, local copies, waits for them, and re-layouts: 3.75 us -> 0.04 us
    slice x4, local copies, waits for them, and re-layouts: 0.8 us -> 2.28 us  [the longest x1 0.77 us: line_scores(): part = after(y_middle2, y_outer)[:, :D]]
    dot_general x1, matrix products: 1.79 us -> 0.85 us  [exact(): lax.dot_general(left, right, (dims, ((), ())), precision=lax.Precision.HI...]
where the time goes in v3:
time: 93.9 us; the launch traced here: 93.4 us
  waiting for transfers between devices  30.8 us (33%)
  starting transfers between devices  19.8 us (21%)
  Pallas kernels  18.8 us (20%)
  matrix products  16.2 us (17%)
  local copies, waits for them, and re-layouts  4.49 us (5%)
  other arithmetic  3.01 us (3%)
    pallas_call x4, Pallas kernels, call(): pl.pallas_call(kernel, grid=(steps,), in_specs=specs, out_specs=[pl.Block...  18.8 us
    dot_general x2, matrix products, gram(): lax.dot_general(left, right, ROWS, preferred_element_type=jnp.float32)  15.4 us
    ppermute x1, waiting for transfers between devices, line_scores(): x_outer = lax.ppermute(x_middle, 'tok', OUTWARD)  9.91 us
    ppermute x1, waiting for transfers between devices, line_scores(): y_outer = lax.ppermute(y_middle, 'tok', OUTWARD)  9.28 us
    ppermute x1, waiting for transfers between devices, line_scores(): x_far = lax.ppermute(part, 'tok', OUTWARD)  4.39 us
    ppermute x1, starting transfers between devices, line_scores(): y_first = lax.ppermute(y_own, 'tok', SIDES)  3.61 us
    ppermute x1, starting transfers between devices, line_scores(): x_first = lax.ppermute(x_own, 'tok', SIDES)  3.09 us
    ppermute x3, waiting for transfers between devices, finish(): lax.ppermute(shares[k], 'can', [(i, (i + k) % can) for i in range(can)])  3.08 us
  transfers between devices with their start and end apart: 15, of which 7 were waited for; matrix products, arithmetic and copies ran while one was open for 23% of the time, Pallas kernels for 15%

profile of v3, /device:TPU:0, one launch (start us, length us, event | category | flops | bytes accessed | tf_op | source)
XLA Modules:
  0.0 93.4 jit_solution(166483734216531196)
XLA Ops:
  0.0 1.1 %slice.36.refs_1_.refs_2_ = bf16[32,10240]{1,0:T(8,128)(2,1)S(1)} slice(bf16[32,14336]{1,0:T(8,128)(2,1)} %param.9), slice={[0:32], [0:10240]} | slice | bytes 1310720 | tf_op jit(solution)/shard_map/slice | solution.py:146
  1.1 0.0 copy-start.3
  1.1 3.1 %collective-permute-start = (bf16[32,10240]{1,0:T(8,128)(2,1)S(1)}, bf16[32,10240]{1,0:T(8,128)(2,1)S(1)}, u32[]{:S(2)}, u32[]{:S(2)}) collective-permute-start(bf16[32,10240]{1,0:T(8,128)(2,1)S(1)} %slice.36.refs_1_.refs_2_), channel_id=1, source_target_pairs={{0,4},{4,0},{8,12},{12,8},{1,5},{5,1},{9,13},{13,9},{2,6},{6,2},{1... | collective-permute-start | bytes 1966088 | tf_op jit(solution)/shard_map/ppermute | solution.py:149
  4.2 1.5 %collective-permute-start.1 = (bf16[32,10240]{1,0:T(8,128)(2,1)S(1)}, bf16[32,10240]{1,0:T(8,128)(2,1)}, u32[]{:S(2)}, u32[]{:S(2)}) collective-permute-start(bf16[32,10240]{1,0:T(8,128)(2,1)S(1)} %slice.36.refs_1_.refs_2_), channel_id=1, source_target_pairs={{4,8},{8,4},{5,9},{9,5},{6,10},{10,6},{7,11},{11,7},{20,24},{24,20... | collective-permute-start | bytes 1966088 | tf_op jit(solution)/shard_map/ppermute | solution.py:150
  5.8 1.0 %slice.37 = bf16[32,4096]{1,0:T(8,128)(2,1)S(1)} slice(bf16[32,14336]{1,0:T(8,128)(2,1)} %param.9), slice={[0:32], [10240:14336]} | slice | bytes 524288 | tf_op jit(solution)/shard_map/slice | solution.py:147
  6.7 0.7 convert_element_type.6
  7.4 0.1 broadcast_in_dim.2
  7.5 1.0 %pad_maximum_fusion.refs_1_.refs_7_ = bf16[32,8320]{1,0:T(8,128)(2,1)S(1)} fusion(bf16[32,128]{1,0:T(8,128)(2,1)S(1)} %broadcast_in_dim.2, bf16[32,4096]{1,0:T(8,128)(2,1)S(1)} %slice.37, bf16[32,4096]{1,0:T(8,128)(2,1)} %param.10), kind=kLoop, calls=%fused_computation.6 | loop fusion | flops 1597440 | bytes 1064960 | tf_op jit(solution)/shard_map/concatenate | solution.py:147
  8.4 0.0 copy-start
  8.5 3.6 %collective-permute-start.4 = (bf16[32,8320]{1,0:T(8,128)(2,1)S(1)}, bf16[32,8320]{1,0:T(8,128)(2,1)S(1)}, u32[]{:S(2)}, u32[]{:S(2)}) collective-permute-start(bf16[32,8320]{1,0:T(8,128)(2,1)S(1)} %pad_maximum_fusion.refs_1_.refs_7_), channel_id=1, source_target_pairs={{0,4},{4,0},{8,12},{12,8},{1,5},{5,1},{9,13},{13,9},{2,6},{6,2},{1... | collective-permute-start | bytes 1597448 | tf_op jit(solution)/shard_map/ppermute | solution.py:151
  12.1 0.7 collective-permute-start.5
  12.8 4.0 %fusion.5 = f32[128,512]{1,0:T(8,128)S(1)} fusion(bf16[512,4096]{1,0:T(8,128)(2,1)} %refs_0_.4, s32[]{:T(128)S(6)} %select_n.2), kind=kOutput, calls=%fused_computation.4 | convolution fusion | flops 536870912 | bytes 5505028 | tf_op jit(solution)/shard_map/dot_general | solution.py:22
  16.8 0.0 copy-start.9
  16.8 3.0 %collective-permute-done.refs_2_.refs_3_ = bf16[32,10240]{1,0:T(8,128)(2,1)S(1)} collective-permute-done((bf16[32,10240]{1,0:T(8,128)(2,1)S(1)}, bf16[32,10240]{1,0:T(8,128)(2,1)S(1)}, u32[]{:S(2)}, u32[]{:S(2)}) %collective-permute-start) | collective-permute-done | bytes 655392 | tf_op jit(solution)/shard_map/ppermute | solution.py:149
  19.8 0.0 copy-done.3
  19.8 0.0 collective-permute-done.1.refs_3_.refs_4_
  19.8 0.7 collective-permute-start.2
  20.5 1.3 %collective-permute-start.3 = (bf16[32,10240]{1,0:T(8,128)(2,1)}, bf16[32,10240]{1,0:T(8,128)(2,1)}, u32[]{:S(2)}, u32[]{:S(2)}) collective-permute-start(bf16[32,10240]{1,0:T(8,128)(2,1)} %collective-permute-done.1.refs_3_.refs_4_), channel_id=1, source_target_pairs={{4,0},{8,12},{5,1},{9,13},{6,2},{10,14},{7,3},{11,15},{20,16},{24,... | collective-permute-start | bytes 1966088 | tf_op jit(solution)/shard_map/ppermute | solution.py:156
  21.8 11.3 %fusion.2 = f32[128,512]{1,0:T(8,128)S(1)} fusion(f32[128,512]{1,0:T(8,128)S(1)} %fusion.5, bf16[512,14336]{1,0:T(8,128)(2,1)} %refs_0_.5, s32[]{:T(128)S(6)} %select_n.2), kind=kOutput, calls=%fused_computation.2 | convolution fusion | flops 1879113728 | bytes 18874372 | tf_op jit(solution)/shard_map/dot_general | solution.py:22
  33.1 0.0 copy-done
  33.1 0.0 copy-done.7
  33.2 0.0 collective-permute-done.4.refs_2_.refs_8_
  33.2 0.0 copy-start.4
  33.2 0.0 collective-permute-done.5.refs_3_.refs_9_
  33.2 0.0 copy-start.5
  33.2 0.7 collective-permute-start.8
  33.9 1.3 %collective-permute-start.9 = (bf16[32,8320]{1,0:T(8,128)(2,1)S(1)}, bf16[32,8320]{1,0:T(8,128)(2,1)S(1)}, u32[]{:S(2)}, u32[]{:S(2)}) collective-permute-start(bf16[32,8320]{1,0:T(8,128)(2,1)S(1)} %collective-permute-done.5.refs_3_.refs_9_), channel_id=1, source_target_pairs={{4,0},{8,12},{5,1},{9,13},{6,2},{10,14},{7,3},{11,15},{20,16},{24,... | collective-permute-start | bytes 1597448 | tf_op jit(solution)/shard_map/ppermute | solution.py:159
  35.2 0.0 copy-done.9
  35.2 0.0 collective-permute-done.2.refs_4_.refs_5_
  35.2 0.0 copy-start.2
  35.2 9.9 %collective-permute-done.3.refs_5_.refs_6_ = bf16[32,10240]{1,0:T(8,128)(2,1)} collective-permute-done((bf16[32,10240]{1,0:T(8,128)(2,1)}, bf16[32,10240]{1,0:T(8,128)(2,1)}, u32[]{:S(2)}, u32[]{:S(2)}) %collective-permute-start.3) | collective-permute-done | bytes 655392 | tf_op jit(solution)/shard_map/ppermute | solution.py:156
  45.2 1.3 %collective-permute-start.6 = (bf16[32,6144]{1,0:T(8,128)(2,1)S(1)}, bf16[32,6144]{1,0:T(8,128)(2,1)}, u32[]{:S(2)}, u32[]{:S(2)}) collective-permute-start(bf16[32,6144]{1,0:T(8,128)(2,1)S(1)} %slice.38), channel_id=1, source_target_pairs={{4,0},{8,12},{5,1},{9,13},{6,2},{10,14},{7,3},{11,15},{20,16},{24,... | collective-permute-start | bytes 1179656 | tf_op jit(solution)/shard_map/ppermute | solution.py:163
  46.5 0.0 copy-start.8
  46.5 0.7 slice.39
  47.3 1.3 %collective-permute-start.7 = (bf16[32,4096]{1,0:T(8,128)(2,1)}, bf16[32,4096]{1,0:T(8,128)(2,1)}, u32[]{:S(2)}, u32[]{:S(2)}) collective-permute-start(bf16[32,4096]{1,0:T(8,128)(2,1)} %slice.39), channel_id=1, source_target_pairs={{4,0},{8,12},{5,1},{9,13},{6,2},{10,14},{7,3},{11,15},{20,16},{24,... | collective-permute-start | bytes 786440 | tf_op jit(solution)/shard_map/ppermute | solution.py:165
  48.5 0.8 convolution_multiply_fusion.self_ref
  49.4 0.0 collective-permute-done.8.refs_4_.refs_10_
  49.4 9.3 %collective-permute-done.9.refs_5_.refs_11_ = bf16[32,8320]{1,0:T(8,128)(2,1)S(1)} collective-permute-done((bf16[32,8320]{1,0:T(8,128)(2,1)S(1)}, bf16[32,8320]{1,0:T(8,128)(2,1)S(1)}, u32[]{:S(2)}, u32[]{:S(2)}) %collective-permute-start.9) | collective-permute-done | bytes 532512 | tf_op jit(solution)/shard_map/ppermute | solution.py:159
  58.7 0.8 slice.40
  59.4 1.3 %collective-permute-start.10 = (bf16[32,4096]{1,0:T(8,128)(2,1)}, bf16[32,4096]{1,0:T(8,128)(2,1)}, u32[]{:S(2)}, u32[]{:S(2)}) collective-permute-start(bf16[32,4096]{1,0:T(8,128)(2,1)} %slice.40), channel_id=1, source_target_pairs={{4,0},{8,12},{5,1},{9,13},{6,2},{10,14},{7,3},{11,15},{20,16},{24,... | collective-permute-start | bytes 786440 | tf_op jit(solution)/shard_map/ppermute | solution.py:168
  60.7 0.0 copy-done.1
  60.7 0.7 slice.41
  61.5 0.0 copy-done.2
  61.5 1.3 %collective-permute-start.11 = (bf16[32,4224]{1,0:T(8,128)(2,1)}, bf16[32,4224]{1,0:T(8,128)(2,1)}, u32[]{:S(2)}, u32[]{:S(2)}) collective-permute-start(bf16[32,4224]{1,0:T(8,128)(2,1)} %slice.41), channel_id=1, source_target_pairs={{4,0},{8,12},{5,1},{9,13},{6,2},{10,14},{7,3},{11,15},{20,16},{24,... | collective-permute-start | bytes 811016 | tf_op jit(solution)/shard_map/ppermute | solution.py:170
  62.8 0.0 copy-done.4
  62.8 0.0 copy-done.5
  62.8 0.0 copy-done.8
  62.8 0.0 copy-done.6
  62.8 4.4 %collective-permute-done.6.refs_6_ = bf16[32,6144]{1,0:T(8,128)(2,1)} collective-permute-done((bf16[32,6144]{1,0:T(8,128)(2,1)S(1)}, bf16[32,6144]{1,0:T(8,128)(2,1)}, u32[]{:S(2)}, u32[]{:S(2)}) %collective-permute-start.6) | collective-permute-done | bytes 393248 | tf_op jit(solution)/shard_map/ppermute | solution.py:163
  67.2 5.8 %cross_gram.3.refs_0_ = f32[512,128]{1,0:T(8,128)} custom-call(bf16[512,14336]{1,0:T(8,128)(2,1)} %refs_0_.5, bf16[32,10240]{1,0:T(8,128)(2,1)} %copy-done.3, bf16[32,10240]{1,0:T(8,128)(2,1)} %copy-done.7, bf16[32,10240]{1,0:T(8,128)(2,1)} %collective-permute-done.1.refs_3_.refs_4_, bf16[32,10240]{1,0:T(8,128)(2,1)} %copy-done.2, ...), custom_call_target="tpu_custom_call" | custom-call | flops 805306368 | bytes 6291456 | tf_op jit(solution)/shard_map/cross_gram/pallas_call | solution.py:41
  73.0 0.0 collective-permute-done.7.refs_7_
  73.0 4.3 %cross_gram.4.x_ref = f32[512,128]{1,0:T(8,128)} custom-call(f32[512,128]{1,0:T(8,128)} %cross_gram.3.refs_0_, bf16[512,14336]{1,0:T(8,128)(2,1)} %refs_0_.5, bf16[32,10240]{1,0:T(8,128)(2,1)} %copy-done.3, bf16[32,10240]{1,0:T(8,128)(2,1)} %copy-done.7, bf16[32,10240]{1,0:T(8,128)(2,1)} %collective-permute-done.1.refs_3_.refs_4_, ...), custom_call_target="tpu_custom_call" | custom-call | flops 536870912 | bytes 4194304 | tf_op jit(solution)/shard_map/cross_gram/pallas_call | solution.py:41
  77.3 1.2 %collective-permute-done.10.refs_6_ = bf16[32,4096]{1,0:T(8,128)(2,1)} collective-permute-done((bf16[32,4096]{1,0:T(8,128)(2,1)}, bf16[32,4096]{1,0:T(8,128)(2,1)}, u32[]{:S(2)}, u32[]{:S(2)}) %collective-permute-start.10) | collective-permute-done | bytes 262176 | tf_op jit(solution)/shard_map/ppermute | solution.py:168
  78.4 4.0 %cross_gram.5.g_ref = f32[512,128]{1,0:T(8,128)} custom-call(bf16[512,4096]{1,0:T(8,128)(2,1)} %refs_0_.4, bf16[32,8320]{1,0:T(8,128)(2,1)} %copy-done, bf16[32,8320]{1,0:T(8,128)(2,1)} %copy-done.4, bf16[32,8320]{1,0:T(8,128)(2,1)} %copy-done.5, bf16[32,8320]{1,0:T(8,128)(2,1)} %copy-done.1, bf16[32,8320]{1,0:T(8,128)(2,1)} %copy-done.6, ...), custom_call_target="tpu_custom_call" | custom-call | flops 536870912 | bytes 4194304 | tf_op jit(solution)/shard_map/cross_gram/pallas_call | solution.py:41
  82.5 0.0 collective-permute-done.11.refs_6_.refs_12_
  82.5 4.7 %score_shares.1 = (f32[8,128]{1,0:T(8,128)}, f32[8,128]{1,0:T(8,128)}, f32[8,128]{1,0:T(8,128)}, f32[8,128]{1,0:T(8,128)}) custom-call(f32[512,128]{1,0:T(8,128)} %cross_gram.4.x_ref, f32[512,128]{1,0:T(8,128)} %cross_gram.5.g_ref, f32[8,512]{1,0:T(8,128)} %copy-done.8, f32[8,128]{1,0:T(8,128)} %convolution_multiply_fusion.self_ref, ...), custom_call_target="tpu_custom_call" | custom-call | flops 536870912 | bytes 4194304 | tf_op jit(solution)/shard_map/score_shares/pallas_call | solution.py:41
  87.2 0.1 collective-permute-start.14
  87.3 1.6 %collective-permute-start.13 = (f32[8,128]{1,0:T(8,128)}, f32[8,128]{1,0:T(8,128)S(1)}, u32[]{:S(2)}, u32[]{:S(2)}) collective-permute-start(f32[8,128]{1,0:T(8,128)} %get-tuple-element.39), channel_id=1, source_target_pairs={{0,2},{1,3},{2,0},{3,1},{4,6},{5,7},{6,4},{7,5},{8,10},{9,11},{10,... | collective-permute-start | bytes 12296 | tf_op jit(solution)/shard_map/ppermute | solution.py:188
  88.8 0.2 collective-permute-start.12
  89.0 0.0 collective-permute-done.14
  89.0 2.2 %collective-permute-done.13 = f32[8,128]{1,0:T(8,128)S(1)} collective-permute-done((f32[8,128]{1,0:T(8,128)}, f32[8,128]{1,0:T(8,128)S(1)}, u32[]{:S(2)}, u32[]{:S(2)}) %collective-permute-start.13) | collective-permute-done | bytes 4128 | tf_op jit(solution)/shard_map/ppermute | solution.py:188
  91.2 0.9 collective-permute-done.12
  92.1 0.7 slice_add_fusion
  92.8 0.7 multiply_divide_fusion
  (6 shorter events, 0.0 us)
Async XLA Ops:
  1.1 18.7 %copy-start.3 = (bf16[32,10240]{1,0:T(8,128)(2,1)}, bf16[32,10240]{1,0:T(8,128)(2,1)S(1)}, u32[]{:S(2)}) copy-start(bf16[32,10240]{1,0:T(8,128)(2,1)S(1)} %slice.36.refs_1_.refs_2_) | copy-start | bytes 1966084
  1.1 18.6 %collective-permute-start = (bf16[32,10240]{1,0:T(8,128)(2,1)S(1)}, bf16[32,10240]{1,0:T(8,128)(2,1)S(1)}, u32[]{:S(2)}, u32[]{:S(2)}) collective-permute-start(bf16[32,10240]{1,0:T(8,128)(2,1)S(1)} %slice.36.refs_1_.refs_2_), channel_id=1, source_target_pairs={{0,4},{4,0},{8,12},{12,8},{1,5},{5,1},{9,13},{13,9},{2,6},{6,2},{1... | collective-permute-start | bytes 1966088 | tf_op jit(solution)/shard_map/ppermute | solution.py:149
  4.2 15.6 %collective-permute-start.1 = (bf16[32,10240]{1,0:T(8,128)(2,1)S(1)}, bf16[32,10240]{1,0:T(8,128)(2,1)}, u32[]{:S(2)}, u32[]{:S(2)}) collective-permute-start(bf16[32,10240]{1,0:T(8,128)(2,1)S(1)} %slice.36.refs_1_.refs_2_), channel_id=1, source_target_pairs={{4,8},{8,4},{5,9},{9,5},{6,10},{10,6},{7,11},{11,7},{20,24},{24,20... | collective-permute-start | bytes 1966088 | tf_op jit(solution)/shard_map/ppermute | solution.py:150
  8.4 24.7 %copy-start = (bf16[32,8320]{1,0:T(8,128)(2,1)}, bf16[32,8320]{1,0:T(8,128)(2,1)S(1)}, u32[]{:S(2)}) copy-start(bf16[32,8320]{1,0:T(8,128)(2,1)S(1)} %pad_maximum_fusion.refs_1_.refs_7_) | copy-start | bytes 1597444
  8.5 24.7 %collective-permute-start.4 = (bf16[32,8320]{1,0:T(8,128)(2,1)S(1)}, bf16[32,8320]{1,0:T(8,128)(2,1)S(1)}, u32[]{:S(2)}, u32[]{:S(2)}) collective-permute-start(bf16[32,8320]{1,0:T(8,128)(2,1)S(1)} %pad_maximum_fusion.refs_1_.refs_7_), channel_id=1, source_target_pairs={{0,4},{4,0},{8,12},{12,8},{1,5},{5,1},{9,13},{13,9},{2,6},{6,2},{1... | collective-permute-start | bytes 1597448 | tf_op jit(solution)/shard_map/ppermute | solution.py:151
  12.1 21.1 %collective-permute-start.5 = (bf16[32,8320]{1,0:T(8,128)(2,1)S(1)}, bf16[32,8320]{1,0:T(8,128)(2,1)S(1)}, u32[]{:S(2)}, u32[]{:S(2)}) collective-permute-start(bf16[32,8320]{1,0:T(8,128)(2,1)S(1)} %pad_maximum_fusion.refs_1_.refs_7_), channel_id=1, source_target_pairs={{4,8},{8,4},{5,9},{9,5},{6,10},{10,6},{7,11},{11,7},{20,24},{24,20... | collective-permute-start | bytes 1597448 | tf_op jit(solution)/shard_map/ppermute | solution.py:152
  16.8 18.4 %copy-start.9 = (s32[512]{0:T(512)S(1)}, s32[512]{0:T(512)}, u32[]{:S(2)}) copy-start(s32[512]{0:T(512)} %param.8) | copy-start | bytes 6148
  19.8 13.3 %copy-start.7 = (bf16[32,10240]{1,0:T(8,128)(2,1)}, bf16[32,10240]{1,0:T(8,128)(2,1)S(1)}, u32[]{:S(2)}) copy-start(bf16[32,10240]{1,0:T(8,128)(2,1)S(1)} %collective-permute-done.refs_2_.refs_3_) | copy-start | bytes 1966084
  19.8 15.4 %collective-permute-start.2 = (bf16[32,10240]{1,0:T(8,128)(2,1)S(1)}, bf16[32,10240]{1,0:T(8,128)(2,1)S(1)}, u32[]{:S(2)}, u32[]{:S(2)}) collective-permute-start(bf16[32,10240]{1,0:T(8,128)(2,1)S(1)} %collective-permute-done.refs_2_.refs_3_), channel_id=1, source_target_pairs={{4,8},{8,4},{5,9},{9,5},{6,10},{10,6},{7,11},{11,7},{20,24},{24,20... | collective-permute-start | bytes 1966088 | tf_op jit(solution)/shard_map/ppermute | solution.py:155
  20.5 24.6 %collective-permute-start.3 = (bf16[32,10240]{1,0:T(8,128)(2,1)}, bf16[32,10240]{1,0:T(8,128)(2,1)}, u32[]{:S(2)}, u32[]{:S(2)}) collective-permute-start(bf16[32,10240]{1,0:T(8,128)(2,1)} %collective-permute-done.1.refs_3_.refs_4_), channel_id=1, source_target_pairs={{4,0},{8,12},{5,1},{9,13},{6,2},{10,14},{7,3},{11,15},{20,16},{24,... | collective-permute-start | bytes 1966088 | tf_op jit(solution)/shard_map/ppermute | solution.py:156
  33.2 29.6 %copy-start.4 = (bf16[32,8320]{1,0:T(8,128)(2,1)}, bf16[32,8320]{1,0:T(8,128)(2,1)S(1)}, u32[]{:S(2)}) copy-start(bf16[32,8320]{1,0:T(8,128)(2,1)S(1)} %collective-permute-done.4.refs_2_.refs_8_) | copy-start | bytes 1597444
  33.2 29.6 %copy-start.5 = (bf16[32,8320]{1,0:T(8,128)(2,1)}, bf16[32,8320]{1,0:T(8,128)(2,1)S(1)}, u32[]{:S(2)}) copy-start(bf16[32,8320]{1,0:T(8,128)(2,1)S(1)} %collective-permute-done.5.refs_3_.refs_9_) | copy-start | bytes 1597444
  33.2 16.2 %collective-permute-start.8 = (bf16[32,8320]{1,0:T(8,128)(2,1)S(1)}, bf16[32,8320]{1,0:T(8,128)(2,1)S(1)}, u32[]{:S(2)}, u32[]{:S(2)}) collective-permute-start(bf16[32,8320]{1,0:T(8,128)(2,1)S(1)} %collective-permute-done.4.refs_2_.refs_8_), channel_id=1, source_target_pairs={{4,8},{8,4},{5,9},{9,5},{6,10},{10,6},{7,11},{11,7},{20,24},{24,20... | collective-permute-start | bytes 1597448 | tf_op jit(solution)/shard_map/ppermute | solution.py:158
  33.9 24.8 %collective-permute-start.9 = (bf16[32,8320]{1,0:T(8,128)(2,1)S(1)}, bf16[32,8320]{1,0:T(8,128)(2,1)S(1)}, u32[]{:S(2)}, u32[]{:S(2)}) collective-permute-start(bf16[32,8320]{1,0:T(8,128)(2,1)S(1)} %collective-permute-done.5.refs_3_.refs_9_), channel_id=1, source_target_pairs={{4,0},{8,12},{5,1},{9,13},{6,2},{10,14},{7,3},{11,15},{20,16},{24,... | collective-permute-start | bytes 1597448 | tf_op jit(solution)/shard_map/ppermute | solution.py:159
  35.2 26.2 %copy-start.2 = (bf16[32,10240]{1,0:T(8,128)(2,1)}, bf16[32,10240]{1,0:T(8,128)(2,1)S(1)}, u32[]{:S(2)}) copy-start(bf16[32,10240]{1,0:T(8,128)(2,1)S(1)} %collective-permute-done.2.refs_4_.refs_5_) | copy-start | bytes 1966084
  45.2 22.0 %collective-permute-start.6 = (bf16[32,6144]{1,0:T(8,128)(2,1)S(1)}, bf16[32,6144]{1,0:T(8,128)(2,1)}, u32[]{:S(2)}, u32[]{:S(2)}) collective-permute-start(bf16[32,6144]{1,0:T(8,128)(2,1)S(1)} %slice.38), channel_id=1, source_target_pairs={{4,0},{8,12},{5,1},{9,13},{6,2},{10,14},{7,3},{11,15},{20,16},{24,... | collective-permute-start | bytes 1179656 | tf_op jit(solution)/shard_map/ppermute | solution.py:163
  46.5 16.3 %copy-start.8 = (f32[8,512]{1,0:T(8,128)}, f32[8,512]{1,0:T(8,128)S(1)}, u32[]{:S(2)}) copy-start(f32[8,512]{1,0:T(8,128)S(1)} %fusion.7.owner_ref) | copy-start | bytes 49156
  47.3 25.8 %collective-permute-start.7 = (bf16[32,4096]{1,0:T(8,128)(2,1)}, bf16[32,4096]{1,0:T(8,128)(2,1)}, u32[]{:S(2)}, u32[]{:S(2)}) collective-permute-start(bf16[32,4096]{1,0:T(8,128)(2,1)} %slice.39), channel_id=1, source_target_pairs={{4,0},{8,12},{5,1},{9,13},{6,2},{10,14},{7,3},{11,15},{20,16},{24,... | collective-permute-start | bytes 786440 | tf_op jit(solution)/shard_map/ppermute | solution.py:165
  49.4 11.3 %copy-start.1 = (bf16[32,8320]{1,0:T(8,128)(2,1)}, bf16[32,8320]{1,0:T(8,128)(2,1)S(1)}, u32[]{:S(2)}) copy-start(bf16[32,8320]{1,0:T(8,128)(2,1)S(1)} %collective-permute-done.8.refs_4_.refs_10_) | copy-start | bytes 1597444
  58.7 4.1 %copy-start.6 = (bf16[32,8320]{1,0:T(8,128)(2,1)}, bf16[32,8320]{1,0:T(8,128)(2,1)S(1)}, u32[]{:S(2)}) copy-start(bf16[32,8320]{1,0:T(8,128)(2,1)S(1)} %collective-permute-done.9.refs_5_.refs_11_) | copy-start | bytes 1597444
  59.4 19.0 %collective-permute-start.10 = (bf16[32,4096]{1,0:T(8,128)(2,1)}, bf16[32,4096]{1,0:T(8,128)(2,1)}, u32[]{:S(2)}, u32[]{:S(2)}) collective-permute-start(bf16[32,4096]{1,0:T(8,128)(2,1)} %slice.40), channel_id=1, source_target_pairs={{4,0},{8,12},{5,1},{9,13},{6,2},{10,14},{7,3},{11,15},{20,16},{24,... | collective-permute-start | bytes 786440 | tf_op jit(solution)/shard_map/ppermute | solution.py:168
  61.5 21.0 %collective-permute-start.11 = (bf16[32,4224]{1,0:T(8,128)(2,1)}, bf16[32,4224]{1,0:T(8,128)(2,1)}, u32[]{:S(2)}, u32[]{:S(2)}) collective-permute-start(bf16[32,4224]{1,0:T(8,128)(2,1)} %slice.41), channel_id=1, source_target_pairs={{4,0},{8,12},{5,1},{9,13},{6,2},{10,14},{7,3},{11,15},{20,16},{24,... | collective-permute-start | bytes 811016 | tf_op jit(solution)/shard_map/ppermute | solution.py:170
  87.2 1.8 %collective-permute-start.14 = (f32[8,128]{1,0:T(8,128)}, f32[8,128]{1,0:T(8,128)S(1)}, u32[]{:S(2)}, u32[]{:S(2)}) collective-permute-start(f32[8,128]{1,0:T(8,128)} %get-tuple-element.40), channel_id=1, source_target_pairs={{0,3},{1,0},{2,1},{3,2},{4,7},{5,4},{6,5},{7,6},{8,11},{9,8},{10,9... | collective-permute-start | bytes 12296 | tf_op jit(solution)/shard_map/ppermute | solution.py:188
  87.3 3.9 %collective-permute-start.13 = (f32[8,128]{1,0:T(8,128)}, f32[8,128]{1,0:T(8,128)S(1)}, u32[]{:S(2)}, u32[]{:S(2)}) collective-permute-start(f32[8,128]{1,0:T(8,128)} %get-tuple-element.39), channel_id=1, source_target_pairs={{0,2},{1,3},{2,0},{3,1},{4,6},{5,7},{6,4},{7,5},{8,10},{9,11},{10,... | collective-permute-start | bytes 12296 | tf_op jit(solution)/shard_map/ppermute | solution.py:188
  88.8 3.2 %collective-permute-start.12 = (f32[8,128]{1,0:T(8,128)}, f32[8,128]{1,0:T(8,128)S(1)}, u32[]{:S(2)}, u32[]{:S(2)}) collective-permute-start(f32[8,128]{1,0:T(8,128)} %get-tuple-element.38), channel_id=1, source_target_pairs={{0,1},{1,2},{2,3},{3,0},{4,5},{5,6},{6,7},{7,4},{8,9},{9,10},{10,1... | collective-permute-start | bytes 12296 | tf_op jit(solution)/shard_map/ppermute | solution.py:188

commit v4 on v3

--- a/solution.py
+++ b/solution.py
@@ -136,12 +136,30 @@
     return call(kernel, inputs, specs, count, [(seq, LANES)] * can, scratch, count * BLOCK, "score_shares")
 
 
+def share_gram(train, share, block):
+    def kernel(train_ref, out_ref):
+        start = pl.multiple_of(lax.axis_index("can") * share, share)
+        part = gram(train_ref[...], train_ref[pl.ds(start, share), :])
+
+        @pl.when(pl.program_id(0) == 0)
+        def _():
+            out_ref[...] = part
+
+        @pl.when(pl.program_id(0) > 0)
+        def _():
+            out_ref[...] += part
+
+    rows, depth = train.shape
+    specs = [pl.BlockSpec((rows, block), lambda k: (0, k))]
+    return call(kernel, (train,), specs, depth // block, (rows, share), [], depth, "share_gram")
+
+
 SIDES = [(0, 1), (1, 0), (2, 3), (3, 2)]
 MIDDLE = [(1, 2), (2, 1)]
 OUTWARD = [(1, 0), (2, 3)]
 
 
-def line_scores(train_acts, train_grads, owner_rows, self_terms, canary_acts, canary_grads, canary_segment):
+def line_scores(train_acts, train_grads, owner_rows, self_g, self_terms, canary_acts, canary_grads, canary_segment):
     tag = jnp.broadcast_to(canary_segment.astype(canary_grads.dtype)[:, None], (canary_segment.shape[0], LANES))
     x_own = canary_acts[:, :CUT]
     y_own = jnp.concatenate([canary_grads, canary_acts[:, CUT:], tag], axis=1)
@@ -151,14 +169,15 @@
     y_first = lax.ppermute(y_own, "tok", SIDES)
     y_middle = lax.ppermute(y_own, "tok", MIDDLE)
 
-    x_first, x_middle = after2(x_first, x_middle, ())
+    x_first = after(x_first, self_g)
+    x_middle = after(x_middle, x_first)
     x_middle2 = lax.ppermute(x_first, "tok", MIDDLE)
     x_outer = lax.ppermute(x_middle, "tok", OUTWARD)
     y_first, y_middle = after2(y_first, y_middle, (x_first, x_middle))
     y_middle2 = lax.ppermute(y_first, "tok", MIDDLE)
     y_outer = lax.ppermute(y_middle, "tok", OUTWARD)
 
-    x_middle2, x_outer = after2(x_middle2, x_outer, (y_first, y_middle))
+    x_middle2, x_outer = after2(x_middle2, x_outer, (y_first, y_middle, self_terms))
     part = x_middle2[:, :SPLIT]
     x_far = lax.ppermute(part, "tok", OUTWARD)
     part = after(x_middle2, part)[:, SPLIT:]
@@ -199,14 +218,17 @@
 
     share = rows // can
     start = lax.axis_index("can") * share
-    pair = gram(train_acts, lax.dynamic_slice_in_dim(train_acts, start, share, 0))
-    pair = pair * gram(train_grads, lax.dynamic_slice_in_dim(train_grads, start, share, 0))
+    self_g = gram(train_grads, lax.dynamic_slice_in_dim(train_grads, start, share, 0))
+    if tok == 4:
+        pair = share_gram(train_acts, share, 7 * BLOCK // 4) * self_g
+    else:
+        pair = gram(train_acts, lax.dynamic_slice_in_dim(train_acts, start, share, 0)) * self_g
     left = exact(owner_rows, pair, ((1,), (0,)))
     self_terms = left * lax.dynamic_slice_in_dim(owner_rows, start, share, 1)
 
     if tok == 4:
         shares = line_scores(
-            train_acts, train_grads, owner_rows, self_terms, canary_acts, canary_grads, canary_segment
+            train_acts, train_grads, owner_rows, self_g, self_terms, canary_acts, canary_grads, canary_segment
         )
     else:
         ids = lax.all_gather(canary_segment, "tok", axis=0, tiled=True)

time: 93.9 us -> 93.2 us (level)
  matrix products: 16.2 us -> 6.34 us
  Pallas kernels: 18.8 us -> 27.2 us
  waiting for transfers between devices: 30.8 us -> 24.6 us
  local copies, waits for them, and re-layouts: 4.49 us -> 8.27 us
  starting transfers between devices: 19.8 us -> 22.3 us
    dot_general x2 -> x1, matrix products: 15.4 us -> 4.49 us  [gram(): lax.dot_general(left, right, ROWS, preferred_element_type=jnp.float32)]
    ppermute x1, waiting for transfers between devices: 9.91 us -> 0.98 us  [line_scores(): x_outer = lax.ppermute(x_middle, 'tok', OUTWARD)]
    pallas_call x4 -> x5, Pallas kernels: 18.8 us -> 27.2 us  [call(): pl.pallas_call(kernel, grid=(steps,), in_specs=specs, out_specs=[pl.Block...]
    ppermute x1, waiting for transfers between devices: 0.01 us -> 7.98 us  [line_scores(): y_first = lax.ppermute(y_own, 'tok', SIDES)]
    ppermute x1, waiting for transfers between devices: 9.28 us -> 6.08 us  [line_scores(): y_outer = lax.ppermute(y_middle, 'tok', OUTWARD)]
    ppermute x1, waiting for transfers between devices: 4.39 us -> 2.51 us  [line_scores(): x_far = lax.ppermute(part, 'tok', OUTWARD)]
    ppermute x1, waiting for transfers between devices: 2.97 us -> 1.85 us  [line_scores(): x_first = lax.ppermute(x_own, 'tok', SIDES)]
    dot_general x1, matrix products: 0.85 us -> 1.86 us  [exact(): lax.dot_general(left, right, (dims, ((), ())), precision=lax.Precision.HI...]
  transfers between devices with their start and end apart: 15 -> 15, of which waited for: 7 -> 9; matrix products, arithmetic and copies ran while one was open for 23% -> 17% of each run, Pallas kernels for 15% -> 24%
where the time goes in v4:
time: 93.2 us; the launch traced here: 92.5 us
  Pallas kernels  27.2 us (29%)
  waiting for transfers between devices  24.6 us (26%)
  starting transfers between devices  22.3 us (24%)
  local copies, waits for them, and re-layouts  8.27 us (9%)
  matrix products  6.34 us (7%)
  other arithmetic  3.6 us (4%)
    pallas_call x5, Pallas kernels, call(): pl.pallas_call(kernel, grid=(steps,), in_specs=specs, out_specs=[pl.Block...  27.2 us
    ppermute x1, waiting for transfers between devices, line_scores(): y_first = lax.ppermute(y_own, 'tok', SIDES)  7.98 us
    ppermute x1, waiting for transfers between devices, line_scores(): y_outer = lax.ppermute(y_middle, 'tok', OUTWARD)  6.08 us
    dot_general x1, matrix products, gram(): lax.dot_general(left, right, ROWS, preferred_element_type=jnp.float32)  4.49 us
    ppermute x1, starting transfers between devices, line_scores(): y_first = lax.ppermute(y_own, 'tok', SIDES)  3.63 us
    ppermute x1, starting transfers between devices, line_scores(): x_first = lax.ppermute(x_own, 'tok', SIDES)  3.09 us
    ppermute x3, waiting for transfers between devices, finish(): lax.ppermute(shares[k], 'can', [(i, (i + k) % can) for i in range(can)])  3.08 us
    ppermute x1, waiting for transfers between devices, line_scores(): x_far = lax.ppermute(part, 'tok', OUTWARD)  2.51 us
  transfers between devices with their start and end apart: 15, of which 9 were waited for; matrix products, arithmetic and copies ran while one was open for 17% of the time, Pallas kernels for 24%

profile of v4, /device:TPU:0, one launch (start us, length us, event | category | flops | bytes accessed | tf_op | source)
XLA Modules:
  0.0 92.5 jit_solution(7699719450593781523)
XLA Ops:
  0.0 0.0 copy-start.3
  0.0 1.1 %slice.36.refs_1_.refs_2_ = bf16[32,10240]{1,0:T(8,128)(2,1)S(1)} slice(bf16[32,14336]{1,0:T(8,128)(2,1)} %param.9), slice={[0:32], [0:10240]} | slice | bytes 1310720 | tf_op jit(solution)/shard_map/slice | solution.py:164
  1.1 0.0 copy-start.1
  1.2 3.1 %collective-permute-start = (bf16[32,10240]{1,0:T(8,128)(2,1)S(1)}, bf16[32,10240]{1,0:T(8,128)(2,1)}, u32[]{:S(2)}, u32[]{:S(2)}) collective-permute-start(bf16[32,10240]{1,0:T(8,128)(2,1)S(1)} %slice.36.refs_1_.refs_2_), channel_id=1, source_target_pairs={{0,4},{4,0},{8,12},{12,8},{1,5},{5,1},{9,13},{13,9},{2,6},{6,2},{1... | collective-permute-start | bytes 1966088 | tf_op jit(solution)/shard_map/ppermute | solution.py:167
  4.2 1.5 %collective-permute-start.1 = (bf16[32,10240]{1,0:T(8,128)(2,1)S(1)}, bf16[32,10240]{1,0:T(8,128)(2,1)}, u32[]{:S(2)}, u32[]{:S(2)}) collective-permute-start(bf16[32,10240]{1,0:T(8,128)(2,1)S(1)} %slice.36.refs_1_.refs_2_), channel_id=1, source_target_pairs={{4,8},{8,4},{5,9},{9,5},{6,10},{10,6},{7,11},{11,7},{20,24},{24,20... | collective-permute-start | bytes 1966088 | tf_op jit(solution)/shard_map/ppermute | solution.py:168
  5.7 1.0 %slice.37 = bf16[32,4096]{1,0:T(8,128)(2,1)S(1)} slice(bf16[32,14336]{1,0:T(8,128)(2,1)} %param.9), slice={[0:32], [10240:14336]} | slice | bytes 524288 | tf_op jit(solution)/shard_map/slice | solution.py:165
  6.7 0.7 convert_element_type.6
  7.4 0.1 broadcast_in_dim.2
  7.5 1.0 %pad_maximum_fusion.refs_1_.refs_7_ = bf16[32,8320]{1,0:T(8,128)(2,1)S(1)} fusion(bf16[32,128]{1,0:T(8,128)(2,1)S(1)} %broadcast_in_dim.2, bf16[32,4096]{1,0:T(8,128)(2,1)S(1)} %slice.37, bf16[32,4096]{1,0:T(8,128)(2,1)} %param.10), kind=kLoop, calls=%fused_computation.3 | loop fusion | flops 1597440 | bytes 1064960 | tf_op jit(solution)/shard_map/concatenate | solution.py:165
  8.4 0.0 copy-start
  8.5 3.6 %collective-permute-start.4 = (bf16[32,8320]{1,0:T(8,128)(2,1)S(1)}, bf16[32,8320]{1,0:T(8,128)(2,1)}, u32[]{:S(2)}, u32[]{:S(2)}) collective-permute-start(bf16[32,8320]{1,0:T(8,128)(2,1)S(1)} %pad_maximum_fusion.refs_1_.refs_7_), channel_id=1, source_target_pairs={{0,4},{4,0},{8,12},{12,8},{1,5},{5,1},{9,13},{13,9},{2,6},{6,2},{1... | collective-permute-start | bytes 1597448 | tf_op jit(solution)/shard_map/ppermute | solution.py:169
  12.1 0.0 copy-done
  12.1 1.5 %collective-permute-start.5 = (bf16[32,8320]{1,0:T(8,128)(2,1)S(1)}, bf16[32,8320]{1,0:T(8,128)(2,1)}, u32[]{:S(2)}, u32[]{:S(2)}) collective-permute-start(bf16[32,8320]{1,0:T(8,128)(2,1)S(1)} %pad_maximum_fusion.refs_1_.refs_7_), channel_id=1, source_target_pairs={{4,8},{8,4},{5,9},{9,5},{6,10},{10,6},{7,11},{11,7},{20,24},{24,20... | collective-permute-start | bytes 1597448 | tf_op jit(solution)/shard_map/ppermute | solution.py:170
  13.6 4.5 %convolution_bitcast_fusion = f32[512,128]{1,0:T(8,128)} fusion(bf16[512,4096]{1,0:T(8,128)(2,1)} %refs_0_.4, s32[]{:T(128)S(6)} %select_n.4), kind=kOutput, calls=%fused_computation | convolution fusion | flops 536870912 | bytes 5505028 | tf_op jit(solution)/shard_map/dot_general | solution.py:22
  18.1 1.9 %collective-permute-done.refs_2_.refs_3_ = bf16[32,10240]{1,0:T(8,128)(2,1)} collective-permute-done((bf16[32,10240]{1,0:T(8,128)(2,1)S(1)}, bf16[32,10240]{1,0:T(8,128)(2,1)}, u32[]{:S(2)}, u32[]{:S(2)}) %collective-permute-start) | collective-permute-done | bytes 655392 | tf_op jit(solution)/shard_map/ppermute | solution.py:167
  19.9 1.5 %collective-permute-start.2 = (bf16[32,10240]{1,0:T(8,128)(2,1)}, bf16[32,10240]{1,0:T(8,128)(2,1)}, u32[]{:S(2)}, u32[]{:S(2)}) collective-permute-start(bf16[32,10240]{1,0:T(8,128)(2,1)} %collective-permute-done.refs_2_.refs_3_), channel_id=1, source_target_pairs={{4,8},{8,4},{5,9},{9,5},{6,10},{10,6},{7,11},{11,7},{20,24},{24,20... | collective-permute-start | bytes 1966088 | tf_op jit(solution)/shard_map/ppermute | solution.py:174
  21.4 0.0 collective-permute-done.1.refs_3_.refs_4_
  21.4 1.3 %collective-permute-start.3 = (bf16[32,10240]{1,0:T(8,128)(2,1)}, bf16[32,10240]{1,0:T(8,128)(2,1)}, u32[]{:S(2)}, u32[]{:S(2)}) collective-permute-start(bf16[32,10240]{1,0:T(8,128)(2,1)} %collective-permute-done.1.refs_3_.refs_4_), channel_id=1, source_target_pairs={{4,0},{8,12},{5,1},{9,13},{6,2},{10,14},{7,3},{11,15},{20,16},{24,... | collective-permute-start | bytes 1966088 | tf_op jit(solution)/shard_map/ppermute | solution.py:175
  22.7 0.0 copy-done.3
  22.7 0.0 copy-start.2
  22.7 0.6 fusion.2.owner_ref
  23.3 8.0 %collective-permute-done.4.refs_2_.refs_8_ = bf16[32,8320]{1,0:T(8,128)(2,1)} collective-permute-done((bf16[32,8320]{1,0:T(8,128)(2,1)S(1)}, bf16[32,8320]{1,0:T(8,128)(2,1)}, u32[]{:S(2)}, u32[]{:S(2)}) %collective-permute-start.4) | collective-permute-done | bytes 532512 | tf_op jit(solution)/shard_map/ppermute | solution.py:169
  31.3 0.0 collective-permute-done.5.refs_3_.refs_9_
  31.3 0.0 copy-done.1
  31.3 1.5 %collective-permute-start.8 = (bf16[32,8320]{1,0:T(8,128)(2,1)}, bf16[32,8320]{1,0:T(8,128)(2,1)}, u32[]{:S(2)}, u32[]{:S(2)}) collective-permute-start(bf16[32,8320]{1,0:T(8,128)(2,1)} %collective-permute-done.4.refs_2_.refs_8_), channel_id=1, source_target_pairs={{4,8},{8,4},{5,9},{9,5},{6,10},{10,6},{7,11},{11,7},{20,24},{24,20... | collective-permute-start | bytes 1597448 | tf_op jit(solution)/shard_map/ppermute | solution.py:177
  32.8 0.0 copy-done.2
  32.8 1.3 %collective-permute-start.9 = (bf16[32,8320]{1,0:T(8,128)(2,1)}, bf16[32,8320]{1,0:T(8,128)(2,1)}, u32[]{:S(2)}, u32[]{:S(2)}) collective-permute-start(bf16[32,8320]{1,0:T(8,128)(2,1)} %collective-permute-done.5.refs_3_.refs_9_), channel_id=1, source_target_pairs={{4,0},{8,12},{5,1},{9,13},{6,2},{10,14},{7,3},{11,15},{20,16},{24,... | collective-permute-start | bytes 1597448 | tf_op jit(solution)/shard_map/ppermute | solution.py:178
  34.1 8.4 %share_gram.1 = f32[512,128]{1,0:T(8,128)} custom-call(bf16[512,14336]{1,0:T(8,128)(2,1)} %refs_0_.5), custom_call_target="tpu_custom_call" | custom-call | flops 1879048192 | bytes 14680064 | tf_op jit(solution)/shard_map/share_gram/pallas_call | solution.py:41
  42.5 1.9 %convolution_multiply_fusion.self_ref = f32[8,128]{1,0:T(8,128)} fusion(f32[512,128]{1,0:T(8,128)} %share_gram.1, f32[512,128]{1,0:T(8,128)} %convolution_bitcast_fusion, s32[512]{0:T(512)} %copy-done.2, f32[8,512]{1,0:T(8,128)} %fusion.2.owner_ref, s32[]{:T(128)S(6)} %select_n.4), kind=kOutput, calls=%fused_computation.1 | convolution fusion | flops 6362112 | bytes 534532 | tf_op jit(solution)/shard_map/dot_general | solution.py:26
  44.4 0.0 collective-permute-done.2.refs_4_.refs_5_
  44.4 1.0 %collective-permute-done.3.refs_5_.refs_6_ = bf16[32,10240]{1,0:T(8,128)(2,1)} collective-permute-done((bf16[32,10240]{1,0:T(8,128)(2,1)}, bf16[32,10240]{1,0:T(8,128)(2,1)}, u32[]{:S(2)}, u32[]{:S(2)}) %collective-permute-start.3) | collective-permute-done | bytes 655392 | tf_op jit(solution)/shard_map/ppermute | solution.py:175
  45.4 1.0 %slice.38 = bf16[32,6144]{1,0:T(8,128)(2,1)S(1)} slice(bf16[32,10240]{1,0:T(8,128)(2,1)} %collective-permute-done.2.refs_4_.refs_5_), slice={[0:32], [0:6144]} | slice | bytes 786432 | tf_op jit(solution)/shard_map/slice | solution.py:181
  46.4 1.3 %collective-permute-start.6 = (bf16[32,6144]{1,0:T(8,128)(2,1)S(1)}, bf16[32,6144]{1,0:T(8,128)(2,1)}, u32[]{:S(2)}, u32[]{:S(2)}) collective-permute-start(bf16[32,6144]{1,0:T(8,128)(2,1)S(1)} %slice.38), channel_id=1, source_target_pairs={{4,0},{8,12},{5,1},{9,13},{6,2},{10,14},{7,3},{11,15},{20,16},{24,... | collective-permute-start | bytes 1179656 | tf_op jit(solution)/shard_map/ppermute | solution.py:182
  47.7 1.7 %slice.39 = bf16[32,4096]{1,0:T(8,128)(2,1)} slice(bf16[32,10240]{1,0:T(8,128)(2,1)} %collective-permute-done.2.refs_4_.refs_5_), slice={[0:32], [6144:10240]} | slice | bytes 524288 | tf_op jit(solution)/shard_map/slice | solution.py:183
  49.4 1.3 %collective-permute-start.7 = (bf16[32,4096]{1,0:T(8,128)(2,1)}, bf16[32,4096]{1,0:T(8,128)(2,1)}, u32[]{:S(2)}, u32[]{:S(2)}) collective-permute-start(bf16[32,4096]{1,0:T(8,128)(2,1)} %slice.39), channel_id=1, source_target_pairs={{4,0},{8,12},{5,1},{9,13},{6,2},{10,14},{7,3},{11,15},{20,16},{24,... | collective-permute-start | bytes 786440 | tf_op jit(solution)/shard_map/ppermute | solution.py:184
  50.7 0.0 collective-permute-done.8.refs_4_.refs_10_
  50.7 6.1 %collective-permute-done.9.refs_5_.refs_11_ = bf16[32,8320]{1,0:T(8,128)(2,1)} collective-permute-done((bf16[32,8320]{1,0:T(8,128)(2,1)}, bf16[32,8320]{1,0:T(8,128)(2,1)}, u32[]{:S(2)}, u32[]{:S(2)}) %collective-permute-start.9) | collective-permute-done | bytes 532512 | tf_op jit(solution)/shard_map/ppermute | solution.py:178
  56.8 1.7 %slice.40 = bf16[32,4096]{1,0:T(8,128)(2,1)} slice(bf16[32,8320]{1,0:T(8,128)(2,1)} %collective-permute-done.8.refs_4_.refs_10_), slice={[0:32], [0:4096]} | slice | bytes 524288 | tf_op jit(solution)/shard_map/slice | solution.py:186
  58.4 1.3 %collective-permute-start.10 = (bf16[32,4096]{1,0:T(8,128)(2,1)}, bf16[32,4096]{1,0:T(8,128)(2,1)}, u32[]{:S(2)}, u32[]{:S(2)}) collective-permute-start(bf16[32,4096]{1,0:T(8,128)(2,1)} %slice.40), channel_id=1, source_target_pairs={{4,0},{8,12},{5,1},{9,13},{6,2},{10,14},{7,3},{11,15},{20,16},{24,... | collective-permute-start | bytes 786440 | tf_op jit(solution)/shard_map/ppermute | solution.py:187
  59.7 1.7 %slice.41 = bf16[32,4224]{1,0:T(8,128)(2,1)} slice(bf16[32,8320]{1,0:T(8,128)(2,1)} %collective-permute-done.8.refs_4_.refs_10_), slice={[0:32], [4096:8320]} | slice | bytes 540672 | tf_op jit(solution)/shard_map/slice | solution.py:188
  61.4 1.3 %collective-permute-start.11 = (bf16[32,4224]{1,0:T(8,128)(2,1)}, bf16[32,4224]{1,0:T(8,128)(2,1)}, u32[]{:S(2)}, u32[]{:S(2)}) collective-permute-start(bf16[32,4224]{1,0:T(8,128)(2,1)} %slice.41), channel_id=1, source_target_pairs={{4,0},{8,12},{5,1},{9,13},{6,2},{10,14},{7,3},{11,15},{20,16},{24,... | collective-permute-start | bytes 811016 | tf_op jit(solution)/shard_map/ppermute | solution.py:189
  62.7 2.5 %collective-permute-done.6.refs_6_ = bf16[32,6144]{1,0:T(8,128)(2,1)} collective-permute-done((bf16[32,6144]{1,0:T(8,128)(2,1)S(1)}, bf16[32,6144]{1,0:T(8,128)(2,1)}, u32[]{:S(2)}, u32[]{:S(2)}) %collective-permute-start.6) | collective-permute-done | bytes 393248 | tf_op jit(solution)/shard_map/ppermute | solution.py:182
  65.2 5.8 %cross_gram.3.refs_0_ = f32[512,128]{1,0:T(8,128)} custom-call(bf16[512,14336]{1,0:T(8,128)(2,1)} %refs_0_.5, bf16[32,10240]{1,0:T(8,128)(2,1)} %copy-done.1, bf16[32,10240]{1,0:T(8,128)(2,1)} %collective-permute-done.refs_2_.refs_3_, bf16[32,10240]{1,0:T(8,128)(2,1)} %collective-permute-done.1.refs_3_.refs_4_, ...), custom_call_target="tpu_custom_call" | custom-call | flops 805306368 | bytes 6291456 | tf_op jit(solution)/shard_map/cross_gram/pallas_call | solution.py:41
  71.0 0.0 collective-permute-done.7.refs_7_
  71.0 4.3 %cross_gram.4.x_ref = f32[512,128]{1,0:T(8,128)} custom-call(f32[512,128]{1,0:T(8,128)} %cross_gram.3.refs_0_, bf16[512,14336]{1,0:T(8,128)(2,1)} %refs_0_.5, bf16[32,10240]{1,0:T(8,128)(2,1)} %copy-done.1, bf16[32,10240]{1,0:T(8,128)(2,1)} %collective-permute-done.refs_2_.refs_3_, bf16[32,10240]{1,0:T(8,128)(2,1)} %collective-permute-done.1.refs_3_.refs_4_, ...), custom_call_target="tpu_custom_call" | custom-call | flops 536870912 | bytes 4194304 | tf_op jit(solution)/shard_map/cross_gram/pallas_call | solution.py:41
  75.3 1.2 %collective-permute-done.10.refs_6_ = bf16[32,4096]{1,0:T(8,128)(2,1)} collective-permute-done((bf16[32,4096]{1,0:T(8,128)(2,1)}, bf16[32,4096]{1,0:T(8,128)(2,1)}, u32[]{:S(2)}, u32[]{:S(2)}) %collective-permute-start.10) | collective-permute-done | bytes 262176 | tf_op jit(solution)/shard_map/ppermute | solution.py:187
  76.4 4.0 %cross_gram.5.g_ref = f32[512,128]{1,0:T(8,128)} custom-call(bf16[512,4096]{1,0:T(8,128)(2,1)} %refs_0_.4, bf16[32,8320]{1,0:T(8,128)(2,1)} %copy-done, bf16[32,8320]{1,0:T(8,128)(2,1)} %collective-permute-done.4.refs_2_.refs_8_, bf16[32,8320]{1,0:T(8,128)(2,1)} %collective-permute-done.5.refs_3_.refs_9_, ...), custom_call_target="tpu_custom_call" | custom-call | flops 536870912 | bytes 4194304 | tf_op jit(solution)/shard_map/cross_gram/pallas_call | solution.py:41
  80.5 0.9 %collective-permute-done.11.refs_6_.refs_12_ = bf16[32,4224]{1,0:T(8,128)(2,1)} collective-permute-done((bf16[32,4224]{1,0:T(8,128)(2,1)}, bf16[32,4224]{1,0:T(8,128)(2,1)}, u32[]{:S(2)}, u32[]{:S(2)}) %collective-permute-start.11) | collective-permute-done | bytes 270368 | tf_op jit(solution)/shard_map/ppermute | solution.py:189
  81.4 4.7 %score_shares.1 = (f32[8,128]{1,0:T(8,128)}, f32[8,128]{1,0:T(8,128)}, f32[8,128]{1,0:T(8,128)}, f32[8,128]{1,0:T(8,128)}) custom-call(f32[512,128]{1,0:T(8,128)} %cross_gram.4.x_ref, f32[512,128]{1,0:T(8,128)} %cross_gram.5.g_ref, f32[8,512]{1,0:T(8,128)} %fusion.2.owner_ref, f32[8,128]{1,0:T(8,128)} %convolution_multiply_fusion.self_ref, ...), custom_call_target="tpu_custom_call" | custom-call | flops 536870912 | bytes 4194304 | tf_op jit(solution)/shard_map/score_shares/pallas_call | solution.py:41
  86.1 0.3 collective-permute-start.14
  86.4 1.5 %collective-permute-start.13 = (f32[8,128]{1,0:T(8,128)}, f32[8,128]{1,0:T(8,128)S(1)}, u32[]{:S(2)}, u32[]{:S(2)}) collective-permute-start(f32[8,128]{1,0:T(8,128)} %get-tuple-element.39), channel_id=1, source_target_pairs={{0,2},{1,3},{2,0},{3,1},{4,6},{5,7},{6,4},{7,5},{8,10},{9,11},{10,... | collective-permute-start | bytes 12296 | tf_op jit(solution)/shard_map/ppermute | solution.py:207
  87.9 0.2 collective-permute-start.12
  88.1 0.0 collective-permute-done.14
  88.1 2.1 %collective-permute-done.13 = f32[8,128]{1,0:T(8,128)S(1)} collective-permute-done((f32[8,128]{1,0:T(8,128)}, f32[8,128]{1,0:T(8,128)S(1)}, u32[]{:S(2)}, u32[]{:S(2)}) %collective-permute-start.13) | collective-permute-done | bytes 4128 | tf_op jit(solution)/shard_map/ppermute | solution.py:207
  90.2 0.9 %collective-permute-done.12 = f32[8,128]{1,0:T(8,128)S(1)} collective-permute-done((f32[8,128]{1,0:T(8,128)}, f32[8,128]{1,0:T(8,128)S(1)}, u32[]{:S(2)}, u32[]{:S(2)}) %collective-permute-start.12) | collective-permute-done | bytes 4128 | tf_op jit(solution)/shard_map/ppermute | solution.py:207
  91.2 0.7 slice_add_fusion
  91.8 0.7 multiply_divide_fusion
  (1 shorter events, 0.0 us)
Async XLA Ops:
  0.0 22.7 %copy-start.3 = (s32[512]{0:T(512)S(1)}, s32[512]{0:T(512)}, u32[]{:S(2)}) copy-start(s32[512]{0:T(512)} %param.8) | copy-start | bytes 6148
  1.1 30.2 %copy-start.1 = (bf16[32,10240]{1,0:T(8,128)(2,1)}, bf16[32,10240]{1,0:T(8,128)(2,1)S(1)}, u32[]{:S(2)}) copy-start(bf16[32,10240]{1,0:T(8,128)(2,1)S(1)} %slice.36.refs_1_.refs_2_) | copy-start | bytes 1966084
  1.2 18.8 %collective-permute-start = (bf16[32,10240]{1,0:T(8,128)(2,1)S(1)}, bf16[32,10240]{1,0:T(8,128)(2,1)}, u32[]{:S(2)}, u32[]{:S(2)}) collective-permute-start(bf16[32,10240]{1,0:T(8,128)(2,1)S(1)} %slice.36.refs_1_.refs_2_), channel_id=1, source_target_pairs={{0,4},{4,0},{8,12},{12,8},{1,5},{5,1},{9,13},{13,9},{2,6},{6,2},{1... | collective-permute-start | bytes 1966088 | tf_op jit(solution)/shard_map/ppermute | solution.py:167
  4.2 17.2 %collective-permute-start.1 = (bf16[32,10240]{1,0:T(8,128)(2,1)S(1)}, bf16[32,10240]{1,0:T(8,128)(2,1)}, u32[]{:S(2)}, u32[]{:S(2)}) collective-permute-start(bf16[32,10240]{1,0:T(8,128)(2,1)S(1)} %slice.36.refs_1_.refs_2_), channel_id=1, source_target_pairs={{4,8},{8,4},{5,9},{9,5},{6,10},{10,6},{7,11},{11,7},{20,24},{24,20... | collective-permute-start | bytes 1966088 | tf_op jit(solution)/shard_map/ppermute | solution.py:168
  8.4 3.6 %copy-start = (bf16[32,8320]{1,0:T(8,128)(2,1)}, bf16[32,8320]{1,0:T(8,128)(2,1)S(1)}, u32[]{:S(2)}) copy-start(bf16[32,8320]{1,0:T(8,128)(2,1)S(1)} %pad_maximum_fusion.refs_1_.refs_7_) | copy-start | bytes 1597444
  8.5 22.9 %collective-permute-start.4 = (bf16[32,8320]{1,0:T(8,128)(2,1)S(1)}, bf16[32,8320]{1,0:T(8,128)(2,1)}, u32[]{:S(2)}, u32[]{:S(2)}) collective-permute-start(bf16[32,8320]{1,0:T(8,128)(2,1)S(1)} %pad_maximum_fusion.refs_1_.refs_7_), channel_id=1, source_target_pairs={{0,4},{4,0},{8,12},{12,8},{1,5},{5,1},{9,13},{13,9},{2,6},{6,2},{1... | collective-permute-start | bytes 1597448 | tf_op jit(solution)/shard_map/ppermute | solution.py:169
  12.1 19.2 %collective-permute-start.5 = (bf16[32,8320]{1,0:T(8,128)(2,1)S(1)}, bf16[32,8320]{1,0:T(8,128)(2,1)}, u32[]{:S(2)}, u32[]{:S(2)}) collective-permute-start(bf16[32,8320]{1,0:T(8,128)(2,1)S(1)} %pad_maximum_fusion.refs_1_.refs_7_), channel_id=1, source_target_pairs={{4,8},{8,4},{5,9},{9,5},{6,10},{10,6},{7,11},{11,7},{20,24},{24,20... | collective-permute-start | bytes 1597448 | tf_op jit(solution)/shard_map/ppermute | solution.py:170
  19.9 24.5 %collective-permute-start.2 = (bf16[32,10240]{1,0:T(8,128)(2,1)}, bf16[32,10240]{1,0:T(8,128)(2,1)}, u32[]{:S(2)}, u32[]{:S(2)}) collective-permute-start(bf16[32,10240]{1,0:T(8,128)(2,1)} %collective-permute-done.refs_2_.refs_3_), channel_id=1, source_target_pairs={{4,8},{8,4},{5,9},{9,5},{6,10},{10,6},{7,11},{11,7},{20,24},{24,20... | collective-permute-start | bytes 1966088 | tf_op jit(solution)/shard_map/ppermute | solution.py:174
  21.4 23.9 %collective-permute-start.3 = (bf16[32,10240]{1,0:T(8,128)(2,1)}, bf16[32,10240]{1,0:T(8,128)(2,1)}, u32[]{:S(2)}, u32[]{:S(2)}) collective-permute-start(bf16[32,10240]{1,0:T(8,128)(2,1)} %collective-permute-done.1.refs_3_.refs_4_), channel_id=1, source_target_pairs={{4,0},{8,12},{5,1},{9,13},{6,2},{10,14},{7,3},{11,15},{20,16},{24,... | collective-permute-start | bytes 1966088 | tf_op jit(solution)/shard_map/ppermute | solution.py:175
  22.7 10.1 %copy-start.2 = (s32[512]{0:T(512)}, s32[512]{0:T(512)S(1)}, u32[]{:S(2)}) copy-start(s32[512]{0:T(512)S(1)} %broadcast_subtract_fusion) | copy-start | bytes 6148
  31.3 19.4 %collective-permute-start.8 = (bf16[32,8320]{1,0:T(8,128)(2,1)}, bf16[32,8320]{1,0:T(8,128)(2,1)}, u32[]{:S(2)}, u32[]{:S(2)}) collective-permute-start(bf16[32,8320]{1,0:T(8,128)(2,1)} %collective-permute-done.4.refs_2_.refs_8_), channel_id=1, source_target_pairs={{4,8},{8,4},{5,9},{9,5},{6,10},{10,6},{7,11},{11,7},{20,24},{24,20... | collective-permute-start | bytes 1597448 | tf_op jit(solution)/shard_map/ppermute | solution.py:177
  32.8 24.0 %collective-permute-start.9 = (bf16[32,8320]{1,0:T(8,128)(2,1)}, bf16[32,8320]{1,0:T(8,128)(2,1)}, u32[]{:S(2)}, u32[]{:S(2)}) collective-permute-start(bf16[32,8320]{1,0:T(8,128)(2,1)} %collective-permute-done.5.refs_3_.refs_9_), channel_id=1, source_target_pairs={{4,0},{8,12},{5,1},{9,13},{6,2},{10,14},{7,3},{11,15},{20,16},{24,... | collective-permute-start | bytes 1597448 | tf_op jit(solution)/shard_map/ppermute | solution.py:178
  46.4 18.8 %collective-permute-start.6 = (bf16[32,6144]{1,0:T(8,128)(2,1)S(1)}, bf16[32,6144]{1,0:T(8,128)(2,1)}, u32[]{:S(2)}, u32[]{:S(2)}) collective-permute-start(bf16[32,6144]{1,0:T(8,128)(2,1)S(1)} %slice.38), channel_id=1, source_target_pairs={{4,0},{8,12},{5,1},{9,13},{6,2},{10,14},{7,3},{11,15},{20,16},{24,... | collective-permute-start | bytes 1179656 | tf_op jit(solution)/shard_map/ppermute | solution.py:182
  49.4 21.6 %collective-permute-start.7 = (bf16[32,4096]{1,0:T(8,128)(2,1)}, bf16[32,4096]{1,0:T(8,128)(2,1)}, u32[]{:S(2)}, u32[]{:S(2)}) collective-permute-start(bf16[32,4096]{1,0:T(8,128)(2,1)} %slice.39), channel_id=1, source_target_pairs={{4,0},{8,12},{5,1},{9,13},{6,2},{10,14},{7,3},{11,15},{20,16},{24,... | collective-permute-start | bytes 786440 | tf_op jit(solution)/shard_map/ppermute | solution.py:184
  58.4 18.0 %collective-permute-start.10 = (bf16[32,4096]{1,0:T(8,128)(2,1)}, bf16[32,4096]{1,0:T(8,128)(2,1)}, u32[]{:S(2)}, u32[]{:S(2)}) collective-permute-start(bf16[32,4096]{1,0:T(8,128)(2,1)} %slice.40), channel_id=1, source_target_pairs={{4,0},{8,12},{5,1},{9,13},{6,2},{10,14},{7,3},{11,15},{20,16},{24,... | collective-permute-start | bytes 786440 | tf_op jit(solution)/shard_map/ppermute | solution.py:187
  61.4 20.0 %collective-permute-start.11 = (bf16[32,4224]{1,0:T(8,128)(2,1)}, bf16[32,4224]{1,0:T(8,128)(2,1)}, u32[]{:S(2)}, u32[]{:S(2)}) collective-permute-start(bf16[32,4224]{1,0:T(8,128)(2,1)} %slice.41), channel_id=1, source_target_pairs={{4,0},{8,12},{5,1},{9,13},{6,2},{10,14},{7,3},{11,15},{20,16},{24,... | collective-permute-start | bytes 811016 | tf_op jit(solution)/shard_map/ppermute | solution.py:189
  86.1 1.9 %collective-permute-start.14 = (f32[8,128]{1,0:T(8,128)}, f32[8,128]{1,0:T(8,128)S(1)}, u32[]{:S(2)}, u32[]{:S(2)}) collective-permute-start(f32[8,128]{1,0:T(8,128)} %get-tuple-element.40), channel_id=1, source_target_pairs={{0,3},{1,0},{2,1},{3,2},{4,7},{5,4},{6,5},{7,6},{8,11},{9,8},{10,9... | collective-permute-start | bytes 12296 | tf_op jit(solution)/shard_map/ppermute | solution.py:207
  86.4 3.8 %collective-permute-start.13 = (f32[8,128]{1,0:T(8,128)}, f32[8,128]{1,0:T(8,128)S(1)}, u32[]{:S(2)}, u32[]{:S(2)}) collective-permute-start(f32[8,128]{1,0:T(8,128)} %get-tuple-element.39), channel_id=1, source_target_pairs={{0,2},{1,3},{2,0},{3,1},{4,6},{5,7},{6,4},{7,5},{8,10},{9,11},{10,... | collective-permute-start | bytes 12296 | tf_op jit(solution)/shard_map/ppermute | solution.py:207
  87.9 3.2 %collective-permute-start.12 = (f32[8,128]{1,0:T(8,128)}, f32[8,128]{1,0:T(8,128)S(1)}, u32[]{:S(2)}, u32[]{:S(2)}) collective-permute-start(f32[8,128]{1,0:T(8,128)} %get-tuple-element.38), channel_id=1, source_target_pairs={{0,1},{1,2},{2,3},{3,0},{4,5},{5,6},{6,7},{7,4},{8,9},{9,10},{10,1... | collective-permute-start | bytes 12296 | tf_op jit(solution)/shard_map/ppermute | solution.py:207

commit v5 on v4

--- a/solution.py
+++ b/solution.py
@@ -202,7 +202,7 @@
 def finish(shares, canary_total):
     can = lax.axis_size("can")
     width = CSEQ // can
-    total = shares[0][:SEQ_DEV]
+    total = lax.optimization_barrier(shares[0][:SEQ_DEV])
     for k in range(1, can):
         total = total + lax.ppermute(shares[k], "can", [(i, (i + k) % can) for i in range(can)])[:SEQ_DEV]
     scale = math.sqrt(FF * D * (canary_total / CSEQ))

time: 93.2 us -> 92.5 us (level)
  transfers between devices with their start and end apart: 15 -> 15, of which waited for: 9 -> 9; matrix products, arithmetic and copies ran while one was open for 17% -> 18% of each run, Pallas kernels for 24% -> 25%
where the time goes in v5:
time: 92.5 us; the launch traced here: 91.8 us
  Pallas kernels  27.2 us (29%)
  waiting for transfers between devices  23.9 us (26%)
  starting transfers between devices  22.3 us (24%)
  local copies, waits for them, and re-layouts  8.94 us (10%)
  matrix products  6.34 us (7%)
  other arithmetic  2.93 us (3%)
    pallas_call x5, Pallas kernels, call(): pl.pallas_call(kernel, grid=(steps,), in_specs=specs, out_specs=[pl.Block...  27.2 us
    ppermute x1, waiting for transfers between devices, line_scores(): y_first = lax.ppermute(y_own, 'tok', SIDES)  7.98 us
    ppermute x1, waiting for transfers between devices, line_scores(): y_outer = lax.ppermute(y_middle, 'tok', OUTWARD)  6.08 us
    dot_general x1, matrix products, gram(): lax.dot_general(left, right, ROWS, preferred_element_type=jnp.float32)  4.49 us
    ppermute x1, starting transfers between devices, line_scores(): y_first = lax.ppermute(y_own, 'tok', SIDES)  3.63 us
    ppermute x1, starting transfers between devices, line_scores(): x_first = lax.ppermute(x_own, 'tok', SIDES)  3.09 us
    ppermute x1, waiting for transfers between devices, line_scores(): x_far = lax.ppermute(part, 'tok', OUTWARD)  2.51 us
    ppermute x3, waiting for transfers between devices, finish(): lax.ppermute(shares[k], 'can', [(i, (i + k) % can) for i in range(can)])  2.4 us
  transfers between devices with their start and end apart: 15, of which 9 were waited for; matrix products, arithmetic and copies ran while one was open for 18% of the time, Pallas kernels for 25%

profile of v5, /device:TPU:0, one launch (start us, length us, event | category | flops | bytes accessed | tf_op | source)
XLA Modules:
  0.0 91.8 jit_solution(8254766149202996827)
XLA Ops:
  0.0 0.0 copy-start.3
  0.0 1.1 %slice.36.refs_1_.refs_2_ = bf16[32,10240]{1,0:T(8,128)(2,1)S(1)} slice(bf16[32,14336]{1,0:T(8,128)(2,1)} %param.9), slice={[0:32], [0:10240]} | slice | bytes 1310720 | tf_op jit(solution)/shard_map/slice | solution.py:164
  1.1 0.0 copy-start.1
  1.2 3.1 %collective-permute-start = (bf16[32,10240]{1,0:T(8,128)(2,1)S(1)}, bf16[32,10240]{1,0:T(8,128)(2,1)}, u32[]{:S(2)}, u32[]{:S(2)}) collective-permute-start(bf16[32,10240]{1,0:T(8,128)(2,1)S(1)} %slice.36.refs_1_.refs_2_), channel_id=1, source_target_pairs={{0,4},{4,0},{8,12},{12,8},{1,5},{5,1},{9,13},{13,9},{2,6},{6,2},{1... | collective-permute-start | bytes 1966088 | tf_op jit(solution)/shard_map/ppermute | solution.py:167
  4.2 1.5 %collective-permute-start.1 = (bf16[32,10240]{1,0:T(8,128)(2,1)S(1)}, bf16[32,10240]{1,0:T(8,128)(2,1)}, u32[]{:S(2)}, u32[]{:S(2)}) collective-permute-start(bf16[32,10240]{1,0:T(8,128)(2,1)S(1)} %slice.36.refs_1_.refs_2_), channel_id=1, source_target_pairs={{4,8},{8,4},{5,9},{9,5},{6,10},{10,6},{7,11},{11,7},{20,24},{24,20... | collective-permute-start | bytes 1966088 | tf_op jit(solution)/shard_map/ppermute | solution.py:168
  5.7 1.0 %slice.37 = bf16[32,4096]{1,0:T(8,128)(2,1)S(1)} slice(bf16[32,14336]{1,0:T(8,128)(2,1)} %param.9), slice={[0:32], [10240:14336]} | slice | bytes 524288 | tf_op jit(solution)/shard_map/slice | solution.py:165
  6.7 0.7 convert_element_type.6
  7.4 0.1 broadcast_in_dim.2
  7.5 1.0 %pad_maximum_fusion.refs_1_.refs_7_ = bf16[32,8320]{1,0:T(8,128)(2,1)S(1)} fusion(bf16[32,128]{1,0:T(8,128)(2,1)S(1)} %broadcast_in_dim.2, bf16[32,4096]{1,0:T(8,128)(2,1)S(1)} %slice.37, bf16[32,4096]{1,0:T(8,128)(2,1)} %param.10), kind=kLoop, calls=%fused_computation.3 | loop fusion | flops 1597440 | bytes 1064960 | tf_op jit(solution)/shard_map/concatenate | solution.py:165
  8.4 0.0 copy-start
  8.5 3.6 %collective-permute-start.4 = (bf16[32,8320]{1,0:T(8,128)(2,1)S(1)}, bf16[32,8320]{1,0:T(8,128)(2,1)}, u32[]{:S(2)}, u32[]{:S(2)}) collective-permute-start(bf16[32,8320]{1,0:T(8,128)(2,1)S(1)} %pad_maximum_fusion.refs_1_.refs_7_), channel_id=1, source_target_pairs={{0,4},{4,0},{8,12},{12,8},{1,5},{5,1},{9,13},{13,9},{2,6},{6,2},{1... | collective-permute-start | bytes 1597448 | tf_op jit(solution)/shard_map/ppermute | solution.py:169
  12.1 0.0 copy-done
  12.1 1.5 %collective-permute-start.5 = (bf16[32,8320]{1,0:T(8,128)(2,1)S(1)}, bf16[32,8320]{1,0:T(8,128)(2,1)}, u32[]{:S(2)}, u32[]{:S(2)}) collective-permute-start(bf16[32,8320]{1,0:T(8,128)(2,1)S(1)} %pad_maximum_fusion.refs_1_.refs_7_), channel_id=1, source_target_pairs={{4,8},{8,4},{5,9},{9,5},{6,10},{10,6},{7,11},{11,7},{20,24},{24,20... | collective-permute-start | bytes 1597448 | tf_op jit(solution)/shard_map/ppermute | solution.py:170
  13.6 4.5 %convolution_bitcast_fusion = f32[512,128]{1,0:T(8,128)} fusion(bf16[512,4096]{1,0:T(8,128)(2,1)} %refs_0_.4, s32[]{:T(128)S(6)} %select_n.4), kind=kOutput, calls=%fused_computation | convolution fusion | flops 536870912 | bytes 5505028 | tf_op jit(solution)/shard_map/dot_general | solution.py:22
  18.1 1.9 %collective-permute-done.refs_2_.refs_3_ = bf16[32,10240]{1,0:T(8,128)(2,1)} collective-permute-done((bf16[32,10240]{1,0:T(8,128)(2,1)S(1)}, bf16[32,10240]{1,0:T(8,128)(2,1)}, u32[]{:S(2)}, u32[]{:S(2)}) %collective-permute-start) | collective-permute-done | bytes 655392 | tf_op jit(solution)/shard_map/ppermute | solution.py:167
  19.9 1.5 %collective-permute-start.2 = (bf16[32,10240]{1,0:T(8,128)(2,1)}, bf16[32,10240]{1,0:T(8,128)(2,1)}, u32[]{:S(2)}, u32[]{:S(2)}) collective-permute-start(bf16[32,10240]{1,0:T(8,128)(2,1)} %collective-permute-done.refs_2_.refs_3_), channel_id=1, source_target_pairs={{4,8},{8,4},{5,9},{9,5},{6,10},{10,6},{7,11},{11,7},{20,24},{24,20... | collective-permute-start | bytes 1966088 | tf_op jit(solution)/shard_map/ppermute | solution.py:174
  21.4 0.0 collective-permute-done.1.refs_3_.refs_4_
  21.4 1.3 %collective-permute-start.3 = (bf16[32,10240]{1,0:T(8,128)(2,1)}, bf16[32,10240]{1,0:T(8,128)(2,1)}, u32[]{:S(2)}, u32[]{:S(2)}) collective-permute-start(bf16[32,10240]{1,0:T(8,128)(2,1)} %collective-permute-done.1.refs_3_.refs_4_), channel_id=1, source_target_pairs={{4,0},{8,12},{5,1},{9,13},{6,2},{10,14},{7,3},{11,15},{20,16},{24,... | collective-permute-start | bytes 1966088 | tf_op jit(solution)/shard_map/ppermute | solution.py:175
  22.7 0.0 copy-done.3
  22.7 0.0 copy-start.2
  22.7 0.6 fusion.2.owner_ref
  23.3 8.0 %collective-permute-done.4.refs_2_.refs_8_ = bf16[32,8320]{1,0:T(8,128)(2,1)} collective-permute-done((bf16[32,8320]{1,0:T(8,128)(2,1)S(1)}, bf16[32,8320]{1,0:T(8,128)(2,1)}, u32[]{:S(2)}, u32[]{:S(2)}) %collective-permute-start.4) | collective-permute-done | bytes 532512 | tf_op jit(solution)/shard_map/ppermute | solution.py:169
  31.3 0.0 collective-permute-done.5.refs_3_.refs_9_
  31.3 0.0 copy-done.1
  31.3 1.5 %collective-permute-start.8 = (bf16[32,8320]{1,0:T(8,128)(2,1)}, bf16[32,8320]{1,0:T(8,128)(2,1)}, u32[]{:S(2)}, u32[]{:S(2)}) collective-permute-start(bf16[32,8320]{1,0:T(8,128)(2,1)} %collective-permute-done.4.refs_2_.refs_8_), channel_id=1, source_target_pairs={{4,8},{8,4},{5,9},{9,5},{6,10},{10,6},{7,11},{11,7},{20,24},{24,20... | collective-permute-start | bytes 1597448 | tf_op jit(solution)/shard_map/ppermute | solution.py:177
  32.8 0.0 copy-done.2
  32.8 1.3 %collective-permute-start.9 = (bf16[32,8320]{1,0:T(8,128)(2,1)}, bf16[32,8320]{1,0:T(8,128)(2,1)}, u32[]{:S(2)}, u32[]{:S(2)}) collective-permute-start(bf16[32,8320]{1,0:T(8,128)(2,1)} %collective-permute-done.5.refs_3_.refs_9_), channel_id=1, source_target_pairs={{4,0},{8,12},{5,1},{9,13},{6,2},{10,14},{7,3},{11,15},{20,16},{24,... | collective-permute-start | bytes 1597448 | tf_op jit(solution)/shard_map/ppermute | solution.py:178
  34.1 8.4 %share_gram.1 = f32[512,128]{1,0:T(8,128)} custom-call(bf16[512,14336]{1,0:T(8,128)(2,1)} %refs_0_.5), custom_call_target="tpu_custom_call" | custom-call | flops 1879048192 | bytes 14680064 | tf_op jit(solution)/shard_map/share_gram/pallas_call | solution.py:41
  42.5 1.9 %convolution_multiply_fusion.self_ref = f32[8,128]{1,0:T(8,128)} fusion(f32[512,128]{1,0:T(8,128)} %share_gram.1, f32[512,128]{1,0:T(8,128)} %convolution_bitcast_fusion, s32[512]{0:T(512)} %copy-done.2, f32[8,512]{1,0:T(8,128)} %fusion.2.owner_ref, s32[]{:T(128)S(6)} %select_n.4), kind=kOutput, calls=%fused_computation.1 | convolution fusion | flops 6362112 | bytes 534532 | tf_op jit(solution)/shard_map/dot_general | solution.py:26
  44.4 0.0 collective-permute-done.2.refs_4_.refs_5_
  44.4 1.0 %collective-permute-done.3.refs_5_.refs_6_ = bf16[32,10240]{1,0:T(8,128)(2,1)} collective-permute-done((bf16[32,10240]{1,0:T(8,128)(2,1)}, bf16[32,10240]{1,0:T(8,128)(2,1)}, u32[]{:S(2)}, u32[]{:S(2)}) %collective-permute-start.3) | collective-permute-done | bytes 655392 | tf_op jit(solution)/shard_map/ppermute | solution.py:175
  45.4 1.0 %slice.38 = bf16[32,6144]{1,0:T(8,128)(2,1)S(1)} slice(bf16[32,10240]{1,0:T(8,128)(2,1)} %collective-permute-done.2.refs_4_.refs_5_), slice={[0:32], [0:6144]} | slice | bytes 786432 | tf_op jit(solution)/shard_map/slice | solution.py:181
  46.4 1.3 %collective-permute-start.6 = (bf16[32,6144]{1,0:T(8,128)(2,1)S(1)}, bf16[32,6144]{1,0:T(8,128)(2,1)}, u32[]{:S(2)}, u32[]{:S(2)}) collective-permute-start(bf16[32,6144]{1,0:T(8,128)(2,1)S(1)} %slice.38), channel_id=1, source_target_pairs={{4,0},{8,12},{5,1},{9,13},{6,2},{10,14},{7,3},{11,15},{20,16},{24,... | collective-permute-start | bytes 1179656 | tf_op jit(solution)/shard_map/ppermute | solution.py:182
  47.7 1.7 %slice.39 = bf16[32,4096]{1,0:T(8,128)(2,1)} slice(bf16[32,10240]{1,0:T(8,128)(2,1)} %collective-permute-done.2.refs_4_.refs_5_), slice={[0:32], [6144:10240]} | slice | bytes 524288 | tf_op jit(solution)/shard_map/slice | solution.py:183
  49.4 1.3 %collective-permute-start.7 = (bf16[32,4096]{1,0:T(8,128)(2,1)}, bf16[32,4096]{1,0:T(8,128)(2,1)}, u32[]{:S(2)}, u32[]{:S(2)}) collective-permute-start(bf16[32,4096]{1,0:T(8,128)(2,1)} %slice.39), channel_id=1, source_target_pairs={{4,0},{8,12},{5,1},{9,13},{6,2},{10,14},{7,3},{11,15},{20,16},{24,... | collective-permute-start | bytes 786440 | tf_op jit(solution)/shard_map/ppermute | solution.py:184
  50.7 0.0 collective-permute-done.8.refs_4_.refs_10_
  50.7 6.1 %collective-permute-done.9.refs_5_.refs_11_ = bf16[32,8320]{1,0:T(8,128)(2,1)} collective-permute-done((bf16[32,8320]{1,0:T(8,128)(2,1)}, bf16[32,8320]{1,0:T(8,128)(2,1)}, u32[]{:S(2)}, u32[]{:S(2)}) %collective-permute-start.9) | collective-permute-done | bytes 532512 | tf_op jit(solution)/shard_map/ppermute | solution.py:178
  56.8 1.7 %slice.40 = bf16[32,4096]{1,0:T(8,128)(2,1)} slice(bf16[32,8320]{1,0:T(8,128)(2,1)} %collective-permute-done.8.refs_4_.refs_10_), slice={[0:32], [0:4096]} | slice | bytes 524288 | tf_op jit(solution)/shard_map/slice | solution.py:186
  58.4 1.3 %collective-permute-start.10 = (bf16[32,4096]{1,0:T(8,128)(2,1)}, bf16[32,4096]{1,0:T(8,128)(2,1)}, u32[]{:S(2)}, u32[]{:S(2)}) collective-permute-start(bf16[32,4096]{1,0:T(8,128)(2,1)} %slice.40), channel_id=1, source_target_pairs={{4,0},{8,12},{5,1},{9,13},{6,2},{10,14},{7,3},{11,15},{20,16},{24,... | collective-permute-start | bytes 786440 | tf_op jit(solution)/shard_map/ppermute | solution.py:187
  59.7 1.7 %slice.41 = bf16[32,4224]{1,0:T(8,128)(2,1)} slice(bf16[32,8320]{1,0:T(8,128)(2,1)} %collective-permute-done.8.refs_4_.refs_10_), slice={[0:32], [4096:8320]} | slice | bytes 540672 | tf_op jit(solution)/shard_map/slice | solution.py:188
  61.4 1.3 %collective-permute-start.11 = (bf16[32,4224]{1,0:T(8,128)(2,1)}, bf16[32,4224]{1,0:T(8,128)(2,1)}, u32[]{:S(2)}, u32[]{:S(2)}) collective-permute-start(bf16[32,4224]{1,0:T(8,128)(2,1)} %slice.41), channel_id=1, source_target_pairs={{4,0},{8,12},{5,1},{9,13},{6,2},{10,14},{7,3},{11,15},{20,16},{24,... | collective-permute-start | bytes 811016 | tf_op jit(solution)/shard_map/ppermute | solution.py:189
  62.7 2.5 %collective-permute-done.6.refs_6_ = bf16[32,6144]{1,0:T(8,128)(2,1)} collective-permute-done((bf16[32,6144]{1,0:T(8,128)(2,1)S(1)}, bf16[32,6144]{1,0:T(8,128)(2,1)}, u32[]{:S(2)}, u32[]{:S(2)}) %collective-permute-start.6) | collective-permute-done | bytes 393248 | tf_op jit(solution)/shard_map/ppermute | solution.py:182
  65.2 5.8 %cross_gram.3.refs_0_ = f32[512,128]{1,0:T(8,128)} custom-call(bf16[512,14336]{1,0:T(8,128)(2,1)} %refs_0_.5, bf16[32,10240]{1,0:T(8,128)(2,1)} %copy-done.1, bf16[32,10240]{1,0:T(8,128)(2,1)} %collective-permute-done.refs_2_.refs_3_, bf16[32,10240]{1,0:T(8,128)(2,1)} %collective-permute-done.1.refs_3_.refs_4_, ...), custom_call_target="tpu_custom_call" | custom-call | flops 805306368 | bytes 6291456 | tf_op jit(solution)/shard_map/cross_gram/pallas_call | solution.py:41
  71.0 0.0 collective-permute-done.7.refs_7_
  71.0 4.3 %cross_gram.4.x_ref = f32[512,128]{1,0:T(8,128)} custom-call(f32[512,128]{1,0:T(8,128)} %cross_gram.3.refs_0_, bf16[512,14336]{1,0:T(8,128)(2,1)} %refs_0_.5, bf16[32,10240]{1,0:T(8,128)(2,1)} %copy-done.1, bf16[32,10240]{1,0:T(8,128)(2,1)} %collective-permute-done.refs_2_.refs_3_, bf16[32,10240]{1,0:T(8,128)(2,1)} %collective-permute-done.1.refs_3_.refs_4_, ...), custom_call_target="tpu_custom_call" | custom-call | flops 536870912 | bytes 4194304 | tf_op jit(solution)/shard_map/cross_gram/pallas_call | solution.py:41
  75.3 1.2 %collective-permute-done.10.refs_6_ = bf16[32,4096]{1,0:T(8,128)(2,1)} collective-permute-done((bf16[32,4096]{1,0:T(8,128)(2,1)}, bf16[32,4096]{1,0:T(8,128)(2,1)}, u32[]{:S(2)}, u32[]{:S(2)}) %collective-permute-start.10) | collective-permute-done | bytes 262176 | tf_op jit(solution)/shard_map/ppermute | solution.py:187
  76.4 4.0 %cross_gram.5.g_ref = f32[512,128]{1,0:T(8,128)} custom-call(bf16[512,4096]{1,0:T(8,128)(2,1)} %refs_0_.4, bf16[32,8320]{1,0:T(8,128)(2,1)} %copy-done, bf16[32,8320]{1,0:T(8,128)(2,1)} %collective-permute-done.4.refs_2_.refs_8_, bf16[32,8320]{1,0:T(8,128)(2,1)} %collective-permute-done.5.refs_3_.refs_9_, ...), custom_call_target="tpu_custom_call" | custom-call | flops 536870912 | bytes 4194304 | tf_op jit(solution)/shard_map/cross_gram/pallas_call | solution.py:41
  80.5 0.9 %collective-permute-done.11.refs_6_.refs_12_ = bf16[32,4224]{1,0:T(8,128)(2,1)} collective-permute-done((bf16[32,4224]{1,0:T(8,128)(2,1)}, bf16[32,4224]{1,0:T(8,128)(2,1)}, u32[]{:S(2)}, u32[]{:S(2)}) %collective-permute-start.11) | collective-permute-done | bytes 270368 | tf_op jit(solution)/shard_map/ppermute | solution.py:189
  81.4 4.7 %score_shares.1 = (f32[8,128]{1,0:T(8,128)}, f32[8,128]{1,0:T(8,128)}, f32[8,128]{1,0:T(8,128)}, f32[8,128]{1,0:T(8,128)}) custom-call(f32[512,128]{1,0:T(8,128)} %cross_gram.4.x_ref, f32[512,128]{1,0:T(8,128)} %cross_gram.5.g_ref, f32[8,512]{1,0:T(8,128)} %fusion.2.owner_ref, f32[8,128]{1,0:T(8,128)} %convolution_multiply_fusion.self_ref, ...), custom_call_target="tpu_custom_call" | custom-call | flops 536870912 | bytes 4194304 | tf_op jit(solution)/shard_map/score_shares/pallas_call | solution.py:41
  86.1 0.3 collective-permute-start.14
  86.4 1.5 %collective-permute-start.13 = (f32[8,128]{1,0:T(8,128)}, f32[8,128]{1,0:T(8,128)S(1)}, u32[]{:S(2)}, u32[]{:S(2)}) collective-permute-start(f32[8,128]{1,0:T(8,128)} %get-tuple-element.39), channel_id=1, source_target_pairs={{0,2},{1,3},{2,0},{3,1},{4,6},{5,7},{6,4},{7,5},{8,10},{9,11},{10,... | collective-permute-start | bytes 12296 | tf_op jit(solution)/shard_map/ppermute | solution.py:207
  87.9 0.2 collective-permute-start.12
  88.1 0.7 slice.42
  88.8 0.0 collective-permute-done.14
  88.8 1.5 %collective-permute-done.13 = f32[8,128]{1,0:T(8,128)S(1)} collective-permute-done((f32[8,128]{1,0:T(8,128)}, f32[8,128]{1,0:T(8,128)S(1)}, u32[]{:S(2)}, u32[]{:S(2)}) %collective-permute-start.13) | collective-permute-done | bytes 4128 | tf_op jit(solution)/shard_map/ppermute | solution.py:207
  90.2 0.9 %collective-permute-done.12 = f32[8,128]{1,0:T(8,128)S(1)} collective-permute-done((f32[8,128]{1,0:T(8,128)}, f32[8,128]{1,0:T(8,128)S(1)}, u32[]{:S(2)}, u32[]{:S(2)}) %collective-permute-start.12) | collective-permute-done | bytes 4128 | tf_op jit(solution)/shard_map/ppermute | solution.py:207
  91.2 0.7 multiply_divide_fusion
  (2 shorter events, 0.0 us)
Async XLA Ops:
  0.0 22.7 %copy-start.3 = (s32[512]{0:T(512)S(1)}, s32[512]{0:T(512)}, u32[]{:S(2)}) copy-start(s32[512]{0:T(512)} %param.8) | copy-start | bytes 6148
  1.1 30.2 %copy-start.1 = (bf16[32,10240]{1,0:T(8,128)(2,1)}, bf16[32,10240]{1,0:T(8,128)(2,1)S(1)}, u32[]{:S(2)}) copy-start(bf16[32,10240]{1,0:T(8,128)(2,1)S(1)} %slice.36.refs_1_.refs_2_) | copy-start | bytes 1966084
  1.2 18.8 %collective-permute-start = (bf16[32,10240]{1,0:T(8,128)(2,1)S(1)}, bf16[32,10240]{1,0:T(8,128)(2,1)}, u32[]{:S(2)}, u32[]{:S(2)}) collective-permute-start(bf16[32,10240]{1,0:T(8,128)(2,1)S(1)} %slice.36.refs_1_.refs_2_), channel_id=1, source_target_pairs={{0,4},{4,0},{8,12},{12,8},{1,5},{5,1},{9,13},{13,9},{2,6},{6,2},{1... | collective-permute-start | bytes 1966088 | tf_op jit(solution)/shard_map/ppermute | solution.py:167
  4.2 17.2 %collective-permute-start.1 = (bf16[32,10240]{1,0:T(8,128)(2,1)S(1)}, bf16[32,10240]{1,0:T(8,128)(2,1)}, u32[]{:S(2)}, u32[]{:S(2)}) collective-permute-start(bf16[32,10240]{1,0:T(8,128)(2,1)S(1)} %slice.36.refs_1_.refs_2_), channel_id=1, source_target_pairs={{4,8},{8,4},{5,9},{9,5},{6,10},{10,6},{7,11},{11,7},{20,24},{24,20... | collective-permute-start | bytes 1966088 | tf_op jit(solution)/shard_map/ppermute | solution.py:168
  8.4 3.6 %copy-start = (bf16[32,8320]{1,0:T(8,128)(2,1)}, bf16[32,8320]{1,0:T(8,128)(2,1)S(1)}, u32[]{:S(2)}) copy-start(bf16[32,8320]{1,0:T(8,128)(2,1)S(1)} %pad_maximum_fusion.refs_1_.refs_7_) | copy-start | bytes 1597444
  8.5 22.9 %collective-permute-start.4 = (bf16[32,8320]{1,0:T(8,128)(2,1)S(1)}, bf16[32,8320]{1,0:T(8,128)(2,1)}, u32[]{:S(2)}, u32[]{:S(2)}) collective-permute-start(bf16[32,8320]{1,0:T(8,128)(2,1)S(1)} %pad_maximum_fusion.refs_1_.refs_7_), channel_id=1, source_target_pairs={{0,4},{4,0},{8,12},{12,8},{1,5},{5,1},{9,13},{13,9},{2,6},{6,2},{1... | collective-permute-start | bytes 1597448 | tf_op jit(solution)/shard_map/ppermute | solution.py:169
  12.1 19.2 %collective-permute-start.5 = (bf16[32,8320]{1,0:T(8,128)(2,1)S(1)}, bf16[32,8320]{1,0:T(8,128)(2,1)}, u32[]{:S(2)}, u32[]{:S(2)}) collective-permute-start(bf16[32,8320]{1,0:T(8,128)(2,1)S(1)} %pad_maximum_fusion.refs_1_.refs_7_), channel_id=1, source_target_pairs={{4,8},{8,4},{5,9},{9,5},{6,10},{10,6},{7,11},{11,7},{20,24},{24,20... | collective-permute-start | bytes 1597448 | tf_op jit(solution)/shard_map/ppermute | solution.py:170
  19.9 24.5 %collective-permute-start.2 = (bf16[32,10240]{1,0:T(8,128)(2,1)}, bf16[32,10240]{1,0:T(8,128)(2,1)}, u32[]{:S(2)}, u32[]{:S(2)}) collective-permute-start(bf16[32,10240]{1,0:T(8,128)(2,1)} %collective-permute-done.refs_2_.refs_3_), channel_id=1, source_target_pairs={{4,8},{8,4},{5,9},{9,5},{6,10},{10,6},{7,11},{11,7},{20,24},{24,20... | collective-permute-start | bytes 1966088 | tf_op jit(solution)/shard_map/ppermute | solution.py:174
  21.4 23.9 %collective-permute-start.3 = (bf16[32,10240]{1,0:T(8,128)(2,1)}, bf16[32,10240]{1,0:T(8,128)(2,1)}, u32[]{:S(2)}, u32[]{:S(2)}) collective-permute-start(bf16[32,10240]{1,0:T(8,128)(2,1)} %collective-permute-done.1.refs_3_.refs_4_), channel_id=1, source_target_pairs={{4,0},{8,12},{5,1},{9,13},{6,2},{10,14},{7,3},{11,15},{20,16},{24,... | collective-permute-start | bytes 1966088 | tf_op jit(solution)/shard_map/ppermute | solution.py:175
  22.7 10.1 %copy-start.2 = (s32[512]{0:T(512)}, s32[512]{0:T(512)S(1)}, u32[]{:S(2)}) copy-start(s32[512]{0:T(512)S(1)} %broadcast_subtract_fusion) | copy-start | bytes 6148
  31.3 19.4 %collective-permute-start.8 = (bf16[32,8320]{1,0:T(8,128)(2,1)}, bf16[32,8320]{1,0:T(8,128)(2,1)}, u32[]{:S(2)}, u32[]{:S(2)}) collective-permute-start(bf16[32,8320]{1,0:T(8,128)(2,1)} %collective-permute-done.4.refs_2_.refs_8_), channel_id=1, source_target_pairs={{4,8},{8,4},{5,9},{9,5},{6,10},{10,6},{7,11},{11,7},{20,24},{24,20... | collective-permute-start | bytes 1597448 | tf_op jit(solution)/shard_map/ppermute | solution.py:177
  32.8 24.0 %collective-permute-start.9 = (bf16[32,8320]{1,0:T(8,128)(2,1)}, bf16[32,8320]{1,0:T(8,128)(2,1)}, u32[]{:S(2)}, u32[]{:S(2)}) collective-permute-start(bf16[32,8320]{1,0:T(8,128)(2,1)} %collective-permute-done.5.refs_3_.refs_9_), channel_id=1, source_target_pairs={{4,0},{8,12},{5,1},{9,13},{6,2},{10,14},{7,3},{11,15},{20,16},{24,... | collective-permute-start | bytes 1597448 | tf_op jit(solution)/shard_map/ppermute | solution.py:178
  46.4 18.8 %collective-permute-start.6 = (bf16[32,6144]{1,0:T(8,128)(2,1)S(1)}, bf16[32,6144]{1,0:T(8,128)(2,1)}, u32[]{:S(2)}, u32[]{:S(2)}) collective-permute-start(bf16[32,6144]{1,0:T(8,128)(2,1)S(1)} %slice.38), channel_id=1, source_target_pairs={{4,0},{8,12},{5,1},{9,13},{6,2},{10,14},{7,3},{11,15},{20,16},{24,... | collective-permute-start | bytes 1179656 | tf_op jit(solution)/shard_map/ppermute | solution.py:182
  49.4 21.6 %collective-permute-start.7 = (bf16[32,4096]{1,0:T(8,128)(2,1)}, bf16[32,4096]{1,0:T(8,128)(2,1)}, u32[]{:S(2)}, u32[]{:S(2)}) collective-permute-start(bf16[32,4096]{1,0:T(8,128)(2,1)} %slice.39), channel_id=1, source_target_pairs={{4,0},{8,12},{5,1},{9,13},{6,2},{10,14},{7,3},{11,15},{20,16},{24,... | collective-permute-start | bytes 786440 | tf_op jit(solution)/shard_map/ppermute | solution.py:184
  58.4 18.0 %collective-permute-start.10 = (bf16[32,4096]{1,0:T(8,128)(2,1)}, bf16[32,4096]{1,0:T(8,128)(2,1)}, u32[]{:S(2)}, u32[]{:S(2)}) collective-permute-start(bf16[32,4096]{1,0:T(8,128)(2,1)} %slice.40), channel_id=1, source_target_pairs={{4,0},{8,12},{5,1},{9,13},{6,2},{10,14},{7,3},{11,15},{20,16},{24,... | collective-permute-start | bytes 786440 | tf_op jit(solution)/shard_map/ppermute | solution.py:187
  61.4 20.0 %collective-permute-start.11 = (bf16[32,4224]{1,0:T(8,128)(2,1)}, bf16[32,4224]{1,0:T(8,128)(2,1)}, u32[]{:S(2)}, u32[]{:S(2)}) collective-permute-start(bf16[32,4224]{1,0:T(8,128)(2,1)} %slice.41), channel_id=1, source_target_pairs={{4,0},{8,12},{5,1},{9,13},{6,2},{10,14},{7,3},{11,15},{20,16},{24,... | collective-permute-start | bytes 811016 | tf_op jit(solution)/shard_map/ppermute | solution.py:189
  86.1 2.6 %collective-permute-start.14 = (f32[8,128]{1,0:T(8,128)}, f32[8,128]{1,0:T(8,128)S(1)}, u32[]{:S(2)}, u32[]{:S(2)}) collective-permute-start(f32[8,128]{1,0:T(8,128)} %get-tuple-element.40), channel_id=1, source_target_pairs={{0,3},{1,0},{2,1},{3,2},{4,7},{5,4},{6,5},{7,6},{8,11},{9,8},{10,9... | collective-permute-start | bytes 12296 | tf_op jit(solution)/shard_map/ppermute | solution.py:207
  86.4 3.8 %collective-permute-start.13 = (f32[8,128]{1,0:T(8,128)}, f32[8,128]{1,0:T(8,128)S(1)}, u32[]{:S(2)}, u32[]{:S(2)}) collective-permute-start(f32[8,128]{1,0:T(8,128)} %get-tuple-element.39), channel_id=1, source_target_pairs={{0,2},{1,3},{2,0},{3,1},{4,6},{5,7},{6,4},{7,5},{8,10},{9,11},{10,... | collective-permute-start | bytes 12296 | tf_op jit(solution)/shard_map/ppermute | solution.py:207
  87.9 3.2 %collective-permute-start.12 = (f32[8,128]{1,0:T(8,128)}, f32[8,128]{1,0:T(8,128)S(1)}, u32[]{:S(2)}, u32[]{:S(2)}) collective-permute-start(f32[8,128]{1,0:T(8,128)} %get-tuple-element.38), channel_id=1, source_target_pairs={{0,1},{1,2},{2,3},{3,0},{4,5},{5,6},{6,7},{7,4},{8,9},{9,10},{10,1... | collective-permute-start | bytes 12296 | tf_op jit(solution)/shard_map/ppermute | solution.py:207

commit v6 on v5

--- a/solution.py
+++ b/solution.py
@@ -117,7 +117,7 @@
             own = jnp.sum(self_ref[...], axis=1, keepdims=True)
             lane = lax.broadcasted_iota(jnp.int32, scores.shape, 1)
             for k in range(can):
-                to = lax.rem(lax.axis_index("can") + k, can)
+                to = lax.axis_index("can") ^ k
                 shifted = pltpu.roll(scores, lax.rem(LANES - to * width, LANES), 1)
                 refs[13 + k][...] = jnp.where(lane < width, shifted, own)
 
@@ -204,7 +204,7 @@
     width = CSEQ // can
     total = lax.optimization_barrier(shares[0][:SEQ_DEV])
     for k in range(1, can):
-        total = total + lax.ppermute(shares[k], "can", [(i, (i + k) % can) for i in range(can)])[:SEQ_DEV]
+        total = total + lax.ppermute(shares[k], "can", [(i, i ^ k) for i in range(can)])[:SEQ_DEV]
     scale = math.sqrt(FF * D * (canary_total / CSEQ))
     return total[:, :width] / (scale * jnp.sqrt(total[:, width : 2 * width] / (FF * D) + 1.0))
 
@@ -238,7 +238,7 @@
         scores = exact(exact(owner_rows, pair, ((1,), (0,))), member, ((1,), (0,)))
         own = jnp.broadcast_to(jnp.sum(self_terms, axis=1)[:, None], (owner_rows.shape[0], CSEQ // can))
         columns = [
-            lax.dynamic_slice_in_dim(scores, lax.rem(lax.axis_index("can") + k, can) * (CSEQ // can), CSEQ // can, 1)
+            lax.dynamic_slice_in_dim(scores, (lax.axis_index("can") ^ k) * (CSEQ // can), CSEQ // can, 1)
             for k in range(can)
         ]
         shares = [jnp.concatenate([c, own], axis=1) for c in columns]

time: 92.5 us -> 91.6 us (level)
  no operation moved by 1% of the time
where the time goes in v6:
time: 91.6 us; the launch traced here: 90.9 us
  Pallas kernels  27.2 us (30%)
  waiting for transfers between devices  23 us (25%)
  starting transfers between devices  22.3 us (24%)
  local copies, waits for them, and re-layouts  8.94 us (10%)
  matrix products  6.34 us (7%)
  other arithmetic  2.93 us (3%)
    pallas_call x5, Pallas kernels, call(): pl.pallas_call(kernel, grid=(steps,), in_specs=specs, out_specs=[pl.Block...  27.2 us
    ppermute x1, waiting for transfers between devices, line_scores(): y_first = lax.ppermute(y_own, 'tok', SIDES)  7.98 us
    ppermute x1, waiting for transfers between devices, line_scores(): y_outer = lax.ppermute(y_middle, 'tok', OUTWARD)  6.08 us
    dot_general x1, matrix products, gram(): lax.dot_general(left, right, ROWS, preferred_element_type=jnp.float32)  4.49 us
    ppermute x1, starting transfers between devices, line_scores(): y_first = lax.ppermute(y_own, 'tok', SIDES)  3.63 us
    ppermute x1, starting transfers between devices, line_scores(): x_first = lax.ppermute(x_own, 'tok', SIDES)  3.09 us
    ppermute x1, waiting for transfers between devices, line_scores(): x_far = lax.ppermute(part, 'tok', OUTWARD)  2.51 us
    ppermute x3, starting transfers between devices, finish(): lax.ppermute(shares[k], 'can', [(i, i ^ k) for i in range(can)])[:SEQ_DEV]  1.95 us
  transfers between devices with their start and end apart: 15, of which 9 were waited for; matrix products, arithmetic and copies ran while one was open for 18% of the time, Pallas kernels for 25%

profile of v6, /device:TPU:0, one launch (start us, length us, event | category | flops | bytes accessed | tf_op | source)
XLA Modules:
  0.0 90.9 jit_solution(293046448948749641)
XLA Ops:
  0.0 0.0 copy-start.3
  0.0 1.1 %slice.36.refs_1_.refs_2_ = bf16[32,10240]{1,0:T(8,128)(2,1)S(1)} slice(bf16[32,14336]{1,0:T(8,128)(2,1)} %param.9), slice={[0:32], [0:10240]} | slice | bytes 1310720 | tf_op jit(solution)/shard_map/slice | solution.py:164
  1.1 0.0 copy-start.1
  1.2 3.1 %collective-permute-start = (bf16[32,10240]{1,0:T(8,128)(2,1)S(1)}, bf16[32,10240]{1,0:T(8,128)(2,1)}, u32[]{:S(2)}, u32[]{:S(2)}) collective-permute-start(bf16[32,10240]{1,0:T(8,128)(2,1)S(1)} %slice.36.refs_1_.refs_2_), channel_id=1, source_target_pairs={{0,4},{4,0},{8,12},{12,8},{1,5},{5,1},{9,13},{13,9},{2,6},{6,2},{1... | collective-permute-start | bytes 1966088 | tf_op jit(solution)/shard_map/ppermute | solution.py:167
  4.2 1.5 %collective-permute-start.1 = (bf16[32,10240]{1,0:T(8,128)(2,1)S(1)}, bf16[32,10240]{1,0:T(8,128)(2,1)}, u32[]{:S(2)}, u32[]{:S(2)}) collective-permute-start(bf16[32,10240]{1,0:T(8,128)(2,1)S(1)} %slice.36.refs_1_.refs_2_), channel_id=1, source_target_pairs={{4,8},{8,4},{5,9},{9,5},{6,10},{10,6},{7,11},{11,7},{20,24},{24,20... | collective-permute-start | bytes 1966088 | tf_op jit(solution)/shard_map/ppermute | solution.py:168
  5.7 1.0 %slice.37 = bf16[32,4096]{1,0:T(8,128)(2,1)S(1)} slice(bf16[32,14336]{1,0:T(8,128)(2,1)} %param.9), slice={[0:32], [10240:14336]} | slice | bytes 524288 | tf_op jit(solution)/shard_map/slice | solution.py:165
  6.7 0.7 convert_element_type.6
  7.4 0.1 broadcast_in_dim.2
  7.5 1.0 %pad_maximum_fusion.refs_1_.refs_7_ = bf16[32,8320]{1,0:T(8,128)(2,1)S(1)} fusion(bf16[32,128]{1,0:T(8,128)(2,1)S(1)} %broadcast_in_dim.2, bf16[32,4096]{1,0:T(8,128)(2,1)S(1)} %slice.37, bf16[32,4096]{1,0:T(8,128)(2,1)} %param.10), kind=kLoop, calls=%fused_computation.3 | loop fusion | flops 1597440 | bytes 1064960 | tf_op jit(solution)/shard_map/concatenate | solution.py:165
  8.4 0.0 copy-start
  8.5 3.6 %collective-permute-start.4 = (bf16[32,8320]{1,0:T(8,128)(2,1)S(1)}, bf16[32,8320]{1,0:T(8,128)(2,1)}, u32[]{:S(2)}, u32[]{:S(2)}) collective-permute-start(bf16[32,8320]{1,0:T(8,128)(2,1)S(1)} %pad_maximum_fusion.refs_1_.refs_7_), channel_id=1, source_target_pairs={{0,4},{4,0},{8,12},{12,8},{1,5},{5,1},{9,13},{13,9},{2,6},{6,2},{1... | collective-permute-start | bytes 1597448 | tf_op jit(solution)/shard_map/ppermute | solution.py:169
  12.1 0.0 copy-done
  12.1 1.5 %collective-permute-start.5 = (bf16[32,8320]{1,0:T(8,128)(2,1)S(1)}, bf16[32,8320]{1,0:T(8,128)(2,1)}, u32[]{:S(2)}, u32[]{:S(2)}) collective-permute-start(bf16[32,8320]{1,0:T(8,128)(2,1)S(1)} %pad_maximum_fusion.refs_1_.refs_7_), channel_id=1, source_target_pairs={{4,8},{8,4},{5,9},{9,5},{6,10},{10,6},{7,11},{11,7},{20,24},{24,20... | collective-permute-start | bytes 1597448 | tf_op jit(solution)/shard_map/ppermute | solution.py:170
  13.6 4.5 %convolution_bitcast_fusion = f32[512,128]{1,0:T(8,128)} fusion(bf16[512,4096]{1,0:T(8,128)(2,1)} %refs_0_.4, s32[]{:T(128)S(6)} %select_n.4), kind=kOutput, calls=%fused_computation | convolution fusion | flops 536870912 | bytes 5505028 | tf_op jit(solution)/shard_map/dot_general | solution.py:22
  18.1 1.9 %collective-permute-done.refs_2_.refs_3_ = bf16[32,10240]{1,0:T(8,128)(2,1)} collective-permute-done((bf16[32,10240]{1,0:T(8,128)(2,1)S(1)}, bf16[32,10240]{1,0:T(8,128)(2,1)}, u32[]{:S(2)}, u32[]{:S(2)}) %collective-permute-start) | collective-permute-done | bytes 655392 | tf_op jit(solution)/shard_map/ppermute | solution.py:167
  19.9 1.5 %collective-permute-start.2 = (bf16[32,10240]{1,0:T(8,128)(2,1)}, bf16[32,10240]{1,0:T(8,128)(2,1)}, u32[]{:S(2)}, u32[]{:S(2)}) collective-permute-start(bf16[32,10240]{1,0:T(8,128)(2,1)} %collective-permute-done.refs_2_.refs_3_), channel_id=1, source_target_pairs={{4,8},{8,4},{5,9},{9,5},{6,10},{10,6},{7,11},{11,7},{20,24},{24,20... | collective-permute-start | bytes 1966088 | tf_op jit(solution)/shard_map/ppermute | solution.py:174
  21.4 0.0 collective-permute-done.1.refs_3_.refs_4_
  21.4 1.3 %collective-permute-start.3 = (bf16[32,10240]{1,0:T(8,128)(2,1)}, bf16[32,10240]{1,0:T(8,128)(2,1)}, u32[]{:S(2)}, u32[]{:S(2)}) collective-permute-start(bf16[32,10240]{1,0:T(8,128)(2,1)} %collective-permute-done.1.refs_3_.refs_4_), channel_id=1, source_target_pairs={{4,0},{8,12},{5,1},{9,13},{6,2},{10,14},{7,3},{11,15},{20,16},{24,... | collective-permute-start | bytes 1966088 | tf_op jit(solution)/shard_map/ppermute | solution.py:175
  22.7 0.0 copy-done.3
  22.7 0.0 copy-start.2
  22.7 0.6 fusion.2.owner_ref
  23.3 8.0 %collective-permute-done.4.refs_2_.refs_8_ = bf16[32,8320]{1,0:T(8,128)(2,1)} collective-permute-done((bf16[32,8320]{1,0:T(8,128)(2,1)S(1)}, bf16[32,8320]{1,0:T(8,128)(2,1)}, u32[]{:S(2)}, u32[]{:S(2)}) %collective-permute-start.4) | collective-permute-done | bytes 532512 | tf_op jit(solution)/shard_map/ppermute | solution.py:169
  31.3 0.0 collective-permute-done.5.refs_3_.refs_9_
  31.3 0.0 copy-done.1
  31.3 1.5 %collective-permute-start.8 = (bf16[32,8320]{1,0:T(8,128)(2,1)}, bf16[32,8320]{1,0:T(8,128)(2,1)}, u32[]{:S(2)}, u32[]{:S(2)}) collective-permute-start(bf16[32,8320]{1,0:T(8,128)(2,1)} %collective-permute-done.4.refs_2_.refs_8_), channel_id=1, source_target_pairs={{4,8},{8,4},{5,9},{9,5},{6,10},{10,6},{7,11},{11,7},{20,24},{24,20... | collective-permute-start | bytes 1597448 | tf_op jit(solution)/shard_map/ppermute | solution.py:177
  32.8 0.0 copy-done.2
  32.8 1.3 %collective-permute-start.9 = (bf16[32,8320]{1,0:T(8,128)(2,1)}, bf16[32,8320]{1,0:T(8,128)(2,1)}, u32[]{:S(2)}, u32[]{:S(2)}) collective-permute-start(bf16[32,8320]{1,0:T(8,128)(2,1)} %collective-permute-done.5.refs_3_.refs_9_), channel_id=1, source_target_pairs={{4,0},{8,12},{5,1},{9,13},{6,2},{10,14},{7,3},{11,15},{20,16},{24,... | collective-permute-start | bytes 1597448 | tf_op jit(solution)/shard_map/ppermute | solution.py:178
  34.1 8.4 %share_gram.1 = f32[512,128]{1,0:T(8,128)} custom-call(bf16[512,14336]{1,0:T(8,128)(2,1)} %refs_0_.5), custom_call_target="tpu_custom_call" | custom-call | flops 1879048192 | bytes 14680064 | tf_op jit(solution)/shard_map/share_gram/pallas_call | solution.py:41
  42.5 1.9 %convolution_multiply_fusion.self_ref = f32[8,128]{1,0:T(8,128)} fusion(f32[512,128]{1,0:T(8,128)} %share_gram.1, f32[512,128]{1,0:T(8,128)} %convolution_bitcast_fusion, s32[512]{0:T(512)} %copy-done.2, f32[8,512]{1,0:T(8,128)} %fusion.2.owner_ref, s32[]{:T(128)S(6)} %select_n.4), kind=kOutput, calls=%fused_computation.1 | convolution fusion | flops 6362112 | bytes 534532 | tf_op jit(solution)/shard_map/dot_general | solution.py:26
  44.4 0.0 collective-permute-done.2.refs_4_.refs_5_
  44.4 1.0 %collective-permute-done.3.refs_5_.refs_6_ = bf16[32,10240]{1,0:T(8,128)(2,1)} collective-permute-done((bf16[32,10240]{1,0:T(8,128)(2,1)}, bf16[32,10240]{1,0:T(8,128)(2,1)}, u32[]{:S(2)}, u32[]{:S(2)}) %collective-permute-start.3) | collective-permute-done | bytes 655392 | tf_op jit(solution)/shard_map/ppermute | solution.py:175
  45.4 1.0 %slice.38 = bf16[32,6144]{1,0:T(8,128)(2,1)S(1)} slice(bf16[32,10240]{1,0:T(8,128)(2,1)} %collective-permute-done.2.refs_4_.refs_5_), slice={[0:32], [0:6144]} | slice | bytes 786432 | tf_op jit(solution)/shard_map/slice | solution.py:181
  46.4 1.3 %collective-permute-start.6 = (bf16[32,6144]{1,0:T(8,128)(2,1)S(1)}, bf16[32,6144]{1,0:T(8,128)(2,1)}, u32[]{:S(2)}, u32[]{:S(2)}) collective-permute-start(bf16[32,6144]{1,0:T(8,128)(2,1)S(1)} %slice.38), channel_id=1, source_target_pairs={{4,0},{8,12},{5,1},{9,13},{6,2},{10,14},{7,3},{11,15},{20,16},{24,... | collective-permute-start | bytes 1179656 | tf_op jit(solution)/shard_map/ppermute | solution.py:182
  47.7 1.7 %slice.39 = bf16[32,4096]{1,0:T(8,128)(2,1)} slice(bf16[32,10240]{1,0:T(8,128)(2,1)} %collective-permute-done.2.refs_4_.refs_5_), slice={[0:32], [6144:10240]} | slice | bytes 524288 | tf_op jit(solution)/shard_map/slice | solution.py:183
  49.4 1.3 %collective-permute-start.7 = (bf16[32,4096]{1,0:T(8,128)(2,1)}, bf16[32,4096]{1,0:T(8,128)(2,1)}, u32[]{:S(2)}, u32[]{:S(2)}) collective-permute-start(bf16[32,4096]{1,0:T(8,128)(2,1)} %slice.39), channel_id=1, source_target_pairs={{4,0},{8,12},{5,1},{9,13},{6,2},{10,14},{7,3},{11,15},{20,16},{24,... | collective-permute-start | bytes 786440 | tf_op jit(solution)/shard_map/ppermute | solution.py:184
  50.7 0.0 collective-permute-done.8.refs_4_.refs_10_
  50.7 6.1 %collective-permute-done.9.refs_5_.refs_11_ = bf16[32,8320]{1,0:T(8,128)(2,1)} collective-permute-done((bf16[32,8320]{1,0:T(8,128)(2,1)}, bf16[32,8320]{1,0:T(8,128)(2,1)}, u32[]{:S(2)}, u32[]{:S(2)}) %collective-permute-start.9) | collective-permute-done | bytes 532512 | tf_op jit(solution)/shard_map/ppermute | solution.py:178
  56.8 1.7 %slice.40 = bf16[32,4096]{1,0:T(8,128)(2,1)} slice(bf16[32,8320]{1,0:T(8,128)(2,1)} %collective-permute-done.8.refs_4_.refs_10_), slice={[0:32], [0:4096]} | slice | bytes 524288 | tf_op jit(solution)/shard_map/slice | solution.py:186
  58.4 1.3 %collective-permute-start.10 = (bf16[32,4096]{1,0:T(8,128)(2,1)}, bf16[32,4096]{1,0:T(8,128)(2,1)}, u32[]{:S(2)}, u32[]{:S(2)}) collective-permute-start(bf16[32,4096]{1,0:T(8,128)(2,1)} %slice.40), channel_id=1, source_target_pairs={{4,0},{8,12},{5,1},{9,13},{6,2},{10,14},{7,3},{11,15},{20,16},{24,... | collective-permute-start | bytes 786440 | tf_op jit(solution)/shard_map/ppermute | solution.py:187
  59.7 1.7 %slice.41 = bf16[32,4224]{1,0:T(8,128)(2,1)} slice(bf16[32,8320]{1,0:T(8,128)(2,1)} %collective-permute-done.8.refs_4_.refs_10_), slice={[0:32], [4096:8320]} | slice | bytes 540672 | tf_op jit(solution)/shard_map/slice | solution.py:188
  61.4 1.3 %collective-permute-start.11 = (bf16[32,4224]{1,0:T(8,128)(2,1)}, bf16[32,4224]{1,0:T(8,128)(2,1)}, u32[]{:S(2)}, u32[]{:S(2)}) collective-permute-start(bf16[32,4224]{1,0:T(8,128)(2,1)} %slice.41), channel_id=1, source_target_pairs={{4,0},{8,12},{5,1},{9,13},{6,2},{10,14},{7,3},{11,15},{20,16},{24,... | collective-permute-start | bytes 811016 | tf_op jit(solution)/shard_map/ppermute | solution.py:189
  62.7 2.5 %collective-permute-done.6.refs_6_ = bf16[32,6144]{1,0:T(8,128)(2,1)} collective-permute-done((bf16[32,6144]{1,0:T(8,128)(2,1)S(1)}, bf16[32,6144]{1,0:T(8,128)(2,1)}, u32[]{:S(2)}, u32[]{:S(2)}) %collective-permute-start.6) | collective-permute-done | bytes 393248 | tf_op jit(solution)/shard_map/ppermute | solution.py:182
  65.2 5.8 %cross_gram.3.refs_0_ = f32[512,128]{1,0:T(8,128)} custom-call(bf16[512,14336]{1,0:T(8,128)(2,1)} %refs_0_.5, bf16[32,10240]{1,0:T(8,128)(2,1)} %copy-done.1, bf16[32,10240]{1,0:T(8,128)(2,1)} %collective-permute-done.refs_2_.refs_3_, bf16[32,10240]{1,0:T(8,128)(2,1)} %collective-permute-done.1.refs_3_.refs_4_, ...), custom_call_target="tpu_custom_call" | custom-call | flops 805306368 | bytes 6291456 | tf_op jit(solution)/shard_map/cross_gram/pallas_call | solution.py:41
  71.0 0.0 collective-permute-done.7.refs_7_
  71.0 4.3 %cross_gram.4.x_ref = f32[512,128]{1,0:T(8,128)} custom-call(f32[512,128]{1,0:T(8,128)} %cross_gram.3.refs_0_, bf16[512,14336]{1,0:T(8,128)(2,1)} %refs_0_.5, bf16[32,10240]{1,0:T(8,128)(2,1)} %copy-done.1, bf16[32,10240]{1,0:T(8,128)(2,1)} %collective-permute-done.refs_2_.refs_3_, bf16[32,10240]{1,0:T(8,128)(2,1)} %collective-permute-done.1.refs_3_.refs_4_, ...), custom_call_target="tpu_custom_call" | custom-call | flops 536870912 | bytes 4194304 | tf_op jit(solution)/shard_map/cross_gram/pallas_call | solution.py:41
  75.3 1.2 %collective-permute-done.10.refs_6_ = bf16[32,4096]{1,0:T(8,128)(2,1)} collective-permute-done((bf16[32,4096]{1,0:T(8,128)(2,1)}, bf16[32,4096]{1,0:T(8,128)(2,1)}, u32[]{:S(2)}, u32[]{:S(2)}) %collective-permute-start.10) | collective-permute-done | bytes 262176 | tf_op jit(solution)/shard_map/ppermute | solution.py:187
  76.4 4.0 %cross_gram.5.g_ref = f32[512,128]{1,0:T(8,128)} custom-call(bf16[512,4096]{1,0:T(8,128)(2,1)} %refs_0_.4, bf16[32,8320]{1,0:T(8,128)(2,1)} %copy-done, bf16[32,8320]{1,0:T(8,128)(2,1)} %collective-permute-done.4.refs_2_.refs_8_, bf16[32,8320]{1,0:T(8,128)(2,1)} %collective-permute-done.5.refs_3_.refs_9_, ...), custom_call_target="tpu_custom_call" | custom-call | flops 536870912 | bytes 4194304 | tf_op jit(solution)/shard_map/cross_gram/pallas_call | solution.py:41
  80.5 0.9 %collective-permute-done.11.refs_6_.refs_12_ = bf16[32,4224]{1,0:T(8,128)(2,1)} collective-permute-done((bf16[32,4224]{1,0:T(8,128)(2,1)}, bf16[32,4224]{1,0:T(8,128)(2,1)}, u32[]{:S(2)}, u32[]{:S(2)}) %collective-permute-start.11) | collective-permute-done | bytes 270368 | tf_op jit(solution)/shard_map/ppermute | solution.py:189
  81.4 4.7 %score_shares.1 = (f32[8,128]{1,0:T(8,128)}, f32[8,128]{1,0:T(8,128)}, f32[8,128]{1,0:T(8,128)}, f32[8,128]{1,0:T(8,128)}) custom-call(f32[512,128]{1,0:T(8,128)} %cross_gram.4.x_ref, f32[512,128]{1,0:T(8,128)} %cross_gram.5.g_ref, f32[8,512]{1,0:T(8,128)} %fusion.2.owner_ref, f32[8,128]{1,0:T(8,128)} %convolution_multiply_fusion.self_ref, ...), custom_call_target="tpu_custom_call" | custom-call | flops 536870912 | bytes 4194304 | tf_op jit(solution)/shard_map/score_shares/pallas_call | solution.py:41
  86.1 0.3 collective-permute-start.14
  86.4 1.5 %collective-permute-start.13 = (f32[8,128]{1,0:T(8,128)}, f32[8,128]{1,0:T(8,128)S(1)}, u32[]{:S(2)}, u32[]{:S(2)}) collective-permute-start(f32[8,128]{1,0:T(8,128)} %get-tuple-element.39), channel_id=1, source_target_pairs={{0,2},{1,3},{2,0},{3,1},{4,6},{5,7},{6,4},{7,5},{8,10},{9,11},{10,... | collective-permute-start | bytes 12296 | tf_op jit(solution)/shard_map/ppermute | solution.py:207
  87.9 0.1 collective-permute-start.12
  88.1 0.7 slice.42
  88.8 0.7 collective-permute-done.14
  89.5 0.8 collective-permute-done.13
  90.2 0.0 collective-permute-done.12
  90.3 0.7 multiply_divide_fusion
  (2 shorter events, 0.0 us)
Async XLA Ops:
  0.0 22.7 %copy-start.3 = (s32[512]{0:T(512)S(1)}, s32[512]{0:T(512)}, u32[]{:S(2)}) copy-start(s32[512]{0:T(512)} %param.8) | copy-start | bytes 6148
  1.1 30.2 %copy-start.1 = (bf16[32,10240]{1,0:T(8,128)(2,1)}, bf16[32,10240]{1,0:T(8,128)(2,1)S(1)}, u32[]{:S(2)}) copy-start(bf16[32,10240]{1,0:T(8,128)(2,1)S(1)} %slice.36.refs_1_.refs_2_) | copy-start | bytes 1966084
  1.2 18.8 %collective-permute-start = (bf16[32,10240]{1,0:T(8,128)(2,1)S(1)}, bf16[32,10240]{1,0:T(8,128)(2,1)}, u32[]{:S(2)}, u32[]{:S(2)}) collective-permute-start(bf16[32,10240]{1,0:T(8,128)(2,1)S(1)} %slice.36.refs_1_.refs_2_), channel_id=1, source_target_pairs={{0,4},{4,0},{8,12},{12,8},{1,5},{5,1},{9,13},{13,9},{2,6},{6,2},{1... | collective-permute-start | bytes 1966088 | tf_op jit(solution)/shard_map/ppermute | solution.py:167
  4.2 17.2 %collective-permute-start.1 = (bf16[32,10240]{1,0:T(8,128)(2,1)S(1)}, bf16[32,10240]{1,0:T(8,128)(2,1)}, u32[]{:S(2)}, u32[]{:S(2)}) collective-permute-start(bf16[32,10240]{1,0:T(8,128)(2,1)S(1)} %slice.36.refs_1_.refs_2_), channel_id=1, source_target_pairs={{4,8},{8,4},{5,9},{9,5},{6,10},{10,6},{7,11},{11,7},{20,24},{24,20... | collective-permute-start | bytes 1966088 | tf_op jit(solution)/shard_map/ppermute | solution.py:168
  8.4 3.6 %copy-start = (bf16[32,8320]{1,0:T(8,128)(2,1)}, bf16[32,8320]{1,0:T(8,128)(2,1)S(1)}, u32[]{:S(2)}) copy-start(bf16[32,8320]{1,0:T(8,128)(2,1)S(1)} %pad_maximum_fusion.refs_1_.refs_7_) | copy-start | bytes 1597444
  8.5 22.9 %collective-permute-start.4 = (bf16[32,8320]{1,0:T(8,128)(2,1)S(1)}, bf16[32,8320]{1,0:T(8,128)(2,1)}, u32[]{:S(2)}, u32[]{:S(2)}) collective-permute-start(bf16[32,8320]{1,0:T(8,128)(2,1)S(1)} %pad_maximum_fusion.refs_1_.refs_7_), channel_id=1, source_target_pairs={{0,4},{4,0},{8,12},{12,8},{1,5},{5,1},{9,13},{13,9},{2,6},{6,2},{1... | collective-permute-start | bytes 1597448 | tf_op jit(solution)/shard_map/ppermute | solution.py:169
  12.1 19.2 %collective-permute-start.5 = (bf16[32,8320]{1,0:T(8,128)(2,1)S(1)}, bf16[32,8320]{1,0:T(8,128)(2,1)}, u32[]{:S(2)}, u32[]{:S(2)}) collective-permute-start(bf16[32,8320]{1,0:T(8,128)(2,1)S(1)} %pad_maximum_fusion.refs_1_.refs_7_), channel_id=1, source_target_pairs={{4,8},{8,4},{5,9},{9,5},{6,10},{10,6},{7,11},{11,7},{20,24},{24,20... | collective-permute-start | bytes 1597448 | tf_op jit(solution)/shard_map/ppermute | solution.py:170
  19.9 24.5 %collective-permute-start.2 = (bf16[32,10240]{1,0:T(8,128)(2,1)}, bf16[32,10240]{1,0:T(8,128)(2,1)}, u32[]{:S(2)}, u32[]{:S(2)}) collective-permute-start(bf16[32,10240]{1,0:T(8,128)(2,1)} %collective-permute-done.refs_2_.refs_3_), channel_id=1, source_target_pairs={{4,8},{8,4},{5,9},{9,5},{6,10},{10,6},{7,11},{11,7},{20,24},{24,20... | collective-permute-start | bytes 1966088 | tf_op jit(solution)/shard_map/ppermute | solution.py:174
  21.4 23.9 %collective-permute-start.3 = (bf16[32,10240]{1,0:T(8,128)(2,1)}, bf16[32,10240]{1,0:T(8,128)(2,1)}, u32[]{:S(2)}, u32[]{:S(2)}) collective-permute-start(bf16[32,10240]{1,0:T(8,128)(2,1)} %collective-permute-done.1.refs_3_.refs_4_), channel_id=1, source_target_pairs={{4,0},{8,12},{5,1},{9,13},{6,2},{10,14},{7,3},{11,15},{20,16},{24,... | collective-permute-start | bytes 1966088 | tf_op jit(solution)/shard_map/ppermute | solution.py:175
  22.7 10.1 %copy-start.2 = (s32[512]{0:T(512)}, s32[512]{0:T(512)S(1)}, u32[]{:S(2)}) copy-start(s32[512]{0:T(512)S(1)} %broadcast_subtract_fusion) | copy-start | bytes 6148
  31.3 19.4 %collective-permute-start.8 = (bf16[32,8320]{1,0:T(8,128)(2,1)}, bf16[32,8320]{1,0:T(8,128)(2,1)}, u32[]{:S(2)}, u32[]{:S(2)}) collective-permute-start(bf16[32,8320]{1,0:T(8,128)(2,1)} %collective-permute-done.4.refs_2_.refs_8_), channel_id=1, source_target_pairs={{4,8},{8,4},{5,9},{9,5},{6,10},{10,6},{7,11},{11,7},{20,24},{24,20... | collective-permute-start | bytes 1597448 | tf_op jit(solution)/shard_map/ppermute | solution.py:177
  32.8 24.0 %collective-permute-start.9 = (bf16[32,8320]{1,0:T(8,128)(2,1)}, bf16[32,8320]{1,0:T(8,128)(2,1)}, u32[]{:S(2)}, u32[]{:S(2)}) collective-permute-start(bf16[32,8320]{1,0:T(8,128)(2,1)} %collective-permute-done.5.refs_3_.refs_9_), channel_id=1, source_target_pairs={{4,0},{8,12},{5,1},{9,13},{6,2},{10,14},{7,3},{11,15},{20,16},{24,... | collective-permute-start | bytes 1597448 | tf_op jit(solution)/shard_map/ppermute | solution.py:178
  46.4 18.8 %collective-permute-start.6 = (bf16[32,6144]{1,0:T(8,128)(2,1)S(1)}, bf16[32,6144]{1,0:T(8,128)(2,1)}, u32[]{:S(2)}, u32[]{:S(2)}) collective-permute-start(bf16[32,6144]{1,0:T(8,128)(2,1)S(1)} %slice.38), channel_id=1, source_target_pairs={{4,0},{8,12},{5,1},{9,13},{6,2},{10,14},{7,3},{11,15},{20,16},{24,... | collective-permute-start | bytes 1179656 | tf_op jit(solution)/shard_map/ppermute | solution.py:182
  49.4 21.6 %collective-permute-start.7 = (bf16[32,4096]{1,0:T(8,128)(2,1)}, bf16[32,4096]{1,0:T(8,128)(2,1)}, u32[]{:S(2)}, u32[]{:S(2)}) collective-permute-start(bf16[32,4096]{1,0:T(8,128)(2,1)} %slice.39), channel_id=1, source_target_pairs={{4,0},{8,12},{5,1},{9,13},{6,2},{10,14},{7,3},{11,15},{20,16},{24,... | collective-permute-start | bytes 786440 | tf_op jit(solution)/shard_map/ppermute | solution.py:184
  58.4 18.0 %collective-permute-start.10 = (bf16[32,4096]{1,0:T(8,128)(2,1)}, bf16[32,4096]{1,0:T(8,128)(2,1)}, u32[]{:S(2)}, u32[]{:S(2)}) collective-permute-start(bf16[32,4096]{1,0:T(8,128)(2,1)} %slice.40), channel_id=1, source_target_pairs={{4,0},{8,12},{5,1},{9,13},{6,2},{10,14},{7,3},{11,15},{20,16},{24,... | collective-permute-start | bytes 786440 | tf_op jit(solution)/shard_map/ppermute | solution.py:187
  61.4 20.0 %collective-permute-start.11 = (bf16[32,4224]{1,0:T(8,128)(2,1)}, bf16[32,4224]{1,0:T(8,128)(2,1)}, u32[]{:S(2)}, u32[]{:S(2)}) collective-permute-start(bf16[32,4224]{1,0:T(8,128)(2,1)} %slice.41), channel_id=1, source_target_pairs={{4,0},{8,12},{5,1},{9,13},{6,2},{10,14},{7,3},{11,15},{20,16},{24,... | collective-permute-start | bytes 811016 | tf_op jit(solution)/shard_map/ppermute | solution.py:189
  86.1 3.3 %collective-permute-start.14 = (f32[8,128]{1,0:T(8,128)}, f32[8,128]{1,0:T(8,128)S(1)}, u32[]{:S(2)}, u32[]{:S(2)}) collective-permute-start(f32[8,128]{1,0:T(8,128)} %get-tuple-element.40), channel_id=1, source_target_pairs={{0,3},{1,2},{2,1},{3,0},{4,7},{5,6},{6,5},{7,4},{8,11},{9,10},{10,... | collective-permute-start | bytes 12296 | tf_op jit(solution)/shard_map/ppermute | solution.py:207
  86.4 3.8 %collective-permute-start.13 = (f32[8,128]{1,0:T(8,128)}, f32[8,128]{1,0:T(8,128)S(1)}, u32[]{:S(2)}, u32[]{:S(2)}) collective-permute-start(f32[8,128]{1,0:T(8,128)} %get-tuple-element.39), channel_id=1, source_target_pairs={{0,2},{1,3},{2,0},{3,1},{4,6},{5,7},{6,4},{7,5},{8,10},{9,11},{10,... | collective-permute-start | bytes 12296 | tf_op jit(solution)/shard_map/ppermute | solution.py:207
  87.9 2.3 %collective-permute-start.12 = (f32[8,128]{1,0:T(8,128)}, f32[8,128]{1,0:T(8,128)S(1)}, u32[]{:S(2)}, u32[]{:S(2)}) collective-permute-start(f32[8,128]{1,0:T(8,128)} %get-tuple-element.38), channel_id=1, source_target_pairs={{0,1},{1,0},{2,3},{3,2},{4,5},{5,4},{6,7},{7,6},{8,9},{9,8},{10,11... | collective-permute-start | bytes 12296 | tf_op jit(solution)/shard_map/ppermute | solution.py:207
